TPU v7x, 128 devices: a whole 4x4x4 slice. The times are simulated.
128 devices in a mesh: row: 8 (over x_hi, z), col: 16 (over y, x_lo, core).
Axes of the slice: x: 4 (x_hi: 2, x_lo: 2; x = x_hi * 2 + x_lo), y: 4, z: 4, core: 2. Of those that a mesh axis runs over, the one named last changes fastest.
Arguments:
- frozen_projection_weight: bfloat16 [16384, 16384], P('row', 'col'), may hold values from -0.046875 to 0.046875
- a_master: float32 [64, 16384], P('row', 'col'), may hold values from -6 to 6
- a_first: float32 [64, 16384], P('row', 'col'), may hold values from -4 to 4
- a_second: float32 [64, 16384], P('row', 'col'), may hold values from 0.1 to 10
- bt_master: float32 [64, 16384], P('col', 'row'), may hold values from -6 to 6
- bt_first: float32 [64, 16384], P('col', 'row'), may hold values from -4 to 4
- bt_second: float32 [64, 16384], P('col', 'row'), may hold values from 0.1 to 10
- grad_a_parts: float32 [8, 64, 16384], P('row', None, 'col'), may hold values from -6 to 6
- grad_bt_parts: float32 [16, 64, 16384], P('col', None, 'row'), may hold values from -6 to 6
Outputs:
- saved: bfloat16 [8, 16384, 2048], P(None, ('row', 'col'))
- a_new: float32 [64, 16384], P('row', 'col')
- a_first_new: float32 [64, 16384], P('row', 'col')
- a_second_new: float32 [64, 16384], P('row', 'col')
- bt_new: float32 [64, 16384], P('col', 'row')
- bt_first_new: float32 [64, 16384], P('col', 'row')
- bt_second_new: float32 [64, 16384], P('col', 'row')
All inputs are finite; a program needn't handle non-finite values.
Results may differ from a plain program's by a relative error of at most 0.0004.
The roundings to bfloat16 on the way count: a program that leaves them out, or rounds other values in their place, can miss the bound.
Values may be sent and summed in bfloat16 or wider, within the bound.
No kernel may reach another device: no remote copies, remote signals or barrier semaphores. Data moves between devices by JAX's collectives and lax.ppermute only.
A program may use at most 64 MiB of HBM per device.

v0:
```python
import math

import jax
import jax.numpy as jnp
from jax import lax
from jax.sharding import PartitionSpec as P

D = 16384
R = 64
TP = 8
STEP = 10


beta_first = 0.9
beta_second = 0.95
adam_eps = 1e-08
learn_rate = 0.08


def adapter_factor():
    return 0.25 / math.sqrt(R * D)


def adam_step(master, first, second, grad):
    first_new = beta_first * first + (1.0 - beta_first) * grad
    second_new = beta_second * second + (1.0 - beta_second) * grad * grad
    corr_first = 1.0 - beta_first**STEP
    corr_second = 1.0 - beta_second**STEP
    update = first_new / corr_first / (jnp.sqrt(second_new / corr_second) + adam_eps)
    return (master - learn_rate * update, first_new, second_new)


def rank_product(left, right):
    return lax.dot_general(
        left, right, (((0,), (0,)), ((), ())), preferred_element_type=jnp.float32
    )


def per_device(
    frozen_projection_weight,
    a_master,
    a_first,
    a_second,
    bt_master,
    bt_first,
    bt_second,
    grad_a_parts,
    grad_bt_parts,
):
    scaling = adapter_factor()
    grad_a = lax.psum(grad_a_parts[0], "row")
    grad_bt = lax.psum(grad_bt_parts[0], "col")
    a_states = (
        lax.all_gather(a_master, "row", axis=0, tiled=True),
        lax.all_gather(a_first, "row", axis=0, tiled=True),
        lax.all_gather(a_second, "row", axis=0, tiled=True),
    )
    bt_states = (
        lax.all_gather(bt_master, "col", axis=0, tiled=True),
        lax.all_gather(bt_first, "col", axis=0, tiled=True),
        lax.all_gather(bt_second, "col", axis=0, tiled=True),
    )
    a_full = adam_step(a_states[0], a_states[1], a_states[2], grad_a)
    bt_full = adam_step(bt_states[0], bt_states[1], bt_states[2], grad_bt)
    a_count = a_master.shape[0]
    bt_count = bt_master.shape[0]
    down_factor_begin = lax.axis_index("row") * a_count
    bt_start = lax.axis_index("col") * bt_count
    a_new, a_first_new, a_second_new = tuple(
        (lax.dynamic_slice_in_dim(member, down_factor_begin, a_count, 0) for member in a_full)
    )
    bt_new, bt_first_new, bt_second_new = tuple(
        (lax.dynamic_slice_in_dim(member, bt_start, bt_count, 0) for member in bt_full)
    )
    a_whole = a_full[0].astype(jnp.bfloat16)
    bt_whole = bt_full[0].astype(jnp.bfloat16)
    rows_here = frozen_projection_weight.shape[0]
    cols_here = frozen_projection_weight.shape[1]
    peers = lax.axis_size("col")
    piece_rows = rows_here // peers
    arrived = lax.all_to_all(
        frozen_projection_weight.reshape(1, rows_here, cols_here),
        "col",
        split_axis=1,
        concat_axis=0,
        tiled=True,
    )
    frozen_row_count = arrived.transpose(1, 0, 2).reshape(piece_rows, peers * cols_here)
    a_columns = lax.all_gather(a_whole, "col", axis=1, tiled=True)
    bt_rows = lax.dynamic_slice_in_dim(bt_whole, lax.axis_index("col") * piece_rows, piece_rows, 1)
    adapter_increment = rank_product(bt_rows, a_columns)
    combined_weight = (frozen_row_count.astype(jnp.float32) + scaling * adapter_increment).astype(
        jnp.bfloat16
    )
    saved = combined_weight.reshape(piece_rows, TP, peers * cols_here // TP).transpose(1, 0, 2)
    return (saved, a_new, a_first_new, a_second_new, bt_new, bt_first_new, bt_second_new)


def solution(mesh):
    return jax.shard_map(
        per_device,
        mesh=mesh,
        in_specs=(
            P("row", "col"),
            P("row", "col"),
            P("row", "col"),
            P("row", "col"),
            P("col", "row"),
            P("col", "row"),
            P("col", "row"),
            P("row", None, "col"),
            P("col", None, "row"),
        ),
        out_specs=(
            P(None, ("row", "col"), None),
            P("row", "col"),
            P("row", "col"),
            P("row", "col"),
            P("col", "row"),
            P("col", "row"),
            P("col", "row"),
        ),
        check_vma=False,
    )
```

profile of v0, /device:TPU:1, one launch (start us, length us, event | category | flops | bytes accessed | tf_op | source)
XLA Modules:
  0.0 317.7 jit_solution(16596844474119781414)
XLA Ops:
  7.2 0.0 all-reduce.5.cloned.1.call-start
  7.2 0.7 all-reduce.5.cloned.1.call-update
  7.9 8.7 %copy.30 = bf16[1,2048,1024]{2,0,1:T(2,128)(2,1)} copy(bf16[1,2048,1024]{2,1,0:T(8,128)(2,1)} %bitcast.29) | data formatting | bytes 8388608 | tf_op jit(solution)/shard_map/reshape | solution.py:82
  16.6 0.5 broadcast.10
  17.1 26.0 %reduce = bf16[2048,1024]{1,0:T(8,128)(2,1)} reduce(bf16[2048,1,1024]{2,1,0:T(2,128)(2,1)} %bitcast.25, bf16[]{:T(256)} %broadcast.10), dimensions={1}, to_apply=%bitcast.23.reduce_sub_computation | reduce | bytes 8388610
  43.1 11.4 %reshape.42 = bf16[16,2,65536]{2,1,0:T(2,128)(2,1)} reshape(bf16[2048,1024]{1,0:T(8,128)(2,1)} %reduce) | data formatting | bytes 8388608
  54.4 0.0 copy-start
  54.5 0.0 copy-start.1
  54.5 0.0 copy-start.2
  54.5 0.0 copy-start.3
  54.5 7.1 %all-to-all-start = ((bf16[16,2,65536]{2,1,0:T(2,128)(2,1)}), bf16[16,2,65536]{2,1,0:T(2,128)(2,1)}, u32[]{:S(2)}, u32[]{:S(2)}) async-start(bf16[16,2,65536]{2,1,0:T(2,128)(2,1)} %reshape.42), calls=%async_computation | async-start | bytes 8388608 | tf_op jit(solution)/shard_map/all_to_all | solution.py:81
  61.5 0.0 copy-start.4
  61.5 0.0 copy-start.5
  61.5 0.0 all-reduce.3.cloned.1.call-start
  61.6 0.7 all-reduce.3.cloned.1.call-update
  62.3 0.0 all-gather.5.cloned.1.call-start
  62.3 0.0 copy-done
  62.3 76.8 %all_gather.24 = f32[64,1024]{1,0:T(8,128)S(1)} all-gather(f32[8,1024]{1,0:T(8,128)S(1)} %copy-done), channel_id=1, replica_groups=mesh['row'=8,'col'=16] {'row'}, dimensions={0}, use_global_device_ids=true | all-gather | bytes 294912 | tf_op jit(solution)/shard_map/all_gather | solution.py:54
  139.1 0.0 copy-done.1
  139.1 28.2 %all_gather.25 = f32[64,1024]{1,0:T(8,128)S(1)} all-gather(f32[8,1024]{1,0:T(8,128)S(1)} %copy-done.1), channel_id=1, replica_groups=mesh['row'=8,'col'=16] {'row'}, dimensions={0}, use_global_device_ids=true | all-gather | bytes 294912 | tf_op jit(solution)/shard_map/all_gather | solution.py:55
  167.3 0.0 copy-done.2
  167.3 28.3 %all_gather.26 = f32[64,1024]{1,0:T(8,128)S(1)} all-gather(f32[8,1024]{1,0:T(8,128)S(1)} %copy-done.2), channel_id=1, replica_groups=mesh['row'=8,'col'=16] {'row'}, dimensions={0}, use_global_device_ids=true | all-gather | bytes 294912 | tf_op jit(solution)/shard_map/all_gather | solution.py:56
  195.7 0.0 all-reduce.5.cloned.1.call-done
  195.7 1.8 fusion.6
  197.5 0.0 all-gather.5.cloned.1.call-update
  197.5 0.0 copy-done.3
  197.5 39.6 %all-gather = f32[16,4,2048]{2,1,0:T(4,128)S(1)} all-gather(f32[1,4,2048]{2,1,0:T(4,128)S(1)} %bitcast.33), channel_id=1, replica_groups=mesh['row'=8,'col'=16] {'col'}, dimensions={0}, use_global_device_ids=true | all-gather | bytes 557056 | tf_op jit(solution)/shard_map/all_gather | solution.py:59
  237.1 0.2 reshape.33
  237.2 0.0 copy-done.4
  237.3 20.9 %all-gather.1 = f32[16,4,2048]{2,1,0:T(4,128)S(1)} all-gather(f32[1,4,2048]{2,1,0:T(4,128)S(1)} %bitcast.34), channel_id=1, replica_groups=mesh['row'=8,'col'=16] {'col'}, dimensions={0}, use_global_device_ids=true | all-gather | bytes 557056 | tf_op jit(solution)/shard_map/all_gather | solution.py:60
  258.1 0.2 broadcast_multiply_fusion.1
  258.3 0.2 reshape.39
  258.5 0.0 copy-done.5
  258.5 18.9 %all-gather.2 = f32[16,4,2048]{2,1,0:T(4,128)S(1)} all-gather(f32[1,4,2048]{2,1,0:T(4,128)S(1)} %bitcast.35), channel_id=1, replica_groups=mesh['row'=8,'col'=16] {'col'}, dimensions={0}, use_global_device_ids=true | all-gather | bytes 557056 | tf_op jit(solution)/shard_map/all_gather | solution.py:61
  277.4 0.2 broadcast_multiply_fusion
  277.5 0.2 reshape.41
  277.7 0.6 constant_dynamic-slice_fusion.5
  278.4 0.6 constant_dynamic-slice_fusion.3
  279.0 1.4 multiply_subtract_fusion
  280.4 0.6 constant_dynamic-slice_fusion.2
  281.0 0.6 constant_dynamic-slice_fusion
  281.6 0.0 all-to-all-done
  281.6 12.4 %reshape.43 = bf16[2048,1,1024]{2,1,0:T(2,128)(2,1)} reshape(bf16[16,2,65536]{2,1,0:T(2,128)(2,1)} %all-to-all-done) | data formatting | bytes 8388608
  294.0 5.5 %copy.23 = f32[1,2048,1024]{2,1,0:T(8,128)S(1)} copy(bf16[1,2048,1024]{2,0,1:T(2,128)(2,1)} %bitcast.26) | data formatting | bytes 12582912
  299.5 4.1 %copy.25 = f32[16,8,16,1024]{3,1,2,0:T(8,128)} copy(f32[16,8,16,1024]{3,1,0,2:T(8,128)S(1)} %bitcast.27) | data formatting | bytes 16777216
  303.6 0.0 all-gather.5.cloned.1.call-done
  303.6 5.3 %fusion.1 = bf16[128,16384]{1,0:T(8,128)(2,1)S(1)} fusion(f32[128,16384]{1,0:T(8,128)} %bitcast.24, bf16[64,16384]{1,0:T(8,128)(2,1)} %all-gather.5.cloned.1.call-done, f32[64,2048]{1,0:T(8,128)S(1)} %get-tuple-element.7, s32[]{:T(128)S(6)} %select_n.6), kind=kOutput, calls=%fused_computation.2 | convolution fusion | flops 274726912 | bytes 14696452 | tf_op jit(solution)/shard_map/dot_general | solution.py:34
  308.9 2.3 copy.29
  (1 shorter events, 0.0 us)
Async XLA Ops:
  7.2 188.5 %all-reduce.5.cloned.1.call-start = ((), (), s32[]{:S(2)}) async-start(), calls=%async_computation.2 | async-start | bytes 524288 | tf_op jit(solution)/shard_map/psum | solution.py:51
  54.4 7.9 %copy-start = (f32[8,1024]{1,0:T(8,128)S(1)}, f32[8,1024]{1,0:T(8,128)}, u32[]{:S(2)}) copy-start(f32[8,1024]{1,0:T(8,128)} %param.10) | copy-start | bytes 98308
  54.5 84.7 %copy-start.1 = (f32[8,1024]{1,0:T(8,128)S(1)}, f32[8,1024]{1,0:T(8,128)}, u32[]{:S(2)}) copy-start(f32[8,1024]{1,0:T(8,128)} %param.11) | copy-start | bytes 98308
  54.5 112.9 %copy-start.2 = (f32[8,1024]{1,0:T(8,128)S(1)}, f32[8,1024]{1,0:T(8,128)}, u32[]{:S(2)}) copy-start(f32[8,1024]{1,0:T(8,128)} %param.12) | copy-start | bytes 98308
  54.5 143.0 %copy-start.3 = (f32[4,2048]{1,0:T(4,128)S(1)}, f32[4,2048]{1,0:T(4,128)}, u32[]{:S(2)}) copy-start(f32[4,2048]{1,0:T(4,128)} %param.13) | copy-start | bytes 98308
  54.5 227.2 %all-to-all-start = ((bf16[16,2,65536]{2,1,0:T(2,128)(2,1)}), bf16[16,2,65536]{2,1,0:T(2,128)(2,1)}, u32[]{:S(2)}, u32[]{:S(2)}) async-start(bf16[16,2,65536]{2,1,0:T(2,128)(2,1)} %reshape.42), calls=%async_computation | async-start | bytes 8388608 | tf_op jit(solution)/shard_map/all_to_all | solution.py:81
  61.5 175.7 %copy-start.4 = (f32[4,2048]{1,0:T(4,128)S(1)}, f32[4,2048]{1,0:T(4,128)}, u32[]{:S(2)}) copy-start(f32[4,2048]{1,0:T(4,128)} %param.14) | copy-start | bytes 98308
  61.5 196.9 %copy-start.5 = (f32[4,2048]{1,0:T(4,128)S(1)}, f32[4,2048]{1,0:T(4,128)}, u32[]{:S(2)}) copy-start(f32[4,2048]{1,0:T(4,128)} %param.15) | copy-start | bytes 98308
  61.5 217.4 %all-reduce.3.cloned.1.call-start = ((), (), s32[]{:S(2)}) async-start(), calls=%async_computation.1 | async-start | bytes 1048576 | tf_op jit(solution)/shard_map/psum | solution.py:52
  62.3 241.3 %all-gather.5.cloned.1.call-start = ((), (), s32[]{:S(2)}) async-start(), calls=%async_computation.3 | async-start | bytes 2228224 | tf_op jit(solution)/shard_map/all_gather | solution.py:89
Sparse Core Ops, SparseCore 0:
  10.5 84.0 all-reduce.4
  97.2 120.9 all-reduce.2
  220.4 35.9 all-gather.4
where the time goes:
time: 319 us; the launch traced here: 318 us
  blocking collectives  213 us (67%)
  local copies, waits for them, and re-layouts  47.9 us (15%)
  other arithmetic  29.5 us (9%)
  between operations  13.9 us (4%)
  starting transfers between devices  7.17 us (2%)
  matrix products  5.3 us (2%)
    all_gather x1, blocking collectives, per_device(): lax.all_gather(a_master, 'row', axis=0, tiled=True)  76.8 us
    all_gather x1, blocking collectives, per_device(): lax.all_gather(bt_master, 'col', axis=0, tiled=True)  39.6 us
    unnamed x18, local copies, waits for them, and re-layouts  34 us
    all_gather x1, blocking collectives, per_device(): lax.all_gather(a_second, 'row', axis=0, tiled=True)  28.3 us
    all_gather x1, blocking collectives, per_device(): lax.all_gather(a_first, 'row', axis=0, tiled=True)  28.2 us
    unnamed x1, other arithmetic  26 us
    all_gather x1, blocking collectives, per_device(): lax.all_gather(bt_first, 'col', axis=0, tiled=True)  20.9 us
    all_gather x1, blocking collectives, per_device(): lax.all_gather(bt_second, 'col', axis=0, tiled=True)  18.9 us
  transfers between devices with their start and end apart: 4, of which 0 were waited for; matrix products, arithmetic and copies ran while one was open for 24% of the time, Pallas kernels for 0%

commit v1 on v0

v1 whole, which is shorter than its diff:
```python
import math

import jax
import jax.numpy as jnp
from jax import lax
from jax.experimental import pallas as pl
from jax.experimental.pallas import tpu as pltpu
from jax.sharding import PartitionSpec as P

D = 16384
R = 64
TP = 8
STEP = 10


beta_first = 0.9
beta_second = 0.95
adam_eps = 1e-08
learn_rate = 0.08


def adapter_factor():
    return 0.25 / math.sqrt(R * D)


def adam_step(master, first, second, grad):
    first_new = beta_first * first + (1.0 - beta_first) * grad
    second_new = beta_second * second + (1.0 - beta_second) * grad * grad
    corr_first = 1.0 - beta_first**STEP
    corr_second = 1.0 - beta_second**STEP
    update = first_new / corr_first / (jnp.sqrt(second_new / corr_second) + adam_eps)
    return (master - learn_rate * update, first_new, second_new)


def merge_kernel(bt_ref, *refs):
    *a_refs, frozen_ref, saved_ref = refs
    a_block = jnp.concatenate([ref[...].reshape(16, 1024) for ref in a_refs], axis=0)
    increment = lax.dot_general(
        bt_ref[...], a_block, (((0,), (0,)), ((), ())), preferred_element_type=jnp.float32
    )
    frozen = frozen_ref[...].reshape(128, 1024).astype(jnp.float32)
    merged = frozen + adapter_factor() * increment
    saved_ref[...] = merged.astype(jnp.bfloat16).reshape(1, 128, 1024)


def merge(bt_rows, a_parts, arrived):
    return pl.pallas_call(
        merge_kernel,
        grid=(16,),
        in_specs=[pl.BlockSpec((64, 128), lambda k: (0, 0))]
        + [pl.BlockSpec((1, 16, 1024), lambda k: (k, 0, 0))] * 4
        + [pl.BlockSpec((1, 128, 1024), lambda k: (k, 0, 0))],
        out_specs=pl.BlockSpec((1, 128, 1024), lambda k: (k // 2, 0, k % 2)),
        out_shape=jax.ShapeDtypeStruct((8, 128, 2048), jnp.bfloat16),
        cost_estimate=pl.CostEstimate(flops=2 * 128 * 64 * 16384, bytes_accessed=10 << 20, transcendentals=0),
    )(bt_rows, *a_parts, arrived)


def per_device(
    frozen_projection_weight,
    a_master,
    a_first,
    a_second,
    bt_master,
    bt_first,
    bt_second,
    grad_a_parts,
    grad_bt_parts,
):
    z = lax.axis_index("row") % 4
    arrived = lax.all_to_all(
        frozen_projection_weight.reshape(16, 128, 1024), "col", 0, 0, tiled=True
    )
    grad_a = lax.all_to_all(grad_a_parts.reshape(8, 8, 1024), "row", 0, 0, tiled=True).sum(0)
    grad_bt = lax.all_to_all(grad_bt_parts.reshape(16, 4, 2048), "col", 0, 0, tiled=True).sum(0)
    a_new, a_first_new, a_second_new = adam_step(a_master, a_first, a_second, grad_a)
    bt_new, bt_first_new, bt_second_new = adam_step(bt_master, bt_first, bt_second, grad_bt)
    a_half = a_new.astype(jnp.bfloat16)
    bt_half = bt_new.astype(jnp.bfloat16)

    low = lax.axis_index("row") < 4
    a_other = lax.ppermute(a_half, "row", [(i, i ^ 4) for i in range(8)])
    a_pair = jnp.where(low, jnp.concatenate([a_half, a_other]), jnp.concatenate([a_other, a_half]))
    a_cols = lax.all_to_all(jnp.broadcast_to(a_pair[None], (16, 16, 1024)), "col", 0, 0, tiled=True)
    a_parts = [a_cols] + [
        lax.ppermute(a_cols, "row", [(i, i // 4 * 4 + (i + k) % 4) for i in range(8)])
        for k in (1, 2, 3)
    ]
    bt_rows = lax.all_to_all(
        bt_half.reshape(4, 16, 128).transpose(1, 0, 2), "col", 0, 0, tiled=True
    ).reshape(2, 4, 8, 128)
    bt_order = jnp.concatenate(
        [
            lax.dynamic_index_in_dim(bt_rows, (z - k) % 4, 1, keepdims=False).reshape(16, 128)
            for k in range(4)
        ]
    )
    saved = merge(bt_order, a_parts, arrived)
    return (saved, a_new, a_first_new, a_second_new, bt_new, bt_first_new, bt_second_new)


def solution(mesh):
    return jax.shard_map(
        per_device,
        mesh=mesh,
        in_specs=(
            P("row", "col"),
            P("row", "col"),
            P("row", "col"),
            P("row", "col"),
            P("col", "row"),
            P("col", "row"),
            P("col", "row"),
            P("row", None, "col"),
            P("col", None, "row"),
        ),
        out_specs=(
            P(None, ("row", "col"), None),
            P("row", "col"),
            P("row", "col"),
            P("row", "col"),
            P("col", "row"),
            P("col", "row"),
            P("col", "row"),
        ),
        check_vma=False,
    )
```

time: 319 us -> 127 us (0.40)
  blocking collectives: 213 us -> 12.7 us
  waiting for transfers between devices: 1.4 us -> 66.2 us
  local copies, waits for them, and re-layouts: 47.9 us -> 2.05 us
  other arithmetic: 29.5 us -> 3.64 us
  starting transfers between devices: 7.17 us -> 27.7 us
  between operations: 13.9 us -> 0.67 us
  Pallas kernels: 0 us -> 12.6 us
  matrix products: 5.3 us -> 0 us
    all_gather x6 -> x0, blocking collectives: 213 us -> none  [the longest x1 76.8 us: per_device(): lax.all_gather(a_master, 'row', axis=0, tiled=True)]
    all_to_all x1 -> x4, waiting for transfers between devices: 0.01 us -> 41.3 us  [the longest x1 22.5 us: per_device(): lax.all_to_all(frozen_projection_weight.reshape(16, 128, 1024), 'col', 0,...]
    unnamed x18 -> x8, local copies, waits for them, and re-layouts: 34 us -> 0.01 us
    unnamed x1 -> x0, other arithmetic: 26 us -> none
    ppermute x0 -> x4, waiting for transfers between devices: none -> 24.9 us  [the longest x3 24.9 us: per_device(): lax.ppermute(a_cols, 'row', [(i, i // 4 * 4 + (i + k) % 4) for i in range...]
    all_to_all x1 -> x4, starting transfers between devices: 7.06 us -> 25 us  [the longest x1 8.34 us: per_device(): lax.all_to_all(grad_a_parts.reshape(8, 8, 1024), 'row', 0, 0, tiled=True)]
    all_to_all x0 -> x1, blocking collectives: none -> 12.7 us  [per_device(): lax.all_to_all(jnp.broadcast_to(a_pair[None], (16, 16, 1024)), 'col', 0,...]
    pallas_call x0 -> x1, Pallas kernels: none -> 12.6 us  [merge(): pl.pallas_call(merge_kernel, grid=(16,), in_specs=[pl.BlockSpec((64, 128)...]
  transfers between devices with their start and end apart: 4 -> 8, of which waited for: 0 -> 7; matrix products, arithmetic and copies ran while one was open for 24% -> 4% of each run, Pallas kernels for 0% -> 0%
where the time goes in v1:
time: 127 us; the launch traced here: 126 us
  waiting for transfers between devices  66.2 us (52%)
  starting transfers between devices  27.7 us (22%)
  blocking collectives  12.7 us (10%)
  Pallas kernels  12.6 us (10%)
  other arithmetic  3.64 us (3%)
  local copies, waits for them, and re-layouts  2.05 us (2%)
    ppermute x3, waiting for transfers between devices, per_device(): lax.ppermute(a_cols, 'row', [(i, i // 4 * 4 + (i + k) % 4) for i in range...  24.9 us
    all_to_all x1, waiting for transfers between devices, per_device(): lax.all_to_all(frozen_projection_weight.reshape(16, 128, 1024), 'col', 0,...  22.5 us
    all_to_all x1, blocking collectives, per_device(): lax.all_to_all(jnp.broadcast_to(a_pair[None], (16, 16, 1024)), 'col', 0,...  12.7 us
    pallas_call x1, Pallas kernels, merge(): pl.pallas_call(merge_kernel, grid=(16,), in_specs=[pl.BlockSpec((64, 128)...  12.6 us
    all_to_all x1, starting transfers between devices, per_device(): lax.all_to_all(grad_a_parts.reshape(8, 8, 1024), 'row', 0, 0, tiled=True)  8.34 us
    all_to_all x1, waiting for transfers between devices, per_device(): lax.all_to_all(grad_bt_parts.reshape(16, 4, 2048), 'col', 0, 0, tiled=True)  7.35 us
    all_to_all x1, starting transfers between devices, per_device(): lax.all_to_all(grad_bt_parts.reshape(16, 4, 2048), 'col', 0, 0, tiled=True)  6.62 us
    all_to_all x1, waiting for transfers between devices, per_device(): lax.all_to_all(bt_half.reshape(4, 16, 128).transpose(1, 0, 2), 'col', 0,...  5.81 us
  transfers between devices with their start and end apart: 8, of which 7 were waited for; matrix products, arithmetic and copies ran while one was open for 4% of the time, Pallas kernels for 0%

profile of v1, /device:TPU:1, one launch (start us, length us, event | category | flops | bytes accessed | tf_op | source)
XLA Modules:
  0.0 125.5 jit_solution(15946820812672857772)
XLA Ops:
  0.6 8.3 %all-to-all-start.2 = ((f32[8,8,1024]{2,1,0:T(8,128)}), f32[8,8,1024]{2,1,0:T(8,128)S(1)}, u32[]{:S(2)}, u32[]{:S(2)}) async-start(f32[8,8,1024]{2,1,0:T(8,128)} %bitcast.16), calls=%async_computation.2 | async-start | bytes 524288 | tf_op jit(solution)/shard_map/all_to_all | solution.py:74
  9.0 2.0 %reshape.74 = f32[16,4,2048]{2,1,0:T(4,128)} reshape(f32[1,64,2048]{2,1,0:T(8,128)} %param.17) | data formatting | bytes 1048576 | tf_op jit(solution)/shard_map/reshape | solution.py:75
  10.9 5.6 %all-to-all-done.2 = f32[8,8,1024]{2,1,0:T(8,128)S(1)} async-done(((f32[8,8,1024]{2,1,0:T(8,128)}), f32[8,8,1024]{2,1,0:T(8,128)S(1)}, u32[]{:S(2)}, u32[]{:S(2)}) %all-to-all-start.2) | async-done | bytes 262176 | tf_op jit(solution)/shard_map/all_to_all | solution.py:74
  16.5 6.6 %all-to-all-start = ((f32[16,4,2048]{2,1,0:T(4,128)}), f32[16,4,2048]{2,1,0:T(4,128)S(1)}, u32[]{:S(2)}, u32[]{:S(2)}) async-start(f32[16,4,2048]{2,1,0:T(4,128)} %reshape.74), calls=%async_computation | async-start | bytes 1048576 | tf_op jit(solution)/shard_map/all_to_all | solution.py:75
  23.2 1.4 %fusion.2 = (bf16[8,1024]{1,0:T(8,128)(2,1)S(1)}, f32[8,1024]{1,0:T(8,128)}, f32[8,1024]{1,0:T(8,128)}, f32[8,1024]{1,0:T(8,128)}) fusion(f32[8,1024]{1,0:T(8,128)} %param.10, f32[8,1024]{1,0:T(8,128)S(1)} %reduce_sum.19, f32[8,1024]{1,0:T(8,128)} %param.11, f32[8,1024]{1,0:T(8,128)} %param.12), kind=kLoop, calls=%fused_computation.16 | loop fusion | flops 114688 | bytes 245760 | tf_op jit(solution)/shard_map/convert_element_type | solution.py:78
  24.6 1.0 collective-permute-start
  25.6 7.4 %all-to-all-done = f32[16,4,2048]{2,1,0:T(4,128)S(1)} async-done(((f32[16,4,2048]{2,1,0:T(4,128)}), f32[16,4,2048]{2,1,0:T(4,128)S(1)}, u32[]{:S(2)}, u32[]{:S(2)}) %all-to-all-start) | async-done | bytes 524320 | tf_op jit(solution)/shard_map/all_to_all | solution.py:75
  33.0 0.1 reduce_sum.18
  33.1 1.5 %convert_bitcast_fusion = (bf16[16,4,128]{2,1,0:T(4,128)(2,1)}, f32[4,2048]{1,0:T(4,128)}, f32[4,2048]{1,0:T(4,128)}, f32[4,2048]{1,0:T(4,128)}) fusion(f32[4,2048]{1,0:T(4,128)} %param.13, f32[4,2048]{1,0:T(4,128)S(1)} %reduce_sum.18, f32[4,2048]{1,0:T(4,128)} %param.14, f32[4,2048]{1,0:T(4,128)} %param.15), kind=kLoop, calls=%fused_computation.11 | loop fusion | flops 114688 | bytes 245760 | tf_op jit(solution)/shard_map/transpose | solution.py:90
  34.5 4.6 %all-to-all-start.1 = ((bf16[16,4,128]{2,1,0:T(4,128)(2,1)}), bf16[16,4,128]{2,1,0:T(4,128)(2,1)S(1)}, u32[]{:S(2)}, u32[]{:S(2)}) async-start(bf16[16,4,128]{2,1,0:T(4,128)(2,1)} %get-tuple-element.11), calls=%async_computation.1 | async-start | bytes 32768 | tf_op jit(solution)/shard_map/all_to_all | solution.py:89
  39.2 0.0 collective-permute-done
  39.2 5.8 %all-to-all-done.1 = bf16[16,4,128]{2,1,0:T(4,128)(2,1)S(1)} async-done(((bf16[16,4,128]{2,1,0:T(4,128)(2,1)}), bf16[16,4,128]{2,1,0:T(4,128)(2,1)S(1)}, u32[]{:S(2)}, u32[]{:S(2)}) %all-to-all-start.1) | async-done | bytes 16416 | tf_op jit(solution)/shard_map/all_to_all | solution.py:89
  45.1 12.7 %all_to_all.25.refs_0_ = bf16[16,16,1024]{2,1,0:T(8,128)(2,1)S(1)} all-to-all(bf16[16,16,1024]{2,1,0:T(8,128)(2,1)S(1)} %broadcast_in_dim.2), channel_id=1, replica_groups=mesh['row'=8,'col'=16] {'col'}, dimensions={0} | all-to-all | bytes 1048576 | tf_op jit(solution)/shard_map/all_to_all | solution.py:84
  57.8 0.0 copy-start
  57.8 5.4 %all-to-all-start.4 = ((bf16[16,128,1024]{2,1,0:T(8,128)(2,1)}), bf16[16,128,1024]{2,1,0:T(8,128)(2,1)}, u32[]{:S(2)}, u32[]{:S(2)}) async-start(bf16[16,128,1024]{2,1,0:T(8,128)(2,1)} %bitcast.15), calls=%async_computation.4 | async-start | bytes 8388608 | tf_op jit(solution)/shard_map/all_to_all | solution.py:71
  63.2 0.5 collective-permute-start.3
  63.7 1.2 collective-permute-start.2
  64.9 0.0 copy-done
  64.9 0.0 collective-permute-start.1
  64.9 0.6 pad_maximum_fusion.bt_ref
  65.5 10.9 %collective-permute-done.3.refs_3_ = bf16[16,16,1024]{2,1,0:T(8,128)(2,1)S(1)} collective-permute-done((bf16[16,16,1024]{2,1,0:T(8,128)(2,1)S(1)}, bf16[16,16,1024]{2,1,0:T(8,128)(2,1)S(1)}, u32[]{:S(2)}, u32[]{:S(2)}) %collective-permute-start.3) | collective-permute-done | bytes 524320 | tf_op jit(solution)/shard_map/ppermute | solution.py:86
  76.5 0.0 copy-start.1
  76.5 1.7 %collective-permute-done.2.refs_2_ = bf16[16,16,1024]{2,1,0:T(8,128)(2,1)S(1)} collective-permute-done((bf16[16,16,1024]{2,1,0:T(8,128)(2,1)S(1)}, bf16[16,16,1024]{2,1,0:T(8,128)(2,1)S(1)}, u32[]{:S(2)}, u32[]{:S(2)}) %collective-permute-start.2) | collective-permute-done | bytes 524320 | tf_op jit(solution)/shard_map/ppermute | solution.py:86
  78.1 0.0 copy-start.2
  78.1 12.3 %collective-permute-done.1.refs_1_ = bf16[16,16,1024]{2,1,0:T(8,128)(2,1)S(1)} collective-permute-done((bf16[16,16,1024]{2,1,0:T(8,128)(2,1)S(1)}, bf16[16,16,1024]{2,1,0:T(8,128)(2,1)S(1)}, u32[]{:S(2)}, u32[]{:S(2)}) %collective-permute-start.1) | collective-permute-done | bytes 524320 | tf_op jit(solution)/shard_map/ppermute | solution.py:86
  90.4 0.0 copy-start.3
  90.4 22.5 %all-to-all-done.4.refs_4_ = bf16[16,128,1024]{2,1,0:T(8,128)(2,1)} async-done(((bf16[16,128,1024]{2,1,0:T(8,128)(2,1)}), bf16[16,128,1024]{2,1,0:T(8,128)(2,1)}, u32[]{:S(2)}, u32[]{:S(2)}) %all-to-all-start.4) | async-done | bytes 4194336 | tf_op jit(solution)/shard_map/all_to_all | solution.py:71
  113.0 0.0 copy-done.1
  113.0 0.0 copy-done.2
  113.0 0.0 copy-done.3
  113.0 12.6 %shard_map.144 = bf16[8,128,2048]{2,1,0:T(8,128)(2,1)} custom-call(bf16[64,128]{1,0:T(8,128)(2,1)} %pad_maximum_fusion.bt_ref, bf16[16,16,1024]{2,1,0:T(8,128)(2,1)} %copy-done, bf16[16,16,1024]{2,1,0:T(8,128)(2,1)} %copy-done.3, bf16[16,16,1024]{2,1,0:T(8,128)(2,1)} %copy-done.2, bf16[16,16,1024]{2,1,0:T(8,128)(2,1)} %copy-done.1, ...), custom_call_target="tpu_custom_call" | custom-call | flops 268435456 | bytes 10485760 | tf_op jit(solution)/shard_map/pallas_call | solution.py:47
  (4 shorter events, 0.1 us)
Async XLA Ops:
  0.6 15.9 %all-to-all-start.2 = ((f32[8,8,1024]{2,1,0:T(8,128)}), f32[8,8,1024]{2,1,0:T(8,128)S(1)}, u32[]{:S(2)}, u32[]{:S(2)}) async-start(f32[8,8,1024]{2,1,0:T(8,128)} %bitcast.16), calls=%async_computation.2 | async-start | bytes 524288 | tf_op jit(solution)/shard_map/all_to_all | solution.py:74
  16.5 16.4 %all-to-all-start = ((f32[16,4,2048]{2,1,0:T(4,128)}), f32[16,4,2048]{2,1,0:T(4,128)S(1)}, u32[]{:S(2)}, u32[]{:S(2)}) async-start(f32[16,4,2048]{2,1,0:T(4,128)} %reshape.74), calls=%async_computation | async-start | bytes 1048576 | tf_op jit(solution)/shard_map/all_to_all | solution.py:75
  24.6 14.5 %collective-permute-start = (bf16[8,1024]{1,0:T(8,128)(2,1)S(1)}, bf16[8,1024]{1,0:T(8,128)(2,1)S(1)}, u32[]{:S(2)}, u32[]{:S(2)}) collective-permute-start(bf16[8,1024]{1,0:T(8,128)(2,1)S(1)} %get-tuple-element.7), channel_id=1, source_target_pairs={{0,64},{16,80},{32,96},{48,112},{64,0},{80,16},{96,32},{112,48},{1... | collective-permute-start | bytes 49160 | tf_op jit(solution)/shard_map/ppermute | solution.py:82
  34.5 10.5 %all-to-all-start.1 = ((bf16[16,4,128]{2,1,0:T(4,128)(2,1)}), bf16[16,4,128]{2,1,0:T(4,128)(2,1)S(1)}, u32[]{:S(2)}, u32[]{:S(2)}) async-start(bf16[16,4,128]{2,1,0:T(4,128)(2,1)} %get-tuple-element.11), calls=%async_computation.1 | async-start | bytes 32768 | tf_op jit(solution)/shard_map/all_to_all | solution.py:89
  57.8 7.2 %copy-start = (bf16[16,16,1024]{2,1,0:T(8,128)(2,1)}, bf16[16,16,1024]{2,1,0:T(8,128)(2,1)S(1)}, u32[]{:S(2)}) copy-start(bf16[16,16,1024]{2,1,0:T(8,128)(2,1)S(1)} %all_to_all.25.refs_0_) | copy-start | bytes 1572868
  57.8 55.2 %all-to-all-start.4 = ((bf16[16,128,1024]{2,1,0:T(8,128)(2,1)}), bf16[16,128,1024]{2,1,0:T(8,128)(2,1)}, u32[]{:S(2)}, u32[]{:S(2)}) async-start(bf16[16,128,1024]{2,1,0:T(8,128)(2,1)} %bitcast.15), calls=%async_computation.4 | async-start | bytes 8388608 | tf_op jit(solution)/shard_map/all_to_all | solution.py:71
  63.2 13.3 %collective-permute-start.3 = (bf16[16,16,1024]{2,1,0:T(8,128)(2,1)S(1)}, bf16[16,16,1024]{2,1,0:T(8,128)(2,1)S(1)}, u32[]{:S(2)}, u32[]{:S(2)}) collective-permute-start(bf16[16,16,1024]{2,1,0:T(8,128)(2,1)S(1)} %all_to_all.25.refs_0_), channel_id=1, source_target_pairs={{0,48},{16,0},{32,16},{48,32},{64,112},{80,64},{96,80},{112,96},{1... | collective-permute-start | bytes 1572872 | tf_op jit(solution)/shard_map/ppermute | solution.py:86
  63.7 14.4 %collective-permute-start.2 = (bf16[16,16,1024]{2,1,0:T(8,128)(2,1)S(1)}, bf16[16,16,1024]{2,1,0:T(8,128)(2,1)S(1)}, u32[]{:S(2)}, u32[]{:S(2)}) collective-permute-start(bf16[16,16,1024]{2,1,0:T(8,128)(2,1)S(1)} %all_to_all.25.refs_0_), channel_id=1, source_target_pairs={{0,32},{16,48},{32,0},{48,16},{64,96},{80,112},{96,64},{112,80},{1... | collective-permute-start | bytes 1572872 | tf_op jit(solution)/shard_map/ppermute | solution.py:86
  64.9 25.5 %collective-permute-start.1 = (bf16[16,16,1024]{2,1,0:T(8,128)(2,1)S(1)}, bf16[16,16,1024]{2,1,0:T(8,128)(2,1)S(1)}, u32[]{:S(2)}, u32[]{:S(2)}) collective-permute-start(bf16[16,16,1024]{2,1,0:T(8,128)(2,1)S(1)} %all_to_all.25.refs_0_), channel_id=1, source_target_pairs={{0,16},{16,32},{32,48},{48,0},{64,80},{80,96},{96,112},{112,64},{1... | collective-permute-start | bytes 1572872 | tf_op jit(solution)/shard_map/ppermute | solution.py:86
  76.5 36.5 %copy-start.1 = (bf16[16,16,1024]{2,1,0:T(8,128)(2,1)}, bf16[16,16,1024]{2,1,0:T(8,128)(2,1)S(1)}, u32[]{:S(2)}) copy-start(bf16[16,16,1024]{2,1,0:T(8,128)(2,1)S(1)} %collective-permute-done.3.refs_3_) | copy-start | bytes 1572868
  78.1 34.9 %copy-start.2 = (bf16[16,16,1024]{2,1,0:T(8,128)(2,1)}, bf16[16,16,1024]{2,1,0:T(8,128)(2,1)S(1)}, u32[]{:S(2)}) copy-start(bf16[16,16,1024]{2,1,0:T(8,128)(2,1)S(1)} %collective-permute-done.2.refs_2_) | copy-start | bytes 1572868
  90.4 22.6 %copy-start.3 = (bf16[16,16,1024]{2,1,0:T(8,128)(2,1)}, bf16[16,16,1024]{2,1,0:T(8,128)(2,1)S(1)}, u32[]{:S(2)}) copy-start(bf16[16,16,1024]{2,1,0:T(8,128)(2,1)S(1)} %collective-permute-done.1.refs_1_) | copy-start | bytes 1572868

commit v2 on v1

v2 whole, which is shorter than its diff:
```python
import math

import jax
import jax.numpy as jnp
from jax import lax
from jax.experimental import pallas as pl
from jax.experimental.pallas import tpu as pltpu
from jax.sharding import PartitionSpec as P

D = 16384
R = 64
TP = 8
STEP = 10


beta_first = 0.9
beta_second = 0.95
adam_eps = 1e-08
learn_rate = 0.08


def adapter_factor():
    return 0.25 / math.sqrt(R * D)


def adam_step(master, first, second, grad):
    first_new = beta_first * first + (1.0 - beta_first) * grad
    second_new = beta_second * second + (1.0 - beta_second) * grad * grad
    corr_first = 1.0 - beta_first**STEP
    corr_second = 1.0 - beta_second**STEP
    update = first_new / corr_first / (jnp.sqrt(second_new / corr_second) + adam_eps)
    return (master - learn_rate * update, first_new, second_new)


def mod4(value):
    return lax.rem(value + 4, 4)


def rank_order(y, x, core, x_hi, z):
    p = lax.broadcasted_iota(jnp.int32, (R, R), 0)
    s = lax.broadcasted_iota(jnp.int32, (R, R), 1)
    from_z = (z - p // 16 + 4) % 4
    from_x_hi = x_hi ^ ((p // 8) % 2)
    rank_a = 8 * (from_x_hi * 4 + from_z) + p % 8
    from_y = (y - s // 16 + 4) % 4
    from_x = x ^ ((s // 8) % 2)
    from_core = core ^ ((s // 4) % 2)
    rank_b = 4 * (from_y * 4 + from_x * 2 + from_core) + s % 4
    return (rank_a == rank_b).astype(jnp.bfloat16)


def merge_kernel(bt_ref, *refs):
    a_refs, arrived_ref, saved_ref = refs[:8], refs[8], refs[9]
    a_buf, in_buf, out_buf, a_sem, in_sem, out_sem = refs[10:]
    row, col = lax.axis_index("row"), lax.axis_index("col")
    x_hi, z = row // 4, row % 4
    y, x, core = col // 4, (col // 2) % 2, col % 2

    def source(step):
        k_core, k_y, k_x = step // 8, (step // 2) % 4, step % 2
        return mod4(y - k_y) * 4 + (x ^ k_x) * 2 + (core ^ k_core)

    a_copies = [pltpu.make_async_copy(a_refs[i], a_buf.at[i], a_sem.at[i]) for i in range(8)]
    in_copies = [
        pltpu.make_async_copy(arrived_ref.at[source(s)], in_buf.at[s], in_sem.at[s])
        for s in range(16)
    ]
    out_copies = [
        pltpu.make_async_copy(
            out_buf.at[s],
            saved_ref.at[source(s) // 2, :, pl.ds((source(s) % 2) * 1024, 1024)],
            out_sem.at[s],
        )
        for s in range(16)
    ]
    for copy in a_copies[:4] + in_copies[:8] + a_copies[4:] + in_copies[8:]:
        copy.start()
    left = lax.dot_general(
        bt_ref[...].astype(jnp.bfloat16),
        rank_order(y, x, core, x_hi, z),
        (((0,), (1,)), ((), ())),
        preferred_element_type=jnp.float32,
    ).astype(jnp.bfloat16)
    for s in range(16):
        k_core, k_y, k_x = s // 8, (s // 2) % 4, s % 2
        if s % 8 == 0:
            for copy in a_copies[4 * k_core : 4 * k_core + 4]:
                copy.wait()
        a_block = jnp.concatenate(
            [
                a_buf[4 * k_core + k_z, k_x_hi, k_y, k_x ^ k_x_hi]
                for k_z in range(4)
                for k_x_hi in range(2)
            ],
            axis=0,
        )
        increment = lax.dot_general(
            left, a_block, (((1,), (0,)), ((), ())), preferred_element_type=jnp.float32
        )
        in_copies[s].wait()
        merged = in_buf[s].astype(jnp.float32) + adapter_factor() * increment
        out_buf[s] = merged.astype(jnp.bfloat16)
        out_copies[s].start()
    for copy in out_copies:
        copy.wait()


def merge(bt_rows, a_parts, arrived):
    return pl.pallas_call(
        merge_kernel,
        in_specs=[pl.BlockSpec(memory_space=pltpu.VMEM)] + [pl.BlockSpec(memory_space=pl.ANY)] * 9,
        out_specs=pl.BlockSpec(memory_space=pl.ANY),
        out_shape=jax.ShapeDtypeStruct((8, 128, 2048), jnp.bfloat16),
        scratch_shapes=[
            pltpu.VMEM((8, 2, 4, 2, 8, 1024), jnp.bfloat16),
            pltpu.VMEM((16, 128, 1024), jnp.bfloat16),
            pltpu.VMEM((16, 128, 1024), jnp.bfloat16),
            pltpu.SemaphoreType.DMA((8,)),
            pltpu.SemaphoreType.DMA((16,)),
            pltpu.SemaphoreType.DMA((16,)),
        ],
        compiler_params=pltpu.CompilerParams(vmem_limit_bytes=56 << 20),
        cost_estimate=pl.CostEstimate(
            flops=2 * 128 * 64 * 16384, bytes_accessed=10 << 20, transcendentals=0
        ),
    )(bt_rows, *a_parts, arrived)


def pick(array, index, axis):
    return lax.dynamic_index_in_dim(array, index, axis, keepdims=False)


def over_core(array):
    return lax.ppermute(array, "col", [(i, i ^ 1) for i in range(16)])


def over_x(array):
    return lax.ppermute(array, "col", [(i, i ^ 2) for i in range(16)])


def over_y(array, k):
    return lax.ppermute(array, "col", [(i, (i + 4 * k) % 16) for i in range(16)])


def over_x_y(array, k_x, k_y):
    return lax.ppermute(array, "col", [(i, ((i + 4 * k_y) % 16) ^ (2 * k_x)) for i in range(16)])


def over_x_hi(array):
    return lax.ppermute(array, "row", [(i, i ^ 4) for i in range(8)])


def over_x_hi_x(array):
    return lax.ppermute(array, ("row", "col"), [(i, i ^ (4 * 16 + 2)) for i in range(128)])


def over_z(array, k):
    return lax.ppermute(array, "row", [(i, i // 4 * 4 + (i + k) % 4) for i in range(8)])


def per_device(
    frozen_projection_weight,
    a_master,
    a_first,
    a_second,
    bt_master,
    bt_first,
    bt_second,
    grad_a_parts,
    grad_bt_parts,
):
    row, col = lax.axis_index("row"), lax.axis_index("col")
    x_hi, z = row // 4, row % 4
    y, x, core = col // 4, (col // 2) % 2, col % 2

    part = grad_a_parts.reshape(2, 4, 8, 1024)
    part = pick(part, z, 1) + sum(over_z(pick(part, (z + k) % 4, 1), k) for k in (1, 2, 3))
    grad_a = pick(part, x_hi, 0) + over_x_hi(pick(part, 1 - x_hi, 0))
    part = grad_bt_parts.reshape(4, 2, 2, 4, 2048)
    part = pick(part, core, 2) + over_core(pick(part, 1 - core, 2))
    part = pick(part, x, 1) + over_x(pick(part, 1 - x, 1))
    grad_bt = pick(part, y, 0) + sum(over_y(pick(part, (y + k) % 4, 0), k) for k in (1, 2, 3))

    a_new, a_first_new, a_second_new = adam_step(a_master, a_first, a_second, grad_a)
    bt_new, bt_first_new, bt_second_new = adam_step(bt_master, bt_first, bt_second, grad_bt)

    part = bt_new.reshape(4, 4, 2, 2, 128).transpose(1, 2, 3, 0, 4)
    part = jnp.concatenate([pick(part, core, 2), over_core(pick(part, 1 - core, 2))], axis=2)
    bt_for = part.astype(jnp.bfloat16)
    a_half = a_new.astype(jnp.bfloat16)
    sent = pick(bt_for, 1 - x, 1).transpose(1, 0, 2).reshape(8, 512)
    came = over_x(jnp.concatenate([a_half, sent], axis=1))
    a_near = jnp.stack([a_half, came[:, :1024]])
    bt_near = jnp.stack([pick(bt_for, x, 1), came[:, 1024:].reshape(8, 4, 128).transpose(1, 0, 2)], axis=1)
    along_y = [
        over_y(jnp.concatenate([a_near, pick(bt_near, (y + k) % 4, 0)], axis=2), k) for k in (1, 2, 3)
    ]
    weight = frozen_projection_weight.reshape(16, 128, 1024)
    weight, *along_y = lax.optimization_barrier((weight, *along_y))
    arrived = lax.all_to_all(weight, "col", 0, 0, tiled=True)
    part = jnp.stack([a_near] + [came[:, :, :1024] for came in along_y])
    bt_rows = jnp.stack([pick(bt_near, y, 0)] + [came[:, :, 1024:] for came in along_y])
    part = jnp.stack([part, over_x_hi_x(part)])
    a_parts = [part] + [over_z(part, k) for k in (1, 2, 3)]
    a_parts = a_parts + [over_core(part) for part in a_parts]
    saved = merge(bt_rows.reshape(R, 128).astype(jnp.float32), a_parts, arrived)
    return (saved, a_new, a_first_new, a_second_new, bt_new, bt_first_new, bt_second_new)


def solution(mesh):
    return jax.shard_map(
        per_device,
        mesh=mesh,
        in_specs=(
            P("row", "col"),
            P("row", "col"),
            P("row", "col"),
            P("row", "col"),
            P("col", "row"),
            P("col", "row"),
            P("col", "row"),
            P("row", None, "col"),
            P("col", None, "row"),
        ),
        out_specs=(
            P(None, ("row", "col"), None),
            P("row", "col"),
            P("row", "col"),
            P("row", "col"),
            P("col", "row"),
            P("col", "row"),
            P("col", "row"),
        ),
        check_vma=False,
    )
```

time: 127 us -> 102 us (0.80)
  waiting for transfers between devices: 66.2 us -> 43.1 us
  starting transfers between devices: 27.7 us -> 44.1 us
  blocking collectives: 12.7 us -> 0 us
  Pallas kernels: 12.6 us -> 7.91 us
    ppermute x4 -> x22, starting transfers between devices: 2.7 us -> 35.9 us  [the longest x6 13.6 us: over_core(): return lax.ppermute(array, 'col', [(i, i ^ 1) for i in range(16)])]
    all_to_all x4 -> x1, waiting for transfers between devices: 41.3 us -> 24.2 us  [per_device(): arrived = lax.all_to_all(weight, 'col', 0, 0, tiled=True)]
    all_to_all x4 -> x1, starting transfers between devices: 25 us -> 8.21 us  [per_device(): arrived = lax.all_to_all(weight, 'col', 0, 0, tiled=True)]
    all_to_all x1 -> x0, blocking collectives: 12.7 us -> none  [per_device(): lax.all_to_all(jnp.broadcast_to(a_pair[None], (16, 16, 1024)), 'col', 0,...]
    ppermute x4 -> x22, waiting for transfers between devices: 24.9 us -> 18.9 us  [the longest x6 8.33 us: over_z(): lax.ppermute(array, 'row', [(i, i // 4 * 4 + (i + k) % 4) for i in range(...]
    pallas_call x1, Pallas kernels: 12.6 us -> 7.91 us  [merge(): pl.pallas_call(merge_kernel, in_specs=[pl.BlockSpec(memory_space=pltpu.VM...]
    transpose x1 -> x0, other arithmetic: 1.47 us -> none  [per_device(): bt_half.reshape(4, 16, 128).transpose(1, 0, 2)]
  transfers between devices with their start and end apart: 8 -> 23, of which waited for: 7 -> 14; matrix products, arithmetic and copies ran while one was open for 4% -> 4% of each run, Pallas kernels for 0% -> 0%
where the time goes in v2:
time: 102 us; the launch traced here: 101 us
  starting transfers between devices  44.1 us (43%)
  waiting for transfers between devices  43.1 us (42%)
  Pallas kernels  7.91 us (8%)
  other arithmetic  3.03 us (3%)
  local copies, waits for them, and re-layouts  2.35 us (2%)
    all_to_all x1, waiting for transfers between devices, per_device(): arrived = lax.all_to_all(weight, 'col', 0, 0, tiled=True)  24.2 us
    ppermute x6, starting transfers between devices, over_core(): return lax.ppermute(array, 'col', [(i, i ^ 1) for i in range(16)])  13.6 us
    ppermute x6, waiting for transfers between devices, over_z(): lax.ppermute(array, 'row', [(i, i // 4 * 4 + (i + k) % 4) for i in range(...  8.33 us
    all_to_all x1, starting transfers between devices, per_device(): arrived = lax.all_to_all(weight, 'col', 0, 0, tiled=True)  8.21 us
    pallas_call x1, Pallas kernels, merge(): pl.pallas_call(merge_kernel, in_specs=[pl.BlockSpec(memory_space=pltpu.VM...  7.91 us
    ppermute x6, starting transfers between devices, over_z(): lax.ppermute(array, 'row', [(i, i // 4 * 4 + (i + k) % 4) for i in range(...  7.84 us
    ppermute x6, starting transfers between devices, over_y(): lax.ppermute(array, 'col', [(i, (i + 4 * k) % 16) for i in range(16)])  6.09 us
    ppermute x6, waiting for transfers between devices, over_y(): lax.ppermute(array, 'col', [(i, (i + 4 * k) % 16) for i in range(16)])  4.57 us
  transfers between devices with their start and end apart: 23, of which 14 were waited for; matrix products, arithmetic and copies ran while one was open for 4% of the time, Pallas kernels for 0%

profile of v2, /device:TPU:1, one launch (start us, length us, event | category | flops | bytes accessed | tf_op | source)
XLA Modules:
  0.0 101.4 jit_solution(14124876477731624205)
XLA Ops:
  0.7 1.2 %reshape.35 = f32[4,2,2,4,2048]{4,3,2,1,0:T(4,128)S(1)} reshape(f32[1,64,2048]{2,1,0:T(8,128)} %param.17) | data formatting | bytes 1048576 | tf_op jit(solution)/shard_map/reshape | solution.py:179
  2.0 1.5 %collective-permute-start = (f32[4,2,4,2048]{3,2,1,0:T(4,128)S(1)}, f32[4,2,4,2048]{3,2,1,0:T(4,128)S(1)}, u32[]{:S(2)}, u32[]{:S(2)}) collective-permute-start(f32[4,2,4,2048]{3,2,1,0:T(4,128)S(1)} %dynamic-slice_bitcast_fusion), channel_id=1, source_target_pairs={{0,1},{1,0},{2,3},{3,2},{4,5},{5,4},{6,7},{7,6},{8,9},{9,8},{10,11... | collective-permute-start | bytes 786440 | tf_op jit(solution)/shard_map/ppermute | solution.py:134
  3.5 0.9 dynamic-slice_bitcast_fusion.3
  4.4 3.8 %collective-permute-start.7 = (f32[2,8,1024]{2,1,0:T(8,128)S(1)}, f32[2,8,1024]{2,1,0:T(8,128)S(1)}, u32[]{:S(2)}, u32[]{:S(2)}) collective-permute-start(f32[2,8,1024]{2,1,0:T(8,128)S(1)} %get-tuple-element.22), channel_id=1, source_target_pairs={{0,32},{16,48},{32,0},{48,16},{64,96},{80,112},{96,64},{112,80},{1... | collective-permute-start | bytes 196616 | tf_op jit(solution)/shard_map/ppermute | solution.py:158
  8.2 0.4 collective-permute-start.8
  8.6 1.0 %collective-permute-start.6 = (f32[2,8,1024]{2,1,0:T(8,128)S(1)}, f32[2,8,1024]{2,1,0:T(8,128)S(1)}, u32[]{:S(2)}, u32[]{:S(2)}) collective-permute-start(f32[2,8,1024]{2,1,0:T(8,128)S(1)} %get-tuple-element.24), channel_id=1, source_target_pairs={{0,16},{16,32},{32,48},{48,0},{64,80},{80,96},{96,112},{112,64},{1... | collective-permute-start | bytes 196616 | tf_op jit(solution)/shard_map/ppermute | solution.py:158
  9.6 0.1 bitcast_add_fusion
  9.7 1.3 %collective-permute-start.1 = (f32[4,4,2048]{2,1,0:T(4,128)S(1)}, f32[4,4,2048]{2,1,0:T(4,128)S(1)}, u32[]{:S(2)}, u32[]{:S(2)}) collective-permute-start(f32[4,4,2048]{2,1,0:T(4,128)S(1)} %dynamic-slice_bitcast_fusion.1), channel_id=1, source_target_pairs={{0,2},{1,3},{2,0},{3,1},{4,6},{5,7},{6,4},{7,5},{8,10},{9,11},{10,... | collective-permute-start | bytes 393224 | tf_op jit(solution)/shard_map/ppermute | solution.py:138
  11.0 1.5 %collective-permute-done.8 = f32[2,8,1024]{2,1,0:T(8,128)S(1)} collective-permute-done((f32[2,8,1024]{2,1,0:T(8,128)S(1)}, f32[2,8,1024]{2,1,0:T(8,128)S(1)}, u32[]{:S(2)}, u32[]{:S(2)}) %collective-permute-start.8) | collective-permute-done | bytes 65568 | tf_op jit(solution)/shard_map/ppermute | solution.py:158
  12.5 0.4 collective-permute-done.6
  12.9 0.9 bitcast_add_fusion.2
  13.8 0.1 collective-permute-done.1
  14.0 3.0 %collective-permute-start.3 = (f32[4,2048]{1,0:T(4,128)S(1)}, f32[4,2048]{1,0:T(4,128)S(1)}, u32[]{:S(2)}, u32[]{:S(2)}) collective-permute-start(f32[4,2048]{1,0:T(4,128)S(1)} %get-tuple-element.27), channel_id=1, source_target_pairs={{0,8},{1,9},{2,10},{3,11},{4,12},{5,13},{6,14},{7,15},{8,0},{9,1},... | collective-permute-start | bytes 98312 | tf_op jit(solution)/shard_map/ppermute | solution.py:142
  17.0 0.8 collective-permute-start.4
  17.8 0.7 collective-permute-start.2
  18.5 2.7 %collective-permute-start.9 = (f32[8,1024]{1,0:T(8,128)S(1)}, f32[8,1024]{1,0:T(8,128)S(1)}, u32[]{:S(2)}, u32[]{:S(2)}) collective-permute-start(f32[8,1024]{1,0:T(8,128)S(1)} %dynamic-slice_bitcast_fusion.5), channel_id=1, source_target_pairs={{0,64},{16,80},{32,96},{48,112},{64,0},{80,16},{96,32},{112,48},{1... | collective-permute-start | bytes 98312 | tf_op jit(solution)/shard_map/ppermute | solution.py:150
  21.2 0.5 collective-permute-done.2
  21.7 0.7 multiply_subtract_fusion.1
  22.5 3.6 %collective-permute-start.5 = (bf16[4,2,4,128]{3,2,1,0:T(4,128)(2,1)S(1)}, bf16[4,2,4,128]{3,2,1,0:T(4,128)(2,1)S(1)}, u32[]{:S(2)}, u32[]{:S(2)}) collective-permute-start(bf16[4,2,4,128]{3,2,1,0:T(4,128)(2,1)S(1)} %bitcast.98), channel_id=1, source_target_pairs={{0,1},{1,0},{2,3},{3,2},{4,5},{5,4},{6,7},{7,6},{8,9},{9,8},{10,11... | collective-permute-start | bytes 24584 | tf_op jit(solution)/shard_map/ppermute | solution.py:134
  26.1 0.0 collective-permute-done.9
  26.1 0.7 fusion.14
  26.8 0.1 collective-permute-done.5
  27.0 1.3 %collective-permute-start.10 = (bf16[8,1536]{1,0:T(8,128)(2,1)S(1)}, bf16[8,1536]{1,0:T(8,128)(2,1)S(1)}, u32[]{:S(2)}, u32[]{:S(2)}) collective-permute-start(bf16[8,1536]{1,0:T(8,128)(2,1)S(1)} %pad_maximum_fusion.6), channel_id=1, source_target_pairs={{0,2},{1,3},{2,0},{3,1},{4,6},{5,7},{6,4},{7,5},{8,10},{9,11},{10,... | collective-permute-start | bytes 73736 | tf_op jit(solution)/shard_map/ppermute | solution.py:138
  28.3 1.5 %collective-permute-done.10 = bf16[8,1536]{1,0:T(8,128)(2,1)S(1)} collective-permute-done((bf16[8,1536]{1,0:T(8,128)(2,1)S(1)}, bf16[8,1536]{1,0:T(8,128)(2,1)S(1)}, u32[]{:S(2)}, u32[]{:S(2)}) %collective-permute-start.10) | collective-permute-done | bytes 24608 | tf_op jit(solution)/shard_map/ppermute | solution.py:138
  29.8 1.0 collective-permute-start.13
  30.7 0.4 collective-permute-start.12
  31.1 0.3 collective-permute-start.11
  31.4 1.2 %collective-permute-done.13 = bf16[2,8,1152]{2,1,0:T(8,128)(2,1)S(1)} collective-permute-done((bf16[2,8,1152]{2,1,0:T(8,128)(2,1)S(1)}, bf16[2,8,1152]{2,1,0:T(8,128)(2,1)S(1)}, u32[]{:S(2)}, u32[]{:S(2)}) %collective-permute-start.13) | collective-permute-done | bytes 36896 | tf_op jit(solution)/shard_map/ppermute | solution.py:142
  32.7 2.4 %collective-permute-done.12 = bf16[2,8,1152]{2,1,0:T(8,128)(2,1)S(1)} collective-permute-done((bf16[2,8,1152]{2,1,0:T(8,128)(2,1)S(1)}, bf16[2,8,1152]{2,1,0:T(8,128)(2,1)S(1)}, u32[]{:S(2)}, u32[]{:S(2)}) %collective-permute-start.12) | collective-permute-done | bytes 36896 | tf_op jit(solution)/shard_map/ppermute | solution.py:142
  35.1 0.4 collective-permute-done.11
  35.4 8.2 %all-to-all-start = ((bf16[16,128,1024]{2,1,0:T(8,128)(2,1)}), bf16[16,128,1024]{2,1,0:T(8,128)(2,1)}, u32[]{:S(2)}, u32[]{:S(2)}) async-start(bf16[16,128,1024]{2,1,0:T(8,128)(2,1)} %bitcast.91), calls=%async_computation | async-start | bytes 8388608 | tf_op jit(solution)/shard_map/all_to_all | solution.py:200
  43.7 3.0 %collective-permute-start.14 = (bf16[4,2,8,1024]{3,2,1,0:T(8,128)(2,1)S(1)}, bf16[4,2,8,1024]{3,2,1,0:T(8,128)(2,1)S(1)}, u32[]{:S(2)}, u32[]{:S(2)}) collective-permute-start(bf16[4,2,8,1024]{3,2,1,0:T(8,128)(2,1)S(1)} %get-tuple-element.26), channel_id=1, source_target_pairs={{0,66},{1,67},{2,64},{3,65},{4,70},{5,71},{6,68},{7,69},{8,74},{9,... | collective-permute-start | bytes 393224 | tf_op jit(solution)/shard_map/ppermute | solution.py:154
  46.8 3.7 %collective-permute-done.14 = bf16[4,2,8,1024]{3,2,1,0:T(8,128)(2,1)S(1)} collective-permute-done((bf16[4,2,8,1024]{3,2,1,0:T(8,128)(2,1)S(1)}, bf16[4,2,8,1024]{3,2,1,0:T(8,128)(2,1)S(1)}, u32[]{:S(2)}, u32[]{:S(2)}) %collective-permute-start.14) | collective-permute-done | bytes 131104 | tf_op jit(solution)/shard_map/ppermute | solution.py:154
  50.5 1.7 %collective-permute-start.17 = (bf16[2,4,2,8,1024]{4,3,2,1,0:T(8,128)(2,1)S(1)}, bf16[2,4,2,8,1024]{4,3,2,1,0:T(8,128)(2,1)S(1)}, u32[]{:S(2)}, u32[]{:S(2)}) collective-permute-start(bf16[2,4,2,8,1024]{4,3,2,1,0:T(8,128)(2,1)S(1)} %pad_maximum_fusion.refs_0_), channel_id=1, source_target_pairs={{0,48},{16,0},{32,16},{48,32},{64,112},{80,64},{96,80},{112,96},{1... | collective-permute-start | bytes 786440 | tf_op jit(solution)/shard_map/ppermute | solution.py:158
  52.2 0.9 collective-permute-start.16
  53.1 0.0 collective-permute-start.15
  53.1 1.4 %collective-permute-start.18 = (bf16[2,4,2,8,1024]{4,3,2,1,0:T(8,128)(2,1)S(1)}, bf16[2,4,2,8,1024]{4,3,2,1,0:T(8,128)(2,1)S(1)}, u32[]{:S(2)}, u32[]{:S(2)}) collective-permute-start(bf16[2,4,2,8,1024]{4,3,2,1,0:T(8,128)(2,1)S(1)} %pad_maximum_fusion.refs_0_), channel_id=1, source_target_pairs={{0,1},{1,0},{2,3},{3,2},{4,5},{5,4},{6,7},{7,6},{8,9},{9,8},{10,11... | collective-permute-start | bytes 786440 | tf_op jit(solution)/shard_map/ppermute | solution.py:134
  54.5 3.2 %collective-permute-done.17.refs_3_ = bf16[2,4,2,8,1024]{4,3,2,1,0:T(8,128)(2,1)S(1)} collective-permute-done((bf16[2,4,2,8,1024]{4,3,2,1,0:T(8,128)(2,1)S(1)}, bf16[2,4,2,8,1024]{4,3,2,1,0:T(8,128)(2,1)S(1)}, u32[]{:S(2)}, u32[]{:S(2)}) %collective-permute-start.17) | collective-permute-done | bytes 262176 | tf_op jit(solution)/shard_map/ppermute | solution.py:158
  57.7 6.6 %collective-permute-start.21 = (bf16[2,4,2,8,1024]{4,3,2,1,0:T(8,128)(2,1)S(1)}, bf16[2,4,2,8,1024]{4,3,2,1,0:T(8,128)(2,1)S(1)}, u32[]{:S(2)}, u32[]{:S(2)}) collective-permute-start(bf16[2,4,2,8,1024]{4,3,2,1,0:T(8,128)(2,1)S(1)} %collective-permute-done.17.refs_3_), channel_id=1, source_target_pairs={{0,1},{1,0},{2,3},{3,2},{4,5},{5,4},{6,7},{7,6},{8,9},{9,8},{10,11... | collective-permute-start | bytes 786440 | tf_op jit(solution)/shard_map/ppermute | solution.py:134
  64.4 0.1 collective-permute-start.20
  64.5 3.2 %collective-permute-done.15.refs_1_ = bf16[2,4,2,8,1024]{4,3,2,1,0:T(8,128)(2,1)S(1)} collective-permute-done((bf16[2,4,2,8,1024]{4,3,2,1,0:T(8,128)(2,1)S(1)}, bf16[2,4,2,8,1024]{4,3,2,1,0:T(8,128)(2,1)S(1)}, u32[]{:S(2)}, u32[]{:S(2)}) %collective-permute-start.15) | collective-permute-done | bytes 262176 | tf_op jit(solution)/shard_map/ppermute | solution.py:158
  67.7 0.4 collective-permute-start.19
  68.0 0.6 bitcast_convert_fusion.bt_ref
  68.7 0.0 collective-permute-done.18.refs_4_
  68.7 0.0 collective-permute-done.20.refs_6_
  68.7 0.5 collective-permute-done.19.refs_5_
  69.2 24.2 %all-to-all-done.refs_8_ = bf16[16,128,1024]{2,1,0:T(8,128)(2,1)} async-done(((bf16[16,128,1024]{2,1,0:T(8,128)(2,1)}), bf16[16,128,1024]{2,1,0:T(8,128)(2,1)}, u32[]{:S(2)}, u32[]{:S(2)}) %all-to-all-start) | async-done | bytes 4194336 | tf_op jit(solution)/shard_map/all_to_all | solution.py:200
  93.5 7.9 %shard_map.144 = bf16[8,128,2048]{2,1,0:T(8,128)(2,1)} custom-call(f32[64,128]{1,0:T(8,128)} %bitcast_convert_fusion.bt_ref, bf16[2,4,2,8,1024]{4,3,2,1,0:T(8,128)(2,1)} %copy-done, bf16[2,4,2,8,1024]{4,3,2,1,0:T(8,128)(2,1)} %copy-done.3, bf16[2,4,2,8,1024]{4,3,2,1,0:T(8,128)(2,1)} %copy-done.2, bf16[2,4,2,8,1024]{4,3,2,1,0:T(8,128)(2,1)} %copy-done.1, ...), custom_call_target="tpu_custom_call" | custom-call | flops 268435456 | bytes 10485760 | tf_op jit(solution)/shard_map/pallas_call | solution.py:109
  (59 shorter events, 0.4 us)
Async XLA Ops:
  0.6 21.1 %copy-start.11 = (f32[4,2048]{1,0:T(4,128)S(1)}, f32[4,2048]{1,0:T(4,128)}, u32[]{:S(2)}) copy-start(f32[4,2048]{1,0:T(4,128)} %param.15) | copy-start | bytes 98308
  0.6 21.1 %copy-start.10 = (f32[4,2048]{1,0:T(4,128)S(1)}, f32[4,2048]{1,0:T(4,128)}, u32[]{:S(2)}) copy-start(f32[4,2048]{1,0:T(4,128)} %param.14) | copy-start | bytes 98308
  0.7 21.1 %copy-start.9 = (f32[4,2048]{1,0:T(4,128)S(1)}, f32[4,2048]{1,0:T(4,128)}, u32[]{:S(2)}) copy-start(f32[4,2048]{1,0:T(4,128)} %param.13) | copy-start | bytes 98308
  0.7 25.5 %copy-start.14 = (f32[8,1024]{1,0:T(8,128)S(1)}, f32[8,1024]{1,0:T(8,128)}, u32[]{:S(2)}) copy-start(f32[8,1024]{1,0:T(8,128)} %param.12) | copy-start | bytes 98308
  0.7 25.4 %copy-start.13 = (f32[8,1024]{1,0:T(8,128)S(1)}, f32[8,1024]{1,0:T(8,128)}, u32[]{:S(2)}) copy-start(f32[8,1024]{1,0:T(8,128)} %param.11) | copy-start | bytes 98308
  0.7 25.4 %copy-start.12 = (f32[8,1024]{1,0:T(8,128)S(1)}, f32[8,1024]{1,0:T(8,128)}, u32[]{:S(2)}) copy-start(f32[8,1024]{1,0:T(8,128)} %param.10) | copy-start | bytes 98308
  2.0 7.7 %collective-permute-start = (f32[4,2,4,2048]{3,2,1,0:T(4,128)S(1)}, f32[4,2,4,2048]{3,2,1,0:T(4,128)S(1)}, u32[]{:S(2)}, u32[]{:S(2)}) collective-permute-start(f32[4,2,4,2048]{3,2,1,0:T(4,128)S(1)} %dynamic-slice_bitcast_fusion), channel_id=1, source_target_pairs={{0,1},{1,0},{2,3},{3,2},{4,5},{5,4},{6,7},{7,6},{8,9},{9,8},{10,11... | collective-permute-start | bytes 786440 | tf_op jit(solution)/shard_map/ppermute | solution.py:134
  4.4 6.6 %collective-permute-start.7 = (f32[2,8,1024]{2,1,0:T(8,128)S(1)}, f32[2,8,1024]{2,1,0:T(8,128)S(1)}, u32[]{:S(2)}, u32[]{:S(2)}) collective-permute-start(f32[2,8,1024]{2,1,0:T(8,128)S(1)} %get-tuple-element.22), channel_id=1, source_target_pairs={{0,32},{16,48},{32,0},{48,16},{64,96},{80,112},{96,64},{112,80},{1... | collective-permute-start | bytes 196616 | tf_op jit(solution)/shard_map/ppermute | solution.py:158
  8.2 4.3 %collective-permute-start.8 = (f32[2,8,1024]{2,1,0:T(8,128)S(1)}, f32[2,8,1024]{2,1,0:T(8,128)S(1)}, u32[]{:S(2)}, u32[]{:S(2)}) collective-permute-start(f32[2,8,1024]{2,1,0:T(8,128)S(1)} %get-tuple-element.23), channel_id=1, source_target_pairs={{0,48},{16,0},{32,16},{48,32},{64,112},{80,64},{96,80},{112,96},{1... | collective-permute-start | bytes 196616 | tf_op jit(solution)/shard_map/ppermute | solution.py:158
  8.6 4.3 %collective-permute-start.6 = (f32[2,8,1024]{2,1,0:T(8,128)S(1)}, f32[2,8,1024]{2,1,0:T(8,128)S(1)}, u32[]{:S(2)}, u32[]{:S(2)}) collective-permute-start(f32[2,8,1024]{2,1,0:T(8,128)S(1)} %get-tuple-element.24), channel_id=1, source_target_pairs={{0,16},{16,32},{32,48},{48,0},{64,80},{80,96},{96,112},{112,64},{1... | collective-permute-start | bytes 196616 | tf_op jit(solution)/shard_map/ppermute | solution.py:158
  9.7 4.2 %collective-permute-start.1 = (f32[4,4,2048]{2,1,0:T(4,128)S(1)}, f32[4,4,2048]{2,1,0:T(4,128)S(1)}, u32[]{:S(2)}, u32[]{:S(2)}) collective-permute-start(f32[4,4,2048]{2,1,0:T(4,128)S(1)} %dynamic-slice_bitcast_fusion.1), channel_id=1, source_target_pairs={{0,2},{1,3},{2,0},{3,1},{4,6},{5,7},{6,4},{7,5},{8,10},{9,11},{10,... | collective-permute-start | bytes 393224 | tf_op jit(solution)/shard_map/ppermute | solution.py:138
  14.0 7.2 %collective-permute-start.3 = (f32[4,2048]{1,0:T(4,128)S(1)}, f32[4,2048]{1,0:T(4,128)S(1)}, u32[]{:S(2)}, u32[]{:S(2)}) collective-permute-start(f32[4,2048]{1,0:T(4,128)S(1)} %get-tuple-element.27), channel_id=1, source_target_pairs={{0,8},{1,9},{2,10},{3,11},{4,12},{5,13},{6,14},{7,15},{8,0},{9,1},... | collective-permute-start | bytes 98312 | tf_op jit(solution)/shard_map/ppermute | solution.py:142
  17.0 4.2 %collective-permute-start.4 = (f32[4,2048]{1,0:T(4,128)S(1)}, f32[4,2048]{1,0:T(4,128)S(1)}, u32[]{:S(2)}, u32[]{:S(2)}) collective-permute-start(f32[4,2048]{1,0:T(4,128)S(1)} %get-tuple-element.28), channel_id=1, source_target_pairs={{0,12},{1,13},{2,14},{3,15},{4,0},{5,1},{6,2},{7,3},{8,4},{9,5},{1... | collective-permute-start | bytes 98312 | tf_op jit(solution)/shard_map/ppermute | solution.py:142
  17.8 4.0 %collective-permute-start.2 = (f32[4,2048]{1,0:T(4,128)S(1)}, f32[4,2048]{1,0:T(4,128)S(1)}, u32[]{:S(2)}, u32[]{:S(2)}) collective-permute-start(f32[4,2048]{1,0:T(4,128)S(1)} %get-tuple-element.29), channel_id=1, source_target_pairs={{0,4},{1,5},{2,6},{3,7},{4,8},{5,9},{6,10},{7,11},{8,12},{9,13},{1... | collective-permute-start | bytes 98312 | tf_op jit(solution)/shard_map/ppermute | solution.py:142
  18.5 7.7 %collective-permute-start.9 = (f32[8,1024]{1,0:T(8,128)S(1)}, f32[8,1024]{1,0:T(8,128)S(1)}, u32[]{:S(2)}, u32[]{:S(2)}) collective-permute-start(f32[8,1024]{1,0:T(8,128)S(1)} %dynamic-slice_bitcast_fusion.5), channel_id=1, source_target_pairs={{0,64},{16,80},{32,96},{48,112},{64,0},{80,16},{96,32},{112,48},{1... | collective-permute-start | bytes 98312 | tf_op jit(solution)/shard_map/ppermute | solution.py:150
  22.4 13.0 %copy-start.8 = (f32[4,2048]{1,0:T(4,128)}, f32[4,2048]{1,0:T(4,128)S(1)}, u32[]{:S(2)}) copy-start(f32[4,2048]{1,0:T(4,128)S(1)} %get-tuple-element.19) | copy-start | bytes 98308
  22.5 4.4 %collective-permute-start.5 = (bf16[4,2,4,128]{3,2,1,0:T(4,128)(2,1)S(1)}, bf16[4,2,4,128]{3,2,1,0:T(4,128)(2,1)S(1)}, u32[]{:S(2)}, u32[]{:S(2)}) collective-permute-start(bf16[4,2,4,128]{3,2,1,0:T(4,128)(2,1)S(1)} %bitcast.98), channel_id=1, source_target_pairs={{0,1},{1,0},{2,3},{3,2},{4,5},{5,4},{6,7},{7,6},{8,9},{9,8},{10,11... | collective-permute-start | bytes 24584 | tf_op jit(solution)/shard_map/ppermute | solution.py:134
  27.0 2.8 %collective-permute-start.10 = (bf16[8,1536]{1,0:T(8,128)(2,1)S(1)}, bf16[8,1536]{1,0:T(8,128)(2,1)S(1)}, u32[]{:S(2)}, u32[]{:S(2)}) collective-permute-start(bf16[8,1536]{1,0:T(8,128)(2,1)S(1)} %pad_maximum_fusion.6), channel_id=1, source_target_pairs={{0,2},{1,3},{2,0},{3,1},{4,6},{5,7},{6,4},{7,5},{8,10},{9,11},{10,... | collective-permute-start | bytes 73736 | tf_op jit(solution)/shard_map/ppermute | solution.py:138
  29.8 2.9 %collective-permute-start.13 = (bf16[2,8,1152]{2,1,0:T(8,128)(2,1)S(1)}, bf16[2,8,1152]{2,1,0:T(8,128)(2,1)S(1)}, u32[]{:S(2)}, u32[]{:S(2)}) collective-permute-start(bf16[2,8,1152]{2,1,0:T(8,128)(2,1)S(1)} %get-tuple-element.30), channel_id=1, source_target_pairs={{0,12},{1,13},{2,14},{3,15},{4,0},{5,1},{6,2},{7,3},{8,4},{9,5},{1... | collective-permute-start | bytes 110600 | tf_op jit(solution)/shard_map/ppermute | solution.py:142
  30.7 4.3 %collective-permute-start.12 = (bf16[2,8,1152]{2,1,0:T(8,128)(2,1)S(1)}, bf16[2,8,1152]{2,1,0:T(8,128)(2,1)S(1)}, u32[]{:S(2)}, u32[]{:S(2)}) collective-permute-start(bf16[2,8,1152]{2,1,0:T(8,128)(2,1)S(1)} %get-tuple-element.31), channel_id=1, source_target_pairs={{0,8},{1,9},{2,10},{3,11},{4,12},{5,13},{6,14},{7,15},{8,0},{9,1},... | collective-permute-start | bytes 110600 | tf_op jit(solution)/shard_map/ppermute | solution.py:142
  31.1 4.3 %collective-permute-start.11 = (bf16[2,8,1152]{2,1,0:T(8,128)(2,1)S(1)}, bf16[2,8,1152]{2,1,0:T(8,128)(2,1)S(1)}, u32[]{:S(2)}, u32[]{:S(2)}) collective-permute-start(bf16[2,8,1152]{2,1,0:T(8,128)(2,1)S(1)} %get-tuple-element.32), channel_id=1, source_target_pairs={{0,4},{1,5},{2,6},{3,7},{4,8},{5,9},{6,10},{7,11},{8,12},{9,13},{1... | collective-permute-start | bytes 110600 | tf_op jit(solution)/shard_map/ppermute | solution.py:142
  35.4 58.0 %all-to-all-start = ((bf16[16,128,1024]{2,1,0:T(8,128)(2,1)}), bf16[16,128,1024]{2,1,0:T(8,128)(2,1)}, u32[]{:S(2)}, u32[]{:S(2)}) async-start(bf16[16,128,1024]{2,1,0:T(8,128)(2,1)} %bitcast.91), calls=%async_computation | async-start | bytes 8388608 | tf_op jit(solution)/shard_map/all_to_all | solution.py:200
  43.7 6.7 %collective-permute-start.14 = (bf16[4,2,8,1024]{3,2,1,0:T(8,128)(2,1)S(1)}, bf16[4,2,8,1024]{3,2,1,0:T(8,128)(2,1)S(1)}, u32[]{:S(2)}, u32[]{:S(2)}) collective-permute-start(bf16[4,2,8,1024]{3,2,1,0:T(8,128)(2,1)S(1)} %get-tuple-element.26), channel_id=1, source_target_pairs={{0,66},{1,67},{2,64},{3,65},{4,70},{5,71},{6,68},{7,69},{8,74},{9,... | collective-permute-start | bytes 393224 | tf_op jit(solution)/shard_map/ppermute | solution.py:154
  50.5 43.0 %copy-start = (bf16[2,4,2,8,1024]{4,3,2,1,0:T(8,128)(2,1)}, bf16[2,4,2,8,1024]{4,3,2,1,0:T(8,128)(2,1)S(1)}, u32[]{:S(2)}) copy-start(bf16[2,4,2,8,1024]{4,3,2,1,0:T(8,128)(2,1)S(1)} %pad_maximum_fusion.refs_0_) | copy-start | bytes 786436
  50.5 7.2 %collective-permute-start.17 = (bf16[2,4,2,8,1024]{4,3,2,1,0:T(8,128)(2,1)S(1)}, bf16[2,4,2,8,1024]{4,3,2,1,0:T(8,128)(2,1)S(1)}, u32[]{:S(2)}, u32[]{:S(2)}) collective-permute-start(bf16[2,4,2,8,1024]{4,3,2,1,0:T(8,128)(2,1)S(1)} %pad_maximum_fusion.refs_0_), channel_id=1, source_target_pairs={{0,48},{16,0},{32,16},{48,32},{64,112},{80,64},{96,80},{112,96},{1... | collective-permute-start | bytes 786440 | tf_op jit(solution)/shard_map/ppermute | solution.py:158
  52.2 12.2 %collective-permute-start.16 = (bf16[2,4,2,8,1024]{4,3,2,1,0:T(8,128)(2,1)S(1)}, bf16[2,4,2,8,1024]{4,3,2,1,0:T(8,128)(2,1)S(1)}, u32[]{:S(2)}, u32[]{:S(2)}) collective-permute-start(bf16[2,4,2,8,1024]{4,3,2,1,0:T(8,128)(2,1)S(1)} %pad_maximum_fusion.refs_0_), channel_id=1, source_target_pairs={{0,32},{16,48},{32,0},{48,16},{64,96},{80,112},{96,64},{112,80},{1... | collective-permute-start | bytes 786440 | tf_op jit(solution)/shard_map/ppermute | solution.py:158
  53.1 14.6 %collective-permute-start.15 = (bf16[2,4,2,8,1024]{4,3,2,1,0:T(8,128)(2,1)S(1)}, bf16[2,4,2,8,1024]{4,3,2,1,0:T(8,128)(2,1)S(1)}, u32[]{:S(2)}, u32[]{:S(2)}) collective-permute-start(bf16[2,4,2,8,1024]{4,3,2,1,0:T(8,128)(2,1)S(1)} %pad_maximum_fusion.refs_0_), channel_id=1, source_target_pairs={{0,16},{16,32},{32,48},{48,0},{64,80},{80,96},{96,112},{112,64},{1... | collective-permute-start | bytes 786440 | tf_op jit(solution)/shard_map/ppermute | solution.py:158
  53.1 15.6 %collective-permute-start.18 = (bf16[2,4,2,8,1024]{4,3,2,1,0:T(8,128)(2,1)S(1)}, bf16[2,4,2,8,1024]{4,3,2,1,0:T(8,128)(2,1)S(1)}, u32[]{:S(2)}, u32[]{:S(2)}) collective-permute-start(bf16[2,4,2,8,1024]{4,3,2,1,0:T(8,128)(2,1)S(1)} %pad_maximum_fusion.refs_0_), channel_id=1, source_target_pairs={{0,1},{1,0},{2,3},{3,2},{4,5},{5,4},{6,7},{7,6},{8,9},{9,8},{10,11... | collective-permute-start | bytes 786440 | tf_op jit(solution)/shard_map/ppermute | solution.py:134
  57.7 35.7 %copy-start.1 = (bf16[2,4,2,8,1024]{4,3,2,1,0:T(8,128)(2,1)}, bf16[2,4,2,8,1024]{4,3,2,1,0:T(8,128)(2,1)S(1)}, u32[]{:S(2)}) copy-start(bf16[2,4,2,8,1024]{4,3,2,1,0:T(8,128)(2,1)S(1)} %collective-permute-done.17.refs_3_) | copy-start | bytes 786436
  57.7 10.9 %collective-permute-start.21 = (bf16[2,4,2,8,1024]{4,3,2,1,0:T(8,128)(2,1)S(1)}, bf16[2,4,2,8,1024]{4,3,2,1,0:T(8,128)(2,1)S(1)}, u32[]{:S(2)}, u32[]{:S(2)}) collective-permute-start(bf16[2,4,2,8,1024]{4,3,2,1,0:T(8,128)(2,1)S(1)} %collective-permute-done.17.refs_3_), channel_id=1, source_target_pairs={{0,1},{1,0},{2,3},{3,2},{4,5},{5,4},{6,7},{7,6},{8,9},{9,8},{10,11... | collective-permute-start | bytes 786440 | tf_op jit(solution)/shard_map/ppermute | solution.py:134
  64.4 29.1 %copy-start.2 = (bf16[2,4,2,8,1024]{4,3,2,1,0:T(8,128)(2,1)}, bf16[2,4,2,8,1024]{4,3,2,1,0:T(8,128)(2,1)S(1)}, u32[]{:S(2)}) copy-start(bf16[2,4,2,8,1024]{4,3,2,1,0:T(8,128)(2,1)S(1)} %collective-permute-done.16.refs_2_) | copy-start | bytes 786436
  64.4 4.3 %collective-permute-start.20 = (bf16[2,4,2,8,1024]{4,3,2,1,0:T(8,128)(2,1)S(1)}, bf16[2,4,2,8,1024]{4,3,2,1,0:T(8,128)(2,1)S(1)}, u32[]{:S(2)}, u32[]{:S(2)}) collective-permute-start(bf16[2,4,2,8,1024]{4,3,2,1,0:T(8,128)(2,1)S(1)} %collective-permute-done.16.refs_2_), channel_id=1, source_target_pairs={{0,1},{1,0},{2,3},{3,2},{4,5},{5,4},{6,7},{7,6},{8,9},{9,8},{10,11... | collective-permute-start | bytes 786440 | tf_op jit(solution)/shard_map/ppermute | solution.py:134
  67.7 25.8 %copy-start.3 = (bf16[2,4,2,8,1024]{4,3,2,1,0:T(8,128)(2,1)}, bf16[2,4,2,8,1024]{4,3,2,1,0:T(8,128)(2,1)S(1)}, u32[]{:S(2)}) copy-start(bf16[2,4,2,8,1024]{4,3,2,1,0:T(8,128)(2,1)S(1)} %collective-permute-done.15.refs_1_) | copy-start | bytes 786436
  67.7 1.6 %collective-permute-start.19 = (bf16[2,4,2,8,1024]{4,3,2,1,0:T(8,128)(2,1)S(1)}, bf16[2,4,2,8,1024]{4,3,2,1,0:T(8,128)(2,1)S(1)}, u32[]{:S(2)}, u32[]{:S(2)}) collective-permute-start(bf16[2,4,2,8,1024]{4,3,2,1,0:T(8,128)(2,1)S(1)} %collective-permute-done.15.refs_1_), channel_id=1, source_target_pairs={{0,1},{1,0},{2,3},{3,2},{4,5},{5,4},{6,7},{7,6},{8,9},{9,8},{10,11... | collective-permute-start | bytes 786440 | tf_op jit(solution)/shard_map/ppermute | solution.py:134
  68.7 24.8 %copy-start.4 = (bf16[2,4,2,8,1024]{4,3,2,1,0:T(8,128)(2,1)}, bf16[2,4,2,8,1024]{4,3,2,1,0:T(8,128)(2,1)S(1)}, u32[]{:S(2)}) copy-start(bf16[2,4,2,8,1024]{4,3,2,1,0:T(8,128)(2,1)S(1)} %collective-permute-done.18.refs_4_) | copy-start | bytes 786436
  68.7 24.8 %copy-start.5 = (bf16[2,4,2,8,1024]{4,3,2,1,0:T(8,128)(2,1)}, bf16[2,4,2,8,1024]{4,3,2,1,0:T(8,128)(2,1)S(1)}, u32[]{:S(2)}) copy-start(bf16[2,4,2,8,1024]{4,3,2,1,0:T(8,128)(2,1)S(1)} %collective-permute-done.21.refs_7_) | copy-start | bytes 786436
  68.7 24.8 %copy-start.6 = (bf16[2,4,2,8,1024]{4,3,2,1,0:T(8,128)(2,1)}, bf16[2,4,2,8,1024]{4,3,2,1,0:T(8,128)(2,1)S(1)}, u32[]{:S(2)}) copy-start(bf16[2,4,2,8,1024]{4,3,2,1,0:T(8,128)(2,1)S(1)} %collective-permute-done.20.refs_6_) | copy-start | bytes 786436
  69.2 24.3 %copy-start.7 = (bf16[2,4,2,8,1024]{4,3,2,1,0:T(8,128)(2,1)}, bf16[2,4,2,8,1024]{4,3,2,1,0:T(8,128)(2,1)S(1)}, u32[]{:S(2)}) copy-start(bf16[2,4,2,8,1024]{4,3,2,1,0:T(8,128)(2,1)S(1)} %collective-permute-done.19.refs_5_) | copy-start | bytes 786436

commit v3 on v2

--- a/solution.py
+++ b/solution.py
@@ -81,26 +81,29 @@
         (((0,), (1,)), ((), ())),
         preferred_element_type=jnp.float32,
     ).astype(jnp.bfloat16)
-    for s in range(16):
-        k_core, k_y, k_x = s // 8, (s // 2) % 4, s % 2
-        if s % 8 == 0:
-            for copy in a_copies[4 * k_core : 4 * k_core + 4]:
-                copy.wait()
-        a_block = jnp.concatenate(
-            [
-                a_buf[4 * k_core + k_z, k_x_hi, k_y, k_x ^ k_x_hi]
-                for k_z in range(4)
-                for k_x_hi in range(2)
-            ],
-            axis=0,
-        )
-        increment = lax.dot_general(
-            left, a_block, (((1,), (0,)), ((), ())), preferred_element_type=jnp.float32
-        )
-        in_copies[s].wait()
-        merged = in_buf[s].astype(jnp.float32) + adapter_factor() * increment
-        out_buf[s] = merged.astype(jnp.bfloat16)
-        out_copies[s].start()
+    for copy in a_copies:
+        copy.wait()
+    for first in range(0, 16, 4):
+        group = range(first, first + 4)
+        for s in group:
+            in_copies[s].wait()
+        for s in group:
+            k_core, k_y, k_x = s // 8, (s // 2) % 4, s % 2
+            a_block = jnp.concatenate(
+                [
+                    a_buf[4 * k_core + k_z, k_x_hi, k_y, k_x ^ k_x_hi]
+                    for k_z in range(4)
+                    for k_x_hi in range(2)
+                ],
+                axis=0,
+            )
+            increment = lax.dot_general(
+                left, a_block, (((1,), (0,)), ((), ())), preferred_element_type=jnp.float32
+            )
+            merged = in_buf[s].astype(jnp.float32) + adapter_factor() * increment
+            out_buf[s] = merged.astype(jnp.bfloat16)
+        for s in group:
+            out_copies[s].start()
     for copy in out_copies:
         copy.wait()
 
@@ -119,7 +122,7 @@
             pltpu.SemaphoreType.DMA((16,)),
             pltpu.SemaphoreType.DMA((16,)),
         ],
-        compiler_params=pltpu.CompilerParams(vmem_limit_bytes=56 << 20),
+        compiler_params=pltpu.CompilerParams(vmem_limit_bytes=32 << 20),
         cost_estimate=pl.CostEstimate(
             flops=2 * 128 * 64 * 16384, bytes_accessed=10 << 20, transcendentals=0
         ),
@@ -144,6 +147,18 @@
 
 def over_x_y(array, k_x, k_y):
     return lax.ppermute(array, "col", [(i, ((i + 4 * k_y) % 16) ^ (2 * k_x)) for i in range(16)])
+
+
+def over_col(array, mask):
+    return lax.ppermute(array, "col", [(i, i ^ mask) for i in range(16)])
+
+
+def over_row(array, mask):
+    return lax.ppermute(array, "row", [(i, i ^ mask) for i in range(8)])
+
+
+def two_of(array, first, second, axis):
+    return jnp.stack([pick(array, first, axis), pick(array, second, axis)], axis=axis)
 
 
 def over_x_hi(array):

time: 102 us -> 98 us (0.961)
  Pallas kernels: 7.91 us -> 4.28 us
    pallas_call x1, Pallas kernels: 7.91 us -> 4.28 us  [merge(): pl.pallas_call(merge_kernel, in_specs=[pl.BlockSpec(memory_space=pltpu.VM...]
  transfers between devices with their start and end apart: 23 -> 23, of which waited for: 14 -> 14; matrix products, arithmetic and copies ran while one was open for 4% -> 3% of each run, Pallas kernels for 0% -> 0%
where the time goes in v3:
time: 98 us; the launch traced here: 97.7 us
  starting transfers between devices  44 us (45%)
  waiting for transfers between devices  43.8 us (45%)
  Pallas kernels  4.28 us (4%)
  other arithmetic  2.43 us (2%)
  local copies, waits for them, and re-layouts  2.31 us (2%)
    all_to_all x1, waiting for transfers between devices, per_device(): arrived = lax.all_to_all(weight, 'col', 0, 0, tiled=True)  24.2 us
    ppermute x6, starting transfers between devices, over_core(): return lax.ppermute(array, 'col', [(i, i ^ 1) for i in range(16)])  13.5 us
    ppermute x6, waiting for transfers between devices, over_z(): lax.ppermute(array, 'row', [(i, i // 4 * 4 + (i + k) % 4) for i in range(...  8.42 us
    all_to_all x1, starting transfers between devices, per_device(): arrived = lax.all_to_all(weight, 'col', 0, 0, tiled=True)  8.21 us
    ppermute x6, starting transfers between devices, over_z(): lax.ppermute(array, 'row', [(i, i // 4 * 4 + (i + k) % 4) for i in range(...  7.84 us
    ppermute x6, starting transfers between devices, over_y(): lax.ppermute(array, 'col', [(i, (i + 4 * k) % 16) for i in range(16)])  6.09 us
    ppermute x6, waiting for transfers between devices, over_y(): lax.ppermute(array, 'col', [(i, (i + 4 * k) % 16) for i in range(16)])  4.57 us
    pallas_call x1, Pallas kernels, merge(): pl.pallas_call(merge_kernel, in_specs=[pl.BlockSpec(memory_space=pltpu.VM...  4.28 us
  transfers between devices with their start and end apart: 23, of which 14 were waited for; matrix products, arithmetic and copies ran while one was open for 3% of the time, Pallas kernels for 0%

profile of v3, /device:TPU:1, one launch (start us, length us, event | category | flops | bytes accessed | tf_op | source)
XLA Modules:
  0.0 97.7 jit_solution(8990085564417869431)
XLA Ops:
  0.7 1.2 %reshape.35 = f32[4,2,2,4,2048]{4,3,2,1,0:T(4,128)S(1)} reshape(f32[1,64,2048]{2,1,0:T(8,128)} %param.17) | data formatting | bytes 1048576 | tf_op jit(solution)/shard_map/reshape | solution.py:194
  2.0 1.5 %collective-permute-start = (f32[4,2,4,2048]{3,2,1,0:T(4,128)S(1)}, f32[4,2,4,2048]{3,2,1,0:T(4,128)S(1)}, u32[]{:S(2)}, u32[]{:S(2)}) collective-permute-start(f32[4,2,4,2048]{3,2,1,0:T(4,128)S(1)} %dynamic-slice_bitcast_fusion), channel_id=1, source_target_pairs={{0,1},{1,0},{2,3},{3,2},{4,5},{5,4},{6,7},{7,6},{8,9},{9,8},{10,11... | collective-permute-start | bytes 786440 | tf_op jit(solution)/shard_map/ppermute | solution.py:137
  3.5 0.9 dynamic-slice_bitcast_fusion.3
  4.4 3.8 %collective-permute-start.7 = (f32[2,8,1024]{2,1,0:T(8,128)S(1)}, f32[2,8,1024]{2,1,0:T(8,128)S(1)}, u32[]{:S(2)}, u32[]{:S(2)}) collective-permute-start(f32[2,8,1024]{2,1,0:T(8,128)S(1)} %get-tuple-element.22), channel_id=1, source_target_pairs={{0,32},{16,48},{32,0},{48,16},{64,96},{80,112},{96,64},{112,80},{1... | collective-permute-start | bytes 196616 | tf_op jit(solution)/shard_map/ppermute | solution.py:173
  8.2 0.4 collective-permute-start.8
  8.6 1.0 %collective-permute-start.6 = (f32[2,8,1024]{2,1,0:T(8,128)S(1)}, f32[2,8,1024]{2,1,0:T(8,128)S(1)}, u32[]{:S(2)}, u32[]{:S(2)}) collective-permute-start(f32[2,8,1024]{2,1,0:T(8,128)S(1)} %get-tuple-element.24), channel_id=1, source_target_pairs={{0,16},{16,32},{32,48},{48,0},{64,80},{80,96},{96,112},{112,64},{1... | collective-permute-start | bytes 196616 | tf_op jit(solution)/shard_map/ppermute | solution.py:173
  9.6 0.0 collective-permute-done
  9.6 0.1 bitcast_add_fusion
  9.7 1.3 %collective-permute-start.1 = (f32[4,4,2048]{2,1,0:T(4,128)S(1)}, f32[4,4,2048]{2,1,0:T(4,128)S(1)}, u32[]{:S(2)}, u32[]{:S(2)}) collective-permute-start(f32[4,4,2048]{2,1,0:T(4,128)S(1)} %dynamic-slice_bitcast_fusion.1), channel_id=1, source_target_pairs={{0,2},{1,3},{2,0},{3,1},{4,6},{5,7},{6,4},{7,5},{8,10},{9,11},{10,... | collective-permute-start | bytes 393224 | tf_op jit(solution)/shard_map/ppermute | solution.py:141
  11.0 0.0 collective-permute-done.7
  11.0 1.5 %collective-permute-done.8 = f32[2,8,1024]{2,1,0:T(8,128)S(1)} collective-permute-done((f32[2,8,1024]{2,1,0:T(8,128)S(1)}, f32[2,8,1024]{2,1,0:T(8,128)S(1)}, u32[]{:S(2)}, u32[]{:S(2)}) %collective-permute-start.8) | collective-permute-done | bytes 65568 | tf_op jit(solution)/shard_map/ppermute | solution.py:173
  12.5 0.4 collective-permute-done.6
  12.9 0.9 bitcast_add_fusion.2
  13.8 0.1 collective-permute-done.1
  14.0 3.0 %collective-permute-start.3 = (f32[4,2048]{1,0:T(4,128)S(1)}, f32[4,2048]{1,0:T(4,128)S(1)}, u32[]{:S(2)}, u32[]{:S(2)}) collective-permute-start(f32[4,2048]{1,0:T(4,128)S(1)} %get-tuple-element.27), channel_id=1, source_target_pairs={{0,8},{1,9},{2,10},{3,11},{4,12},{5,13},{6,14},{7,15},{8,0},{9,1},... | collective-permute-start | bytes 98312 | tf_op jit(solution)/shard_map/ppermute | solution.py:145
  17.0 0.8 collective-permute-start.4
  17.8 0.7 collective-permute-start.2
  18.5 2.7 %collective-permute-start.9 = (f32[8,1024]{1,0:T(8,128)S(1)}, f32[8,1024]{1,0:T(8,128)S(1)}, u32[]{:S(2)}, u32[]{:S(2)}) collective-permute-start(f32[8,1024]{1,0:T(8,128)S(1)} %dynamic-slice_bitcast_fusion.5), channel_id=1, source_target_pairs={{0,64},{16,80},{32,96},{48,112},{64,0},{80,16},{96,32},{112,48},{1... | collective-permute-start | bytes 98312 | tf_op jit(solution)/shard_map/ppermute | solution.py:165
  21.2 0.0 collective-permute-done.3
  21.2 0.0 collective-permute-done.4
  21.2 0.5 collective-permute-done.2
  21.7 0.7 multiply_subtract_fusion.1
  22.5 3.6 %collective-permute-start.5 = (bf16[4,2,4,128]{3,2,1,0:T(4,128)(2,1)S(1)}, bf16[4,2,4,128]{3,2,1,0:T(4,128)(2,1)S(1)}, u32[]{:S(2)}, u32[]{:S(2)}) collective-permute-start(bf16[4,2,4,128]{3,2,1,0:T(4,128)(2,1)S(1)} %bitcast.98), channel_id=1, source_target_pairs={{0,1},{1,0},{2,3},{3,2},{4,5},{5,4},{6,7},{7,6},{8,9},{9,8},{10,11... | collective-permute-start | bytes 24584 | tf_op jit(solution)/shard_map/ppermute | solution.py:137
  26.1 0.7 fusion.14
  26.8 0.1 collective-permute-done.5
  27.0 1.3 %collective-permute-start.10 = (bf16[8,1536]{1,0:T(8,128)(2,1)S(1)}, bf16[8,1536]{1,0:T(8,128)(2,1)S(1)}, u32[]{:S(2)}, u32[]{:S(2)}) collective-permute-start(bf16[8,1536]{1,0:T(8,128)(2,1)S(1)} %pad_maximum_fusion.6), channel_id=1, source_target_pairs={{0,2},{1,3},{2,0},{3,1},{4,6},{5,7},{6,4},{7,5},{8,10},{9,11},{10,... | collective-permute-start | bytes 73736 | tf_op jit(solution)/shard_map/ppermute | solution.py:141
  28.3 1.5 %collective-permute-done.10 = bf16[8,1536]{1,0:T(8,128)(2,1)S(1)} collective-permute-done((bf16[8,1536]{1,0:T(8,128)(2,1)S(1)}, bf16[8,1536]{1,0:T(8,128)(2,1)S(1)}, u32[]{:S(2)}, u32[]{:S(2)}) %collective-permute-start.10) | collective-permute-done | bytes 24608 | tf_op jit(solution)/shard_map/ppermute | solution.py:141
  29.8 1.0 collective-permute-start.13
  30.7 0.4 collective-permute-start.12
  31.1 0.3 collective-permute-start.11
  31.4 1.2 %collective-permute-done.13 = bf16[2,8,1152]{2,1,0:T(8,128)(2,1)S(1)} collective-permute-done((bf16[2,8,1152]{2,1,0:T(8,128)(2,1)S(1)}, bf16[2,8,1152]{2,1,0:T(8,128)(2,1)S(1)}, u32[]{:S(2)}, u32[]{:S(2)}) %collective-permute-start.13) | collective-permute-done | bytes 36896 | tf_op jit(solution)/shard_map/ppermute | solution.py:145
  32.7 2.4 %collective-permute-done.12 = bf16[2,8,1152]{2,1,0:T(8,128)(2,1)S(1)} collective-permute-done((bf16[2,8,1152]{2,1,0:T(8,128)(2,1)S(1)}, bf16[2,8,1152]{2,1,0:T(8,128)(2,1)S(1)}, u32[]{:S(2)}, u32[]{:S(2)}) %collective-permute-start.12) | collective-permute-done | bytes 36896 | tf_op jit(solution)/shard_map/ppermute | solution.py:145
  35.1 0.4 collective-permute-done.11
  35.4 8.2 %all-to-all-start = ((bf16[16,128,1024]{2,1,0:T(8,128)(2,1)}), bf16[16,128,1024]{2,1,0:T(8,128)(2,1)}, u32[]{:S(2)}, u32[]{:S(2)}) async-start(bf16[16,128,1024]{2,1,0:T(8,128)(2,1)} %bitcast.91), calls=%async_computation | async-start | bytes 8388608 | tf_op jit(solution)/shard_map/all_to_all | solution.py:215
  43.7 3.0 %collective-permute-start.14 = (bf16[4,2,8,1024]{3,2,1,0:T(8,128)(2,1)S(1)}, bf16[4,2,8,1024]{3,2,1,0:T(8,128)(2,1)S(1)}, u32[]{:S(2)}, u32[]{:S(2)}) collective-permute-start(bf16[4,2,8,1024]{3,2,1,0:T(8,128)(2,1)S(1)} %get-tuple-element.26), channel_id=1, source_target_pairs={{0,66},{1,67},{2,64},{3,65},{4,70},{5,71},{6,68},{7,69},{8,74},{9,... | collective-permute-start | bytes 393224 | tf_op jit(solution)/shard_map/ppermute | solution.py:169
  46.8 3.7 %collective-permute-done.14 = bf16[4,2,8,1024]{3,2,1,0:T(8,128)(2,1)S(1)} collective-permute-done((bf16[4,2,8,1024]{3,2,1,0:T(8,128)(2,1)S(1)}, bf16[4,2,8,1024]{3,2,1,0:T(8,128)(2,1)S(1)}, u32[]{:S(2)}, u32[]{:S(2)}) %collective-permute-start.14) | collective-permute-done | bytes 131104 | tf_op jit(solution)/shard_map/ppermute | solution.py:169
  50.5 1.7 %collective-permute-start.17 = (bf16[2,4,2,8,1024]{4,3,2,1,0:T(8,128)(2,1)S(1)}, bf16[2,4,2,8,1024]{4,3,2,1,0:T(8,128)(2,1)S(1)}, u32[]{:S(2)}, u32[]{:S(2)}) collective-permute-start(bf16[2,4,2,8,1024]{4,3,2,1,0:T(8,128)(2,1)S(1)} %pad_maximum_fusion.refs_0_), channel_id=1, source_target_pairs={{0,48},{16,0},{32,16},{48,32},{64,112},{80,64},{96,80},{112,96},{1... | collective-permute-start | bytes 786440 | tf_op jit(solution)/shard_map/ppermute | solution.py:173
  52.2 0.9 collective-permute-start.16
  53.1 1.4 %collective-permute-start.18 = (bf16[2,4,2,8,1024]{4,3,2,1,0:T(8,128)(2,1)S(1)}, bf16[2,4,2,8,1024]{4,3,2,1,0:T(8,128)(2,1)S(1)}, u32[]{:S(2)}, u32[]{:S(2)}) collective-permute-start(bf16[2,4,2,8,1024]{4,3,2,1,0:T(8,128)(2,1)S(1)} %pad_maximum_fusion.refs_0_), channel_id=1, source_target_pairs={{0,1},{1,0},{2,3},{3,2},{4,5},{5,4},{6,7},{7,6},{8,9},{9,8},{10,11... | collective-permute-start | bytes 786440 | tf_op jit(solution)/shard_map/ppermute | solution.py:137
  54.5 3.2 %collective-permute-done.17.refs_3_ = bf16[2,4,2,8,1024]{4,3,2,1,0:T(8,128)(2,1)S(1)} collective-permute-done((bf16[2,4,2,8,1024]{4,3,2,1,0:T(8,128)(2,1)S(1)}, bf16[2,4,2,8,1024]{4,3,2,1,0:T(8,128)(2,1)S(1)}, u32[]{:S(2)}, u32[]{:S(2)}) %collective-permute-start.17) | collective-permute-done | bytes 262176 | tf_op jit(solution)/shard_map/ppermute | solution.py:173
  57.7 6.6 %collective-permute-start.21 = (bf16[2,4,2,8,1024]{4,3,2,1,0:T(8,128)(2,1)S(1)}, bf16[2,4,2,8,1024]{4,3,2,1,0:T(8,128)(2,1)S(1)}, u32[]{:S(2)}, u32[]{:S(2)}) collective-permute-start(bf16[2,4,2,8,1024]{4,3,2,1,0:T(8,128)(2,1)S(1)} %collective-permute-done.17.refs_3_), channel_id=1, source_target_pairs={{0,1},{1,0},{2,3},{3,2},{4,5},{5,4},{6,7},{7,6},{8,9},{9,8},{10,11... | collective-permute-start | bytes 786440 | tf_op jit(solution)/shard_map/ppermute | solution.py:137
  64.4 0.0 collective-permute-start.20
  64.4 3.3 %collective-permute-done.15.refs_1_ = bf16[2,4,2,8,1024]{4,3,2,1,0:T(8,128)(2,1)S(1)} collective-permute-done((bf16[2,4,2,8,1024]{4,3,2,1,0:T(8,128)(2,1)S(1)}, bf16[2,4,2,8,1024]{4,3,2,1,0:T(8,128)(2,1)S(1)}, u32[]{:S(2)}, u32[]{:S(2)}) %collective-permute-start.15) | collective-permute-done | bytes 262176 | tf_op jit(solution)/shard_map/ppermute | solution.py:173
  67.6 0.4 collective-permute-start.19
  68.1 0.0 collective-permute-done.18.refs_4_
  68.1 1.1 %collective-permute-done.19.refs_5_ = bf16[2,4,2,8,1024]{4,3,2,1,0:T(8,128)(2,1)S(1)} collective-permute-done((bf16[2,4,2,8,1024]{4,3,2,1,0:T(8,128)(2,1)S(1)}, bf16[2,4,2,8,1024]{4,3,2,1,0:T(8,128)(2,1)S(1)}, u32[]{:S(2)}, u32[]{:S(2)}) %collective-permute-start.19) | collective-permute-done | bytes 262176 | tf_op jit(solution)/shard_map/ppermute | solution.py:137
  69.2 24.2 %all-to-all-done.refs_8_ = bf16[16,128,1024]{2,1,0:T(8,128)(2,1)} async-done(((bf16[16,128,1024]{2,1,0:T(8,128)(2,1)}), bf16[16,128,1024]{2,1,0:T(8,128)(2,1)}, u32[]{:S(2)}, u32[]{:S(2)}) %all-to-all-start) | async-done | bytes 4194336 | tf_op jit(solution)/shard_map/all_to_all | solution.py:215
  93.4 4.3 %shard_map.144 = bf16[8,128,2048]{2,1,0:T(8,128)(2,1)} custom-call(f32[64,128]{1,0:T(8,128)S(1)} %bitcast_convert_fusion.bt_ref, bf16[2,4,2,8,1024]{4,3,2,1,0:T(8,128)(2,1)S(1)} %pad_maximum_fusion.refs_0_, bf16[2,4,2,8,1024]{4,3,2,1,0:T(8,128)(2,1)S(1)} %collective-permute-done.15.refs_1_, bf16[2,4,2,8,1024]{4,3,2,1,0:T(8,128)(2,1)S(1)} %collective-permute-done.16.refs_2_, ...), custom_call_target="tpu_custom_call" | custom-call | flops 268435456 | bytes 10485760 | tf_op jit(solution)/shard_map/pallas_call | solution.py:112
  (43 shorter events, 0.4 us)
Async XLA Ops:
  0.6 21.1 %copy-start.3 = (f32[4,2048]{1,0:T(4,128)S(1)}, f32[4,2048]{1,0:T(4,128)}, u32[]{:S(2)}) copy-start(f32[4,2048]{1,0:T(4,128)} %param.15) | copy-start | bytes 98308
  0.6 21.1 %copy-start.2 = (f32[4,2048]{1,0:T(4,128)S(1)}, f32[4,2048]{1,0:T(4,128)}, u32[]{:S(2)}) copy-start(f32[4,2048]{1,0:T(4,128)} %param.14) | copy-start | bytes 98308
  0.7 21.1 %copy-start.1 = (f32[4,2048]{1,0:T(4,128)S(1)}, f32[4,2048]{1,0:T(4,128)}, u32[]{:S(2)}) copy-start(f32[4,2048]{1,0:T(4,128)} %param.13) | copy-start | bytes 98308
  0.7 25.5 %copy-start.6 = (f32[8,1024]{1,0:T(8,128)S(1)}, f32[8,1024]{1,0:T(8,128)}, u32[]{:S(2)}) copy-start(f32[8,1024]{1,0:T(8,128)} %param.12) | copy-start | bytes 98308
  0.7 25.4 %copy-start.5 = (f32[8,1024]{1,0:T(8,128)S(1)}, f32[8,1024]{1,0:T(8,128)}, u32[]{:S(2)}) copy-start(f32[8,1024]{1,0:T(8,128)} %param.11) | copy-start | bytes 98308
  0.7 25.4 %copy-start.4 = (f32[8,1024]{1,0:T(8,128)S(1)}, f32[8,1024]{1,0:T(8,128)}, u32[]{:S(2)}) copy-start(f32[8,1024]{1,0:T(8,128)} %param.10) | copy-start | bytes 98308
  2.0 7.7 %collective-permute-start = (f32[4,2,4,2048]{3,2,1,0:T(4,128)S(1)}, f32[4,2,4,2048]{3,2,1,0:T(4,128)S(1)}, u32[]{:S(2)}, u32[]{:S(2)}) collective-permute-start(f32[4,2,4,2048]{3,2,1,0:T(4,128)S(1)} %dynamic-slice_bitcast_fusion), channel_id=1, source_target_pairs={{0,1},{1,0},{2,3},{3,2},{4,5},{5,4},{6,7},{7,6},{8,9},{9,8},{10,11... | collective-permute-start | bytes 786440 | tf_op jit(solution)/shard_map/ppermute | solution.py:137
  4.4 6.6 %collective-permute-start.7 = (f32[2,8,1024]{2,1,0:T(8,128)S(1)}, f32[2,8,1024]{2,1,0:T(8,128)S(1)}, u32[]{:S(2)}, u32[]{:S(2)}) collective-permute-start(f32[2,8,1024]{2,1,0:T(8,128)S(1)} %get-tuple-element.22), channel_id=1, source_target_pairs={{0,32},{16,48},{32,0},{48,16},{64,96},{80,112},{96,64},{112,80},{1... | collective-permute-start | bytes 196616 | tf_op jit(solution)/shard_map/ppermute | solution.py:173
  8.2 4.3 %collective-permute-start.8 = (f32[2,8,1024]{2,1,0:T(8,128)S(1)}, f32[2,8,1024]{2,1,0:T(8,128)S(1)}, u32[]{:S(2)}, u32[]{:S(2)}) collective-permute-start(f32[2,8,1024]{2,1,0:T(8,128)S(1)} %get-tuple-element.23), channel_id=1, source_target_pairs={{0,48},{16,0},{32,16},{48,32},{64,112},{80,64},{96,80},{112,96},{1... | collective-permute-start | bytes 196616 | tf_op jit(solution)/shard_map/ppermute | solution.py:173
  8.6 4.3 %collective-permute-start.6 = (f32[2,8,1024]{2,1,0:T(8,128)S(1)}, f32[2,8,1024]{2,1,0:T(8,128)S(1)}, u32[]{:S(2)}, u32[]{:S(2)}) collective-permute-start(f32[2,8,1024]{2,1,0:T(8,128)S(1)} %get-tuple-element.24), channel_id=1, source_target_pairs={{0,16},{16,32},{32,48},{48,0},{64,80},{80,96},{96,112},{112,64},{1... | collective-permute-start | bytes 196616 | tf_op jit(solution)/shard_map/ppermute | solution.py:173
  9.7 4.2 %collective-permute-start.1 = (f32[4,4,2048]{2,1,0:T(4,128)S(1)}, f32[4,4,2048]{2,1,0:T(4,128)S(1)}, u32[]{:S(2)}, u32[]{:S(2)}) collective-permute-start(f32[4,4,2048]{2,1,0:T(4,128)S(1)} %dynamic-slice_bitcast_fusion.1), channel_id=1, source_target_pairs={{0,2},{1,3},{2,0},{3,1},{4,6},{5,7},{6,4},{7,5},{8,10},{9,11},{10,... | collective-permute-start | bytes 393224 | tf_op jit(solution)/shard_map/ppermute | solution.py:141
  14.0 7.2 %collective-permute-start.3 = (f32[4,2048]{1,0:T(4,128)S(1)}, f32[4,2048]{1,0:T(4,128)S(1)}, u32[]{:S(2)}, u32[]{:S(2)}) collective-permute-start(f32[4,2048]{1,0:T(4,128)S(1)} %get-tuple-element.27), channel_id=1, source_target_pairs={{0,8},{1,9},{2,10},{3,11},{4,12},{5,13},{6,14},{7,15},{8,0},{9,1},... | collective-permute-start | bytes 98312 | tf_op jit(solution)/shard_map/ppermute | solution.py:145
  17.0 4.2 %collective-permute-start.4 = (f32[4,2048]{1,0:T(4,128)S(1)}, f32[4,2048]{1,0:T(4,128)S(1)}, u32[]{:S(2)}, u32[]{:S(2)}) collective-permute-start(f32[4,2048]{1,0:T(4,128)S(1)} %get-tuple-element.28), channel_id=1, source_target_pairs={{0,12},{1,13},{2,14},{3,15},{4,0},{5,1},{6,2},{7,3},{8,4},{9,5},{1... | collective-permute-start | bytes 98312 | tf_op jit(solution)/shard_map/ppermute | solution.py:145
  17.8 4.0 %collective-permute-start.2 = (f32[4,2048]{1,0:T(4,128)S(1)}, f32[4,2048]{1,0:T(4,128)S(1)}, u32[]{:S(2)}, u32[]{:S(2)}) collective-permute-start(f32[4,2048]{1,0:T(4,128)S(1)} %get-tuple-element.29), channel_id=1, source_target_pairs={{0,4},{1,5},{2,6},{3,7},{4,8},{5,9},{6,10},{7,11},{8,12},{9,13},{1... | collective-permute-start | bytes 98312 | tf_op jit(solution)/shard_map/ppermute | solution.py:145
  18.5 7.7 %collective-permute-start.9 = (f32[8,1024]{1,0:T(8,128)S(1)}, f32[8,1024]{1,0:T(8,128)S(1)}, u32[]{:S(2)}, u32[]{:S(2)}) collective-permute-start(f32[8,1024]{1,0:T(8,128)S(1)} %dynamic-slice_bitcast_fusion.5), channel_id=1, source_target_pairs={{0,64},{16,80},{32,96},{48,112},{64,0},{80,16},{96,32},{112,48},{1... | collective-permute-start | bytes 98312 | tf_op jit(solution)/shard_map/ppermute | solution.py:165
  22.4 13.0 %copy-start = (f32[4,2048]{1,0:T(4,128)}, f32[4,2048]{1,0:T(4,128)S(1)}, u32[]{:S(2)}) copy-start(f32[4,2048]{1,0:T(4,128)S(1)} %get-tuple-element.19) | copy-start | bytes 98308
  22.5 4.4 %collective-permute-start.5 = (bf16[4,2,4,128]{3,2,1,0:T(4,128)(2,1)S(1)}, bf16[4,2,4,128]{3,2,1,0:T(4,128)(2,1)S(1)}, u32[]{:S(2)}, u32[]{:S(2)}) collective-permute-start(bf16[4,2,4,128]{3,2,1,0:T(4,128)(2,1)S(1)} %bitcast.98), channel_id=1, source_target_pairs={{0,1},{1,0},{2,3},{3,2},{4,5},{5,4},{6,7},{7,6},{8,9},{9,8},{10,11... | collective-permute-start | bytes 24584 | tf_op jit(solution)/shard_map/ppermute | solution.py:137
  27.0 2.8 %collective-permute-start.10 = (bf16[8,1536]{1,0:T(8,128)(2,1)S(1)}, bf16[8,1536]{1,0:T(8,128)(2,1)S(1)}, u32[]{:S(2)}, u32[]{:S(2)}) collective-permute-start(bf16[8,1536]{1,0:T(8,128)(2,1)S(1)} %pad_maximum_fusion.6), channel_id=1, source_target_pairs={{0,2},{1,3},{2,0},{3,1},{4,6},{5,7},{6,4},{7,5},{8,10},{9,11},{10,... | collective-permute-start | bytes 73736 | tf_op jit(solution)/shard_map/ppermute | solution.py:141
  29.8 2.9 %collective-permute-start.13 = (bf16[2,8,1152]{2,1,0:T(8,128)(2,1)S(1)}, bf16[2,8,1152]{2,1,0:T(8,128)(2,1)S(1)}, u32[]{:S(2)}, u32[]{:S(2)}) collective-permute-start(bf16[2,8,1152]{2,1,0:T(8,128)(2,1)S(1)} %get-tuple-element.30), channel_id=1, source_target_pairs={{0,12},{1,13},{2,14},{3,15},{4,0},{5,1},{6,2},{7,3},{8,4},{9,5},{1... | collective-permute-start | bytes 110600 | tf_op jit(solution)/shard_map/ppermute | solution.py:145
  30.7 4.3 %collective-permute-start.12 = (bf16[2,8,1152]{2,1,0:T(8,128)(2,1)S(1)}, bf16[2,8,1152]{2,1,0:T(8,128)(2,1)S(1)}, u32[]{:S(2)}, u32[]{:S(2)}) collective-permute-start(bf16[2,8,1152]{2,1,0:T(8,128)(2,1)S(1)} %get-tuple-element.31), channel_id=1, source_target_pairs={{0,8},{1,9},{2,10},{3,11},{4,12},{5,13},{6,14},{7,15},{8,0},{9,1},... | collective-permute-start | bytes 110600 | tf_op jit(solution)/shard_map/ppermute | solution.py:145
  31.1 4.3 %collective-permute-start.11 = (bf16[2,8,1152]{2,1,0:T(8,128)(2,1)S(1)}, bf16[2,8,1152]{2,1,0:T(8,128)(2,1)S(1)}, u32[]{:S(2)}, u32[]{:S(2)}) collective-permute-start(bf16[2,8,1152]{2,1,0:T(8,128)(2,1)S(1)} %get-tuple-element.32), channel_id=1, source_target_pairs={{0,4},{1,5},{2,6},{3,7},{4,8},{5,9},{6,10},{7,11},{8,12},{9,13},{1... | collective-permute-start | bytes 110600 | tf_op jit(solution)/shard_map/ppermute | solution.py:145
  35.4 58.0 %all-to-all-start = ((bf16[16,128,1024]{2,1,0:T(8,128)(2,1)}), bf16[16,128,1024]{2,1,0:T(8,128)(2,1)}, u32[]{:S(2)}, u32[]{:S(2)}) async-start(bf16[16,128,1024]{2,1,0:T(8,128)(2,1)} %bitcast.91), calls=%async_computation | async-start | bytes 8388608 | tf_op jit(solution)/shard_map/all_to_all | solution.py:215
  43.7 6.7 %collective-permute-start.14 = (bf16[4,2,8,1024]{3,2,1,0:T(8,128)(2,1)S(1)}, bf16[4,2,8,1024]{3,2,1,0:T(8,128)(2,1)S(1)}, u32[]{:S(2)}, u32[]{:S(2)}) collective-permute-start(bf16[4,2,8,1024]{3,2,1,0:T(8,128)(2,1)S(1)} %get-tuple-element.26), channel_id=1, source_target_pairs={{0,66},{1,67},{2,64},{3,65},{4,70},{5,71},{6,68},{7,69},{8,74},{9,... | collective-permute-start | bytes 393224 | tf_op jit(solution)/shard_map/ppermute | solution.py:169
  50.5 7.2 %collective-permute-start.17 = (bf16[2,4,2,8,1024]{4,3,2,1,0:T(8,128)(2,1)S(1)}, bf16[2,4,2,8,1024]{4,3,2,1,0:T(8,128)(2,1)S(1)}, u32[]{:S(2)}, u32[]{:S(2)}) collective-permute-start(bf16[2,4,2,8,1024]{4,3,2,1,0:T(8,128)(2,1)S(1)} %pad_maximum_fusion.refs_0_), channel_id=1, source_target_pairs={{0,48},{16,0},{32,16},{48,32},{64,112},{80,64},{96,80},{112,96},{1... | collective-permute-start | bytes 786440 | tf_op jit(solution)/shard_map/ppermute | solution.py:173
  52.2 12.2 %collective-permute-start.16 = (bf16[2,4,2,8,1024]{4,3,2,1,0:T(8,128)(2,1)S(1)}, bf16[2,4,2,8,1024]{4,3,2,1,0:T(8,128)(2,1)S(1)}, u32[]{:S(2)}, u32[]{:S(2)}) collective-permute-start(bf16[2,4,2,8,1024]{4,3,2,1,0:T(8,128)(2,1)S(1)} %pad_maximum_fusion.refs_0_), channel_id=1, source_target_pairs={{0,32},{16,48},{32,0},{48,16},{64,96},{80,112},{96,64},{112,80},{1... | collective-permute-start | bytes 786440 | tf_op jit(solution)/shard_map/ppermute | solution.py:173
  53.1 14.6 %collective-permute-start.15 = (bf16[2,4,2,8,1024]{4,3,2,1,0:T(8,128)(2,1)S(1)}, bf16[2,4,2,8,1024]{4,3,2,1,0:T(8,128)(2,1)S(1)}, u32[]{:S(2)}, u32[]{:S(2)}) collective-permute-start(bf16[2,4,2,8,1024]{4,3,2,1,0:T(8,128)(2,1)S(1)} %pad_maximum_fusion.refs_0_), channel_id=1, source_target_pairs={{0,16},{16,32},{32,48},{48,0},{64,80},{80,96},{96,112},{112,64},{1... | collective-permute-start | bytes 786440 | tf_op jit(solution)/shard_map/ppermute | solution.py:173
  53.1 15.0 %collective-permute-start.18 = (bf16[2,4,2,8,1024]{4,3,2,1,0:T(8,128)(2,1)S(1)}, bf16[2,4,2,8,1024]{4,3,2,1,0:T(8,128)(2,1)S(1)}, u32[]{:S(2)}, u32[]{:S(2)}) collective-permute-start(bf16[2,4,2,8,1024]{4,3,2,1,0:T(8,128)(2,1)S(1)} %pad_maximum_fusion.refs_0_), channel_id=1, source_target_pairs={{0,1},{1,0},{2,3},{3,2},{4,5},{5,4},{6,7},{7,6},{8,9},{9,8},{10,11... | collective-permute-start | bytes 786440 | tf_op jit(solution)/shard_map/ppermute | solution.py:137
  57.7 10.3 %collective-permute-start.21 = (bf16[2,4,2,8,1024]{4,3,2,1,0:T(8,128)(2,1)S(1)}, bf16[2,4,2,8,1024]{4,3,2,1,0:T(8,128)(2,1)S(1)}, u32[]{:S(2)}, u32[]{:S(2)}) collective-permute-start(bf16[2,4,2,8,1024]{4,3,2,1,0:T(8,128)(2,1)S(1)} %collective-permute-done.17.refs_3_), channel_id=1, source_target_pairs={{0,1},{1,0},{2,3},{3,2},{4,5},{5,4},{6,7},{7,6},{8,9},{9,8},{10,11... | collective-permute-start | bytes 786440 | tf_op jit(solution)/shard_map/ppermute | solution.py:137
  64.4 3.7 %collective-permute-start.20 = (bf16[2,4,2,8,1024]{4,3,2,1,0:T(8,128)(2,1)S(1)}, bf16[2,4,2,8,1024]{4,3,2,1,0:T(8,128)(2,1)S(1)}, u32[]{:S(2)}, u32[]{:S(2)}) collective-permute-start(bf16[2,4,2,8,1024]{4,3,2,1,0:T(8,128)(2,1)S(1)} %collective-permute-done.16.refs_2_), channel_id=1, source_target_pairs={{0,1},{1,0},{2,3},{3,2},{4,5},{5,4},{6,7},{7,6},{8,9},{9,8},{10,11... | collective-permute-start | bytes 786440 | tf_op jit(solution)/shard_map/ppermute | solution.py:137
  67.6 1.6 %collective-permute-start.19 = (bf16[2,4,2,8,1024]{4,3,2,1,0:T(8,128)(2,1)S(1)}, bf16[2,4,2,8,1024]{4,3,2,1,0:T(8,128)(2,1)S(1)}, u32[]{:S(2)}, u32[]{:S(2)}) collective-permute-start(bf16[2,4,2,8,1024]{4,3,2,1,0:T(8,128)(2,1)S(1)} %collective-permute-done.15.refs_1_), channel_id=1, source_target_pairs={{0,1},{1,0},{2,3},{3,2},{4,5},{5,4},{6,7},{7,6},{8,9},{9,8},{10,11... | collective-permute-start | bytes 786440 | tf_op jit(solution)/shard_map/ppermute | solution.py:137

commit v4 on v3

--- a/solution.py
+++ b/solution.py
@@ -188,16 +188,20 @@
     x_hi, z = row // 4, row % 4
     y, x, core = col // 4, (col // 2) % 2, col % 2
 
+    bt_part = grad_bt_parts.reshape(4, 2, 2, 4, 2048)
+    kept, sent = lax.optimization_barrier((pick(bt_part, core, 2), pick(bt_part, 1 - core, 2)))
+    bt_part = kept + over_core(sent)
     part = grad_a_parts.reshape(2, 4, 8, 1024)
-    part = pick(part, z, 1) + sum(over_z(pick(part, (z + k) % 4, 1), k) for k in (1, 2, 3))
+    kept, *sent = lax.optimization_barrier([pick(part, (z + k) % 4, 1) for k in range(4)])
+    bt_part, *sent = lax.optimization_barrier((bt_part, *sent))
+    part = kept + sum(over_z(array, k) for array, k in zip(sent, (1, 2, 3)))
     grad_a = pick(part, x_hi, 0) + over_x_hi(pick(part, 1 - x_hi, 0))
-    part = grad_bt_parts.reshape(4, 2, 2, 4, 2048)
-    part = pick(part, core, 2) + over_core(pick(part, 1 - core, 2))
-    part = pick(part, x, 1) + over_x(pick(part, 1 - x, 1))
-    grad_bt = pick(part, y, 0) + sum(over_y(pick(part, (y + k) % 4, 0), k) for k in (1, 2, 3))
-
-    a_new, a_first_new, a_second_new = adam_step(a_master, a_first, a_second, grad_a)
-    bt_new, bt_first_new, bt_second_new = adam_step(bt_master, bt_first, bt_second, grad_bt)
+    bt_part = pick(bt_part, x, 1) + over_x(pick(bt_part, 1 - x, 1))
+    bt_part = two_of(bt_part, y, y ^ 3, 0) + over_col(two_of(bt_part, y ^ 1, y ^ 2, 0), 4)
+    grad_bt = bt_part[0] + over_col(bt_part[1], 12)
+
+    a_new = adam_step(a_master, a_first, a_second, grad_a)[0]
+    bt_new = adam_step(bt_master, bt_first, bt_second, grad_bt)[0]
 
     part = bt_new.reshape(4, 4, 2, 2, 128).transpose(1, 2, 3, 0, 4)
     part = jnp.concatenate([pick(part, core, 2), over_core(pick(part, 1 - core, 2))], axis=2)
@@ -211,7 +215,7 @@
         over_y(jnp.concatenate([a_near, pick(bt_near, (y + k) % 4, 0)], axis=2), k) for k in (1, 2, 3)
     ]
     weight = frozen_projection_weight.reshape(16, 128, 1024)
-    weight, *along_y = lax.optimization_barrier((weight, *along_y))
+    weight, grad_a, grad_bt, *along_y = lax.optimization_barrier((weight, grad_a, grad_bt, *along_y))
     arrived = lax.all_to_all(weight, "col", 0, 0, tiled=True)
     part = jnp.stack([a_near] + [came[:, :, :1024] for came in along_y])
     bt_rows = jnp.stack([pick(bt_near, y, 0)] + [came[:, :, 1024:] for came in along_y])
@@ -219,6 +223,8 @@
     a_parts = [part] + [over_z(part, k) for k in (1, 2, 3)]
     a_parts = a_parts + [over_core(part) for part in a_parts]
     saved = merge(bt_rows.reshape(R, 128).astype(jnp.float32), a_parts, arrived)
+    a_new, a_first_new, a_second_new = adam_step(a_master, a_first, a_second, grad_a)
+    bt_new, bt_first_new, bt_second_new = adam_step(bt_master, bt_first, bt_second, grad_bt)
     return (saved, a_new, a_first_new, a_second_new, bt_new, bt_first_new, bt_second_new)
 
 

time: 98 us -> 95.5 us (0.974)
  starting transfers between devices: 44 us -> 42.5 us
    ppermute x0 -> x2, starting transfers between devices: none -> 4.19 us  [over_col(): return lax.ppermute(array, 'col', [(i, i ^ mask) for i in range(16)])]
    ppermute x6 -> x3, starting transfers between devices: 6.09 us -> 3.35 us  [over_y(): lax.ppermute(array, 'col', [(i, (i + 4 * k) % 16) for i in range(16)])]
    ppermute x6, starting transfers between devices: 13.5 us -> 11.5 us  [over_core(): return lax.ppermute(array, 'col', [(i, i ^ 1) for i in range(16)])]
    all_to_all x1, waiting for transfers between devices: 24.2 us -> 26.1 us  [per_device(): arrived = lax.all_to_all(weight, 'col', 0, 0, tiled=True)]
    ppermute x6 -> x3, waiting for transfers between devices: 4.57 us -> 2.8 us  [over_y(): lax.ppermute(array, 'col', [(i, (i + 4 * k) % 16) for i in range(16)])]
    ppermute x6, starting transfers between devices: 7.84 us -> 9.4 us  [over_z(): lax.ppermute(array, 'row', [(i, i // 4 * 4 + (i + k) % 4) for i in range(...]
    ppermute x6, waiting for transfers between devices: 8.42 us -> 6.99 us  [over_z(): lax.ppermute(array, 'row', [(i, i // 4 * 4 + (i + k) % 4) for i in range(...]
    ppermute x2, starting transfers between devices: 2.58 us -> 1.46 us  [over_x(): return lax.ppermute(array, 'col', [(i, i ^ 2) for i in range(16)])]
  transfers between devices with their start and end apart: 23 -> 22, of which waited for: 14 -> 15; matrix products, arithmetic and copies ran while one was open for 3% -> 3% of each run, Pallas kernels for 0% -> 0%
where the time goes in v4:
time: 95.5 us; the launch traced here: 95.3 us
  waiting for transfers between devices  43.3 us (45%)
  starting transfers between devices  42.5 us (45%)
  Pallas kernels  4.27 us (4%)
  local copies, waits for them, and re-layouts  2.41 us (3%)
  other arithmetic  1.73 us (2%)
  between operations  1.02 us (1%)
    all_to_all x1, waiting for transfers between devices, per_device(): arrived = lax.all_to_all(weight, 'col', 0, 0, tiled=True)  26.1 us
    ppermute x6, starting transfers between devices, over_core(): return lax.ppermute(array, 'col', [(i, i ^ 1) for i in range(16)])  11.5 us
    ppermute x6, starting transfers between devices, over_z(): lax.ppermute(array, 'row', [(i, i // 4 * 4 + (i + k) % 4) for i in range(...  9.4 us
    all_to_all x1, starting transfers between devices, per_device(): arrived = lax.all_to_all(weight, 'col', 0, 0, tiled=True)  7.48 us
    ppermute x6, waiting for transfers between devices, over_z(): lax.ppermute(array, 'row', [(i, i // 4 * 4 + (i + k) % 4) for i in range(...  6.99 us
    pallas_call x1, Pallas kernels, merge(): pl.pallas_call(merge_kernel, in_specs=[pl.BlockSpec(memory_space=pltpu.VM...  4.27 us
    ppermute x2, starting transfers between devices, over_col(): return lax.ppermute(array, 'col', [(i, i ^ mask) for i in range(16)])  4.19 us
    ppermute x3, starting transfers between devices, over_y(): lax.ppermute(array, 'col', [(i, (i + 4 * k) % 16) for i in range(16)])  3.35 us
  transfers between devices with their start and end apart: 22, of which 15 were waited for; matrix products, arithmetic and copies ran while one was open for 3% of the time, Pallas kernels for 0%

profile of v4, /device:TPU:1, one launch (start us, length us, event | category | flops | bytes accessed | tf_op | source)
XLA Modules:
  0.0 95.3 jit_solution(15684984840879240054)
XLA Ops:
  0.7 1.2 %reshape.35 = f32[4,2,2,4,2048]{4,3,2,1,0:T(4,128)S(1)} reshape(f32[1,64,2048]{2,1,0:T(8,128)} %param.17) | data formatting | bytes 1048576 | tf_op jit(solution)/shard_map/reshape | solution.py:191
  2.0 1.5 %collective-permute-start = (f32[4,2,4,2048]{3,2,0,1:T(4,128)S(1)}, f32[4,2,4,2048]{3,2,0,1:T(4,128)S(1)}, u32[]{:S(2)}, u32[]{:S(2)}) collective-permute-start(f32[4,2,4,2048]{3,2,0,1:T(4,128)S(1)} %get-tuple-element.24), channel_id=1, source_target_pairs={{0,1},{1,0},{2,3},{3,2},{4,5},{5,4},{6,7},{7,6},{8,9},{9,8},{10,11... | collective-permute-start | bytes 786440 | tf_op jit(solution)/shard_map/ppermute | solution.py:137
  3.5 1.0 %dynamic-slice_bitcast_fusion.1 = (f32[2,8,1024]{2,1,0:T(8,128)S(1)}, f32[2,8,1024]{2,1,0:T(8,128)S(1)}, f32[2,8,1024]{2,1,0:T(8,128)S(1)}, f32[2,8,1024]{2,1,0:T(8,128)S(1)}) fusion(f32[2,4,8,1024]{3,2,1,0:T(8,128)} %bitcast.82, s32[]{:T(128)S(6)} %select_n.128, s32[]{:T(128)S(6)} %select_n.126, s32[]{:T(128)S(6)} %select_n.124, s32[]{:T(128)S(6)} %select_n.122), kind=kLoop, calls=%fused_computation.9 | loop fusion | bytes 524304 | tf_op jit(solution)/shard_map/jit(dynamic_index_in_dim)/squeeze | solution.py:133
  4.5 0.2 collective-permute-done
  4.7 0.1 add.182
  4.8 1.4 %collective-permute-start.1 = (f32[4,4,2048]{2,1,0:T(4,128)S(1)}, f32[4,4,2048]{2,1,0:T(4,128)S(1)}, u32[]{:S(2)}, u32[]{:S(2)}) collective-permute-start(f32[4,4,2048]{2,1,0:T(4,128)S(1)} %dynamic-slice_bitcast_fusion), channel_id=1, source_target_pairs={{0,2},{1,3},{2,0},{3,1},{4,6},{5,7},{6,4},{7,5},{8,10},{9,11},{10,... | collective-permute-start | bytes 393224 | tf_op jit(solution)/shard_map/ppermute | solution.py:141
  6.2 1.6 %collective-permute-start.5 = (f32[2,8,1024]{2,1,0:T(8,128)S(1)}, f32[2,8,1024]{2,1,0:T(8,128)S(1)}, u32[]{:S(2)}, u32[]{:S(2)}) collective-permute-start(f32[2,8,1024]{2,1,0:T(8,128)S(1)} %get-tuple-element.30), channel_id=1, source_target_pairs={{0,16},{16,32},{32,48},{48,0},{64,80},{80,96},{96,112},{112,64},{1... | collective-permute-start | bytes 196616 | tf_op jit(solution)/shard_map/ppermute | solution.py:173
  7.8 3.3 %collective-permute-start.6 = (f32[2,8,1024]{2,1,0:T(8,128)S(1)}, f32[2,8,1024]{2,1,0:T(8,128)S(1)}, u32[]{:S(2)}, u32[]{:S(2)}) collective-permute-start(f32[2,8,1024]{2,1,0:T(8,128)S(1)} %get-tuple-element.31), channel_id=1, source_target_pairs={{0,32},{16,48},{32,0},{48,16},{64,96},{80,112},{96,64},{112,80},{1... | collective-permute-start | bytes 196616 | tf_op jit(solution)/shard_map/ppermute | solution.py:173
  11.1 0.7 collective-permute-start.7
  11.8 0.0 collective-permute-done.1
  11.9 1.4 %collective-permute-start.2 = (f32[2,4,2048]{2,1,0:T(4,128)S(1)}, f32[2,4,2048]{2,1,0:T(4,128)S(1)}, u32[]{:S(2)}, u32[]{:S(2)}) collective-permute-start(f32[2,4,2048]{2,1,0:T(4,128)S(1)} %pad_maximum_fusion.2), channel_id=1, source_target_pairs={{0,4},{1,5},{2,6},{3,7},{4,0},{5,1},{6,2},{7,3},{8,12},{9,13},{10,... | collective-permute-start | bytes 196616 | tf_op jit(solution)/shard_map/ppermute | solution.py:153
  13.3 0.4 collective-permute-done.6
  13.7 0.8 collective-permute-done.7
  14.5 0.6 collective-permute-done.2
  15.2 2.8 %collective-permute-start.3 = (f32[4,2048]{1,0:T(4,128)S(1)}, f32[4,2048]{1,0:T(4,128)S(1)}, u32[]{:S(2)}, u32[]{:S(2)}) collective-permute-start(f32[4,2048]{1,0:T(4,128)S(1)} %slice_bitcast_fusion), channel_id=1, source_target_pairs={{0,12},{1,13},{2,14},{3,15},{4,8},{5,9},{6,10},{7,11},{8,4},{9,5},... | collective-permute-start | bytes 98312 | tf_op jit(solution)/shard_map/ppermute | solution.py:153
  18.0 2.5 %collective-permute-start.8 = (f32[8,1024]{1,0:T(8,128)S(1)}, f32[8,1024]{1,0:T(8,128)S(1)}, u32[]{:S(2)}, u32[]{:S(2)}) collective-permute-start(f32[8,1024]{1,0:T(8,128)S(1)} %dynamic-slice_bitcast_fusion.5), channel_id=1, source_target_pairs={{0,64},{16,80},{32,96},{48,112},{64,0},{80,16},{96,32},{112,48},{1... | collective-permute-start | bytes 98312 | tf_op jit(solution)/shard_map/ppermute | solution.py:165
  20.5 0.0 collective-permute-done.3
  20.5 0.1 multiply_subtract_fusion.2
  20.7 3.3 %collective-permute-start.4 = (bf16[4,2,4,128]{3,2,1,0:T(4,128)(2,1)S(1)}, bf16[4,2,4,128]{3,2,1,0:T(4,128)(2,1)S(1)}, u32[]{:S(2)}, u32[]{:S(2)}) collective-permute-start(bf16[4,2,4,128]{3,2,1,0:T(4,128)(2,1)S(1)} %bitcast.87), channel_id=1, source_target_pairs={{0,1},{1,0},{2,3},{3,2},{4,5},{5,4},{6,7},{7,6},{8,9},{9,8},{10,11... | collective-permute-start | bytes 24584 | tf_op jit(solution)/shard_map/ppermute | solution.py:137
  23.9 0.0 collective-permute-done.8
  24.0 0.7 collective-permute-done.4
  24.8 0.1 collective-permute-start.9
  24.9 2.6 %collective-permute-done.9 = bf16[8,1536]{1,0:T(8,128)(2,1)S(1)} collective-permute-done((bf16[8,1536]{1,0:T(8,128)(2,1)S(1)}, bf16[8,1536]{1,0:T(8,128)(2,1)S(1)}, u32[]{:S(2)}, u32[]{:S(2)}) %collective-permute-start.9) | collective-permute-done | bytes 24608 | tf_op jit(solution)/shard_map/ppermute | solution.py:141
  27.6 0.1 collective-permute-start.10
  27.7 3.3 %collective-permute-start.11 = (bf16[2,8,1152]{2,1,0:T(8,128)(2,1)S(1)}, bf16[2,8,1152]{2,1,0:T(8,128)(2,1)S(1)}, u32[]{:S(2)}, u32[]{:S(2)}) collective-permute-start(bf16[2,8,1152]{2,1,0:T(8,128)(2,1)S(1)} %get-tuple-element.62), channel_id=1, source_target_pairs={{0,8},{1,9},{2,10},{3,11},{4,12},{5,13},{6,14},{7,15},{8,0},{9,1},... | collective-permute-start | bytes 110600 | tf_op jit(solution)/shard_map/ppermute | solution.py:145
  30.9 0.0 collective-permute-start.12
  30.9 0.7 collective-permute-done.10
  31.7 1.0 %collective-permute-done.11 = bf16[2,8,1152]{2,1,0:T(8,128)(2,1)S(1)} collective-permute-done((bf16[2,8,1152]{2,1,0:T(8,128)(2,1)S(1)}, bf16[2,8,1152]{2,1,0:T(8,128)(2,1)S(1)}, u32[]{:S(2)}, u32[]{:S(2)}) %collective-permute-start.11) | collective-permute-done | bytes 36896 | tf_op jit(solution)/shard_map/ppermute | solution.py:145
  32.7 1.1 %collective-permute-done.12 = bf16[2,8,1152]{2,1,0:T(8,128)(2,1)S(1)} collective-permute-done((bf16[2,8,1152]{2,1,0:T(8,128)(2,1)S(1)}, bf16[2,8,1152]{2,1,0:T(8,128)(2,1)S(1)}, u32[]{:S(2)}, u32[]{:S(2)}) %collective-permute-start.12) | collective-permute-done | bytes 36896 | tf_op jit(solution)/shard_map/ppermute | solution.py:145
  33.7 7.5 %all-to-all-start = ((bf16[16,128,1024]{2,1,0:T(8,128)(2,1)}), bf16[16,128,1024]{2,1,0:T(8,128)(2,1)}, u32[]{:S(2)}, u32[]{:S(2)}) async-start(bf16[16,128,1024]{2,1,0:T(8,128)(2,1)} %bitcast.81), calls=%async_computation | async-start | bytes 8388608 | tf_op jit(solution)/shard_map/all_to_all | solution.py:219
  41.3 2.7 %collective-permute-start.13 = (bf16[4,2,8,1024]{3,2,1,0:T(8,128)(2,1)S(1)}, bf16[4,2,8,1024]{3,2,1,0:T(8,128)(2,1)S(1)}, u32[]{:S(2)}, u32[]{:S(2)}) collective-permute-start(bf16[4,2,8,1024]{3,2,1,0:T(8,128)(2,1)S(1)} %get-tuple-element.56), channel_id=1, source_target_pairs={{0,66},{1,67},{2,64},{3,65},{4,70},{5,71},{6,68},{7,69},{8,74},{9,... | collective-permute-start | bytes 393224 | tf_op jit(solution)/shard_map/ppermute | solution.py:169
  44.0 0.7 multiply_subtract_fusion
  44.7 2.8 %collective-permute-done.13 = bf16[4,2,8,1024]{3,2,1,0:T(8,128)(2,1)S(1)} collective-permute-done((bf16[4,2,8,1024]{3,2,1,0:T(8,128)(2,1)S(1)}, bf16[4,2,8,1024]{3,2,1,0:T(8,128)(2,1)S(1)}, u32[]{:S(2)}, u32[]{:S(2)}) %collective-permute-start.13) | collective-permute-done | bytes 131104 | tf_op jit(solution)/shard_map/ppermute | solution.py:169
  47.5 0.8 collective-permute-start.14
  48.3 2.2 %collective-permute-start.15 = (bf16[2,4,2,8,1024]{4,3,2,1,0:T(8,128)(2,1)S(1)}, bf16[2,4,2,8,1024]{4,3,2,1,0:T(8,128)(2,1)S(1)}, u32[]{:S(2)}, u32[]{:S(2)}) collective-permute-start(bf16[2,4,2,8,1024]{4,3,2,1,0:T(8,128)(2,1)S(1)} %pad_maximum_fusion.refs_0_), channel_id=1, source_target_pairs={{0,32},{16,48},{32,0},{48,16},{64,96},{80,112},{96,64},{112,80},{1... | collective-permute-start | bytes 786440 | tf_op jit(solution)/shard_map/ppermute | solution.py:173
  50.5 0.7 collective-permute-start.16
  51.3 1.8 %collective-permute-start.17 = (bf16[2,4,2,8,1024]{4,3,2,1,0:T(8,128)(2,1)S(1)}, bf16[2,4,2,8,1024]{4,3,2,1,0:T(8,128)(2,1)S(1)}, u32[]{:S(2)}, u32[]{:S(2)}) collective-permute-start(bf16[2,4,2,8,1024]{4,3,2,1,0:T(8,128)(2,1)S(1)} %pad_maximum_fusion.refs_0_), channel_id=1, source_target_pairs={{0,1},{1,0},{2,3},{3,2},{4,5},{5,4},{6,7},{7,6},{8,9},{9,8},{10,11... | collective-permute-start | bytes 786440 | tf_op jit(solution)/shard_map/ppermute | solution.py:137
  53.0 2.7 %collective-permute-done.14.refs_1_ = bf16[2,4,2,8,1024]{4,3,2,1,0:T(8,128)(2,1)S(1)} collective-permute-done((bf16[2,4,2,8,1024]{4,3,2,1,0:T(8,128)(2,1)S(1)}, bf16[2,4,2,8,1024]{4,3,2,1,0:T(8,128)(2,1)S(1)}, u32[]{:S(2)}, u32[]{:S(2)}) %collective-permute-start.14) | collective-permute-done | bytes 262176 | tf_op jit(solution)/shard_map/ppermute | solution.py:173
  55.7 2.9 %collective-permute-start.18 = (bf16[2,4,2,8,1024]{4,3,2,1,0:T(8,128)(2,1)S(1)}, bf16[2,4,2,8,1024]{4,3,2,1,0:T(8,128)(2,1)S(1)}, u32[]{:S(2)}, u32[]{:S(2)}) collective-permute-start(bf16[2,4,2,8,1024]{4,3,2,1,0:T(8,128)(2,1)S(1)} %collective-permute-done.14.refs_1_), channel_id=1, source_target_pairs={{0,1},{1,0},{2,3},{3,2},{4,5},{5,4},{6,7},{7,6},{8,9},{9,8},{10,11... | collective-permute-start | bytes 786440 | tf_op jit(solution)/shard_map/ppermute | solution.py:137
  58.6 3.1 %collective-permute-done.15.refs_2_ = bf16[2,4,2,8,1024]{4,3,2,1,0:T(8,128)(2,1)S(1)} collective-permute-done((bf16[2,4,2,8,1024]{4,3,2,1,0:T(8,128)(2,1)S(1)}, bf16[2,4,2,8,1024]{4,3,2,1,0:T(8,128)(2,1)S(1)}, u32[]{:S(2)}, u32[]{:S(2)}) %collective-permute-start.15) | collective-permute-done | bytes 262176 | tf_op jit(solution)/shard_map/ppermute | solution.py:173
  61.8 1.6 %collective-permute-start.19 = (bf16[2,4,2,8,1024]{4,3,2,1,0:T(8,128)(2,1)S(1)}, bf16[2,4,2,8,1024]{4,3,2,1,0:T(8,128)(2,1)S(1)}, u32[]{:S(2)}, u32[]{:S(2)}) collective-permute-start(bf16[2,4,2,8,1024]{4,3,2,1,0:T(8,128)(2,1)S(1)} %collective-permute-done.15.refs_2_), channel_id=1, source_target_pairs={{0,1},{1,0},{2,3},{3,2},{4,5},{5,4},{6,7},{7,6},{8,9},{9,8},{10,11... | collective-permute-start | bytes 786440 | tf_op jit(solution)/shard_map/ppermute | solution.py:137
  63.4 0.0 collective-permute-done.16.refs_3_
  63.4 0.4 collective-permute-start.20
  63.8 0.7 multiply_subtract_fusion.1
  64.4 0.1 collective-permute-done.19.refs_6_
  64.6 0.4 collective-permute-done.20.refs_7_
  64.9 26.1 %all-to-all-done.refs_8_ = bf16[16,128,1024]{2,1,0:T(8,128)(2,1)} async-done(((bf16[16,128,1024]{2,1,0:T(8,128)(2,1)}), bf16[16,128,1024]{2,1,0:T(8,128)(2,1)}, u32[]{:S(2)}, u32[]{:S(2)}) %all-to-all-start) | async-done | bytes 4194336 | tf_op jit(solution)/shard_map/all_to_all | solution.py:219
  91.0 4.3 %shard_map.144 = bf16[8,128,2048]{2,1,0:T(8,128)(2,1)} custom-call(f32[64,128]{1,0:T(8,128)S(1)} %bitcast_convert_fusion.bt_ref, bf16[2,4,2,8,1024]{4,3,2,1,0:T(8,128)(2,1)S(1)} %pad_maximum_fusion.refs_0_, bf16[2,4,2,8,1024]{4,3,2,1,0:T(8,128)(2,1)S(1)} %collective-permute-done.14.refs_1_, bf16[2,4,2,8,1024]{4,3,2,1,0:T(8,128)(2,1)S(1)} %collective-permute-done.15.refs_2_, ...), custom_call_target="tpu_custom_call" | custom-call | flops 268435456 | bytes 10485760 | tf_op jit(solution)/shard_map/pallas_call | solution.py:112
  (47 shorter events, 0.5 us)
Async XLA Ops:
  0.6 19.8 %copy-start = (f32[4,2048]{1,0:T(4,128)S(1)}, f32[4,2048]{1,0:T(4,128)}, u32[]{:S(2)}) copy-start(f32[4,2048]{1,0:T(4,128)} %param.13) | copy-start | bytes 98308
  0.6 19.8 %copy-start.2 = (f32[4,2048]{1,0:T(4,128)S(1)}, f32[4,2048]{1,0:T(4,128)}, u32[]{:S(2)}) copy-start(f32[4,2048]{1,0:T(4,128)} %param.14) | copy-start | bytes 98308
  0.7 19.8 %copy-start.1 = (f32[4,2048]{1,0:T(4,128)S(1)}, f32[4,2048]{1,0:T(4,128)}, u32[]{:S(2)}) copy-start(f32[4,2048]{1,0:T(4,128)} %param.15) | copy-start | bytes 98308
  0.7 23.3 %copy-start.3 = (f32[8,1024]{1,0:T(8,128)S(1)}, f32[8,1024]{1,0:T(8,128)}, u32[]{:S(2)}) copy-start(f32[8,1024]{1,0:T(8,128)} %param.10) | copy-start | bytes 98308
  0.7 23.2 %copy-start.5 = (f32[8,1024]{1,0:T(8,128)S(1)}, f32[8,1024]{1,0:T(8,128)}, u32[]{:S(2)}) copy-start(f32[8,1024]{1,0:T(8,128)} %param.11) | copy-start | bytes 98308
  0.7 23.2 %copy-start.4 = (f32[8,1024]{1,0:T(8,128)S(1)}, f32[8,1024]{1,0:T(8,128)}, u32[]{:S(2)}) copy-start(f32[8,1024]{1,0:T(8,128)} %param.12) | copy-start | bytes 98308
  2.0 2.7 %collective-permute-start = (f32[4,2,4,2048]{3,2,0,1:T(4,128)S(1)}, f32[4,2,4,2048]{3,2,0,1:T(4,128)S(1)}, u32[]{:S(2)}, u32[]{:S(2)}) collective-permute-start(f32[4,2,4,2048]{3,2,0,1:T(4,128)S(1)} %get-tuple-element.24), channel_id=1, source_target_pairs={{0,1},{1,0},{2,3},{3,2},{4,5},{5,4},{6,7},{7,6},{8,9},{9,8},{10,11... | collective-permute-start | bytes 786440 | tf_op jit(solution)/shard_map/ppermute | solution.py:137
  4.8 7.0 %collective-permute-start.1 = (f32[4,4,2048]{2,1,0:T(4,128)S(1)}, f32[4,4,2048]{2,1,0:T(4,128)S(1)}, u32[]{:S(2)}, u32[]{:S(2)}) collective-permute-start(f32[4,4,2048]{2,1,0:T(4,128)S(1)} %dynamic-slice_bitcast_fusion), channel_id=1, source_target_pairs={{0,2},{1,3},{2,0},{3,1},{4,6},{5,7},{6,4},{7,5},{8,10},{9,11},{10,... | collective-permute-start | bytes 393224 | tf_op jit(solution)/shard_map/ppermute | solution.py:141
  6.2 7.1 %collective-permute-start.5 = (f32[2,8,1024]{2,1,0:T(8,128)S(1)}, f32[2,8,1024]{2,1,0:T(8,128)S(1)}, u32[]{:S(2)}, u32[]{:S(2)}) collective-permute-start(f32[2,8,1024]{2,1,0:T(8,128)S(1)} %get-tuple-element.30), channel_id=1, source_target_pairs={{0,16},{16,32},{32,48},{48,0},{64,80},{80,96},{96,112},{112,64},{1... | collective-permute-start | bytes 196616 | tf_op jit(solution)/shard_map/ppermute | solution.py:173
  7.8 5.9 %collective-permute-start.6 = (f32[2,8,1024]{2,1,0:T(8,128)S(1)}, f32[2,8,1024]{2,1,0:T(8,128)S(1)}, u32[]{:S(2)}, u32[]{:S(2)}) collective-permute-start(f32[2,8,1024]{2,1,0:T(8,128)S(1)} %get-tuple-element.31), channel_id=1, source_target_pairs={{0,32},{16,48},{32,0},{48,16},{64,96},{80,112},{96,64},{112,80},{1... | collective-permute-start | bytes 196616 | tf_op jit(solution)/shard_map/ppermute | solution.py:173
  11.1 3.4 %collective-permute-start.7 = (f32[2,8,1024]{2,1,0:T(8,128)S(1)}, f32[2,8,1024]{2,1,0:T(8,128)S(1)}, u32[]{:S(2)}, u32[]{:S(2)}) collective-permute-start(f32[2,8,1024]{2,1,0:T(8,128)S(1)} %get-tuple-element.32), channel_id=1, source_target_pairs={{0,48},{16,0},{32,16},{48,32},{64,112},{80,64},{96,80},{112,96},{1... | collective-permute-start | bytes 196616 | tf_op jit(solution)/shard_map/ppermute | solution.py:173
  11.9 3.2 %collective-permute-start.2 = (f32[2,4,2048]{2,1,0:T(4,128)S(1)}, f32[2,4,2048]{2,1,0:T(4,128)S(1)}, u32[]{:S(2)}, u32[]{:S(2)}) collective-permute-start(f32[2,4,2048]{2,1,0:T(4,128)S(1)} %pad_maximum_fusion.2), channel_id=1, source_target_pairs={{0,4},{1,5},{2,6},{3,7},{4,0},{5,1},{6,2},{7,3},{8,12},{9,13},{10,... | collective-permute-start | bytes 196616 | tf_op jit(solution)/shard_map/ppermute | solution.py:153
  15.2 5.3 %collective-permute-start.3 = (f32[4,2048]{1,0:T(4,128)S(1)}, f32[4,2048]{1,0:T(4,128)S(1)}, u32[]{:S(2)}, u32[]{:S(2)}) collective-permute-start(f32[4,2048]{1,0:T(4,128)S(1)} %slice_bitcast_fusion), channel_id=1, source_target_pairs={{0,12},{1,13},{2,14},{3,15},{4,8},{5,9},{6,10},{7,11},{8,4},{9,5},... | collective-permute-start | bytes 98312 | tf_op jit(solution)/shard_map/ppermute | solution.py:153
  18.0 5.9 %collective-permute-start.8 = (f32[8,1024]{1,0:T(8,128)S(1)}, f32[8,1024]{1,0:T(8,128)S(1)}, u32[]{:S(2)}, u32[]{:S(2)}) collective-permute-start(f32[8,1024]{1,0:T(8,128)S(1)} %dynamic-slice_bitcast_fusion.5), channel_id=1, source_target_pairs={{0,64},{16,80},{32,96},{48,112},{64,0},{80,16},{96,32},{112,48},{1... | collective-permute-start | bytes 98312 | tf_op jit(solution)/shard_map/ppermute | solution.py:165
  20.7 4.1 %collective-permute-start.4 = (bf16[4,2,4,128]{3,2,1,0:T(4,128)(2,1)S(1)}, bf16[4,2,4,128]{3,2,1,0:T(4,128)(2,1)S(1)}, u32[]{:S(2)}, u32[]{:S(2)}) collective-permute-start(bf16[4,2,4,128]{3,2,1,0:T(4,128)(2,1)S(1)} %bitcast.87), channel_id=1, source_target_pairs={{0,1},{1,0},{2,3},{3,2},{4,5},{5,4},{6,7},{7,6},{8,9},{9,8},{10,11... | collective-permute-start | bytes 24584 | tf_op jit(solution)/shard_map/ppermute | solution.py:137
  24.8 2.8 %collective-permute-start.9 = (bf16[8,1536]{1,0:T(8,128)(2,1)S(1)}, bf16[8,1536]{1,0:T(8,128)(2,1)S(1)}, u32[]{:S(2)}, u32[]{:S(2)}) collective-permute-start(bf16[8,1536]{1,0:T(8,128)(2,1)S(1)} %pad_maximum_fusion.7), channel_id=1, source_target_pairs={{0,2},{1,3},{2,0},{3,1},{4,6},{5,7},{6,4},{7,5},{8,10},{9,11},{10,... | collective-permute-start | bytes 73736 | tf_op jit(solution)/shard_map/ppermute | solution.py:141
  27.6 4.1 %collective-permute-start.10 = (bf16[2,8,1152]{2,1,0:T(8,128)(2,1)S(1)}, bf16[2,8,1152]{2,1,0:T(8,128)(2,1)S(1)}, u32[]{:S(2)}, u32[]{:S(2)}) collective-permute-start(bf16[2,8,1152]{2,1,0:T(8,128)(2,1)S(1)} %get-tuple-element.63), channel_id=1, source_target_pairs={{0,4},{1,5},{2,6},{3,7},{4,8},{5,9},{6,10},{7,11},{8,12},{9,13},{1... | collective-permute-start | bytes 110600 | tf_op jit(solution)/shard_map/ppermute | solution.py:145
  27.7 5.0 %collective-permute-start.11 = (bf16[2,8,1152]{2,1,0:T(8,128)(2,1)S(1)}, bf16[2,8,1152]{2,1,0:T(8,128)(2,1)S(1)}, u32[]{:S(2)}, u32[]{:S(2)}) collective-permute-start(bf16[2,8,1152]{2,1,0:T(8,128)(2,1)S(1)} %get-tuple-element.62), channel_id=1, source_target_pairs={{0,8},{1,9},{2,10},{3,11},{4,12},{5,13},{6,14},{7,15},{8,0},{9,1},... | collective-permute-start | bytes 110600 | tf_op jit(solution)/shard_map/ppermute | solution.py:145
  30.9 2.8 %collective-permute-start.12 = (bf16[2,8,1152]{2,1,0:T(8,128)(2,1)S(1)}, bf16[2,8,1152]{2,1,0:T(8,128)(2,1)S(1)}, u32[]{:S(2)}, u32[]{:S(2)}) collective-permute-start(bf16[2,8,1152]{2,1,0:T(8,128)(2,1)S(1)} %get-tuple-element.61), channel_id=1, source_target_pairs={{0,12},{1,13},{2,14},{3,15},{4,0},{5,1},{6,2},{7,3},{8,4},{9,5},{1... | collective-permute-start | bytes 110600 | tf_op jit(solution)/shard_map/ppermute | solution.py:145
  33.7 57.3 %all-to-all-start = ((bf16[16,128,1024]{2,1,0:T(8,128)(2,1)}), bf16[16,128,1024]{2,1,0:T(8,128)(2,1)}, u32[]{:S(2)}, u32[]{:S(2)}) async-start(bf16[16,128,1024]{2,1,0:T(8,128)(2,1)} %bitcast.81), calls=%async_computation | async-start | bytes 8388608 | tf_op jit(solution)/shard_map/all_to_all | solution.py:219
  41.3 6.2 %collective-permute-start.13 = (bf16[4,2,8,1024]{3,2,1,0:T(8,128)(2,1)S(1)}, bf16[4,2,8,1024]{3,2,1,0:T(8,128)(2,1)S(1)}, u32[]{:S(2)}, u32[]{:S(2)}) collective-permute-start(bf16[4,2,8,1024]{3,2,1,0:T(8,128)(2,1)S(1)} %get-tuple-element.56), channel_id=1, source_target_pairs={{0,66},{1,67},{2,64},{3,65},{4,70},{5,71},{6,68},{7,69},{8,74},{9,... | collective-permute-start | bytes 393224 | tf_op jit(solution)/shard_map/ppermute | solution.py:169
  47.5 8.2 %collective-permute-start.14 = (bf16[2,4,2,8,1024]{4,3,2,1,0:T(8,128)(2,1)S(1)}, bf16[2,4,2,8,1024]{4,3,2,1,0:T(8,128)(2,1)S(1)}, u32[]{:S(2)}, u32[]{:S(2)}) collective-permute-start(bf16[2,4,2,8,1024]{4,3,2,1,0:T(8,128)(2,1)S(1)} %pad_maximum_fusion.refs_0_), channel_id=1, source_target_pairs={{0,16},{16,32},{32,48},{48,0},{64,80},{80,96},{96,112},{112,64},{1... | collective-permute-start | bytes 786440 | tf_op jit(solution)/shard_map/ppermute | solution.py:173
  48.3 13.4 %collective-permute-start.15 = (bf16[2,4,2,8,1024]{4,3,2,1,0:T(8,128)(2,1)S(1)}, bf16[2,4,2,8,1024]{4,3,2,1,0:T(8,128)(2,1)S(1)}, u32[]{:S(2)}, u32[]{:S(2)}) collective-permute-start(bf16[2,4,2,8,1024]{4,3,2,1,0:T(8,128)(2,1)S(1)} %pad_maximum_fusion.refs_0_), channel_id=1, source_target_pairs={{0,32},{16,48},{32,0},{48,16},{64,96},{80,112},{96,64},{112,80},{1... | collective-permute-start | bytes 786440 | tf_op jit(solution)/shard_map/ppermute | solution.py:173
  50.5 12.9 %collective-permute-start.16 = (bf16[2,4,2,8,1024]{4,3,2,1,0:T(8,128)(2,1)S(1)}, bf16[2,4,2,8,1024]{4,3,2,1,0:T(8,128)(2,1)S(1)}, u32[]{:S(2)}, u32[]{:S(2)}) collective-permute-start(bf16[2,4,2,8,1024]{4,3,2,1,0:T(8,128)(2,1)S(1)} %pad_maximum_fusion.refs_0_), channel_id=1, source_target_pairs={{0,48},{16,0},{32,16},{48,32},{64,112},{80,64},{96,80},{112,96},{1... | collective-permute-start | bytes 786440 | tf_op jit(solution)/shard_map/ppermute | solution.py:173
  51.3 13.2 %collective-permute-start.17 = (bf16[2,4,2,8,1024]{4,3,2,1,0:T(8,128)(2,1)S(1)}, bf16[2,4,2,8,1024]{4,3,2,1,0:T(8,128)(2,1)S(1)}, u32[]{:S(2)}, u32[]{:S(2)}) collective-permute-start(bf16[2,4,2,8,1024]{4,3,2,1,0:T(8,128)(2,1)S(1)} %pad_maximum_fusion.refs_0_), channel_id=1, source_target_pairs={{0,1},{1,0},{2,3},{3,2},{4,5},{5,4},{6,7},{7,6},{8,9},{9,8},{10,11... | collective-permute-start | bytes 786440 | tf_op jit(solution)/shard_map/ppermute | solution.py:137
  55.7 8.7 %collective-permute-start.18 = (bf16[2,4,2,8,1024]{4,3,2,1,0:T(8,128)(2,1)S(1)}, bf16[2,4,2,8,1024]{4,3,2,1,0:T(8,128)(2,1)S(1)}, u32[]{:S(2)}, u32[]{:S(2)}) collective-permute-start(bf16[2,4,2,8,1024]{4,3,2,1,0:T(8,128)(2,1)S(1)} %collective-permute-done.14.refs_1_), channel_id=1, source_target_pairs={{0,1},{1,0},{2,3},{3,2},{4,5},{5,4},{6,7},{7,6},{8,9},{9,8},{10,11... | collective-permute-start | bytes 786440 | tf_op jit(solution)/shard_map/ppermute | solution.py:137
  61.8 2.8 %collective-permute-start.19 = (bf16[2,4,2,8,1024]{4,3,2,1,0:T(8,128)(2,1)S(1)}, bf16[2,4,2,8,1024]{4,3,2,1,0:T(8,128)(2,1)S(1)}, u32[]{:S(2)}, u32[]{:S(2)}) collective-permute-start(bf16[2,4,2,8,1024]{4,3,2,1,0:T(8,128)(2,1)S(1)} %collective-permute-done.15.refs_2_), channel_id=1, source_target_pairs={{0,1},{1,0},{2,3},{3,2},{4,5},{5,4},{6,7},{7,6},{8,9},{9,8},{10,11... | collective-permute-start | bytes 786440 | tf_op jit(solution)/shard_map/ppermute | solution.py:137
  63.4 1.5 %collective-permute-start.20 = (bf16[2,4,2,8,1024]{4,3,2,1,0:T(8,128)(2,1)S(1)}, bf16[2,4,2,8,1024]{4,3,2,1,0:T(8,128)(2,1)S(1)}, u32[]{:S(2)}, u32[]{:S(2)}) collective-permute-start(bf16[2,4,2,8,1024]{4,3,2,1,0:T(8,128)(2,1)S(1)} %collective-permute-done.16.refs_3_), channel_id=1, source_target_pairs={{0,1},{1,0},{2,3},{3,2},{4,5},{5,4},{6,7},{7,6},{8,9},{9,8},{10,11... | collective-permute-start | bytes 786440 | tf_op jit(solution)/shard_map/ppermute | solution.py:137

commit v5 on v4

--- a/solution.py
+++ b/solution.py
@@ -129,6 +129,18 @@
     )(bt_rows, *a_parts, arrived)
 
 
+def hold_kernel(array_ref, held_ref):
+    held_ref[...] = array_ref[...]
+
+
+def hold(array):
+    return pl.pallas_call(
+        hold_kernel,
+        out_shape=jax.ShapeDtypeStruct(array.shape, array.dtype),
+        cost_estimate=pl.CostEstimate(flops=100000000000, bytes_accessed=1 << 18, transcendentals=0),
+    )(array)
+
+
 def pick(array, index, axis):
     return lax.dynamic_index_in_dim(array, index, axis, keepdims=False)
 
@@ -215,10 +227,11 @@
         over_y(jnp.concatenate([a_near, pick(bt_near, (y + k) % 4, 0)], axis=2), k) for k in (1, 2, 3)
     ]
     weight = frozen_projection_weight.reshape(16, 128, 1024)
-    weight, grad_a, grad_bt, *along_y = lax.optimization_barrier((weight, grad_a, grad_bt, *along_y))
+    weight, grad_a, grad_bt, a_near = lax.optimization_barrier((weight, grad_a, grad_bt, a_near))
     arrived = lax.all_to_all(weight, "col", 0, 0, tiled=True)
     part = jnp.stack([a_near] + [came[:, :, :1024] for came in along_y])
     bt_rows = jnp.stack([pick(bt_near, y, 0)] + [came[:, :, 1024:] for came in along_y])
+    part = hold(part)
     part = jnp.stack([part, over_x_hi_x(part)])
     a_parts = [part] + [over_z(part, k) for k in (1, 2, 3)]
     a_parts = a_parts + [over_core(part) for part in a_parts]

time: 95.5 us -> 92.2 us (0.965)
  waiting for transfers between devices: 43.3 us -> 37.6 us
  Pallas kernels: 4.27 us -> 5.84 us
  other arithmetic: 1.73 us -> 3.29 us
    all_to_all x1, waiting for transfers between devices: 26.1 us -> 20.8 us  [per_device(): arrived = lax.all_to_all(weight, 'col', 0, 0, tiled=True)]
    ppermute x3, waiting for transfers between devices: 2.8 us -> 0.01 us  [over_y(): lax.ppermute(array, 'col', [(i, (i + 4 * k) % 16) for i in range(16)])]
    pallas_call x0 -> x1, Pallas kernels: none -> 1.57 us  [hold(): pl.pallas_call(hold_kernel, out_shape=jax.ShapeDtypeStruct(array.shape, a...]
    ppermute x1, waiting for transfers between devices: 2.78 us -> 3.89 us  [over_x_hi_x(): lax.ppermute(array, ('row', 'col'), [(i, i ^ 4 * 16 + 2) for i in range(1...]
  transfers between devices with their start and end apart: 22 -> 22, of which waited for: 15 -> 12; matrix products, arithmetic and copies ran while one was open for 3% -> 5% of each run, Pallas kernels for 0% -> 2%
where the time goes in v5:
time: 92.2 us; the launch traced here: 91.9 us
  starting transfers between devices  41.8 us (45%)
  waiting for transfers between devices  37.6 us (41%)
  Pallas kernels  5.84 us (6%)
  other arithmetic  3.29 us (4%)
  local copies, waits for them, and re-layouts  2.41 us (3%)
  between operations  1.03 us (1%)
    all_to_all x1, waiting for transfers between devices, per_device(): arrived = lax.all_to_all(weight, 'col', 0, 0, tiled=True)  20.8 us
    ppermute x6, starting transfers between devices, over_core(): return lax.ppermute(array, 'col', [(i, i ^ 1) for i in range(16)])  10.9 us
    ppermute x6, starting transfers between devices, over_z(): lax.ppermute(array, 'row', [(i, i // 4 * 4 + (i + k) % 4) for i in range(...  9.53 us
    all_to_all x1, starting transfers between devices, per_device(): arrived = lax.all_to_all(weight, 'col', 0, 0, tiled=True)  7.52 us
    ppermute x6, waiting for transfers between devices, over_z(): lax.ppermute(array, 'row', [(i, i // 4 * 4 + (i + k) % 4) for i in range(...  7.45 us
    pallas_call x1, Pallas kernels, merge(): pl.pallas_call(merge_kernel, in_specs=[pl.BlockSpec(memory_space=pltpu.VM...  4.28 us
    ppermute x2, starting transfers between devices, over_col(): return lax.ppermute(array, 'col', [(i, i ^ mask) for i in range(16)])  4.19 us
    ppermute x1, waiting for transfers between devices, over_x_hi_x(): lax.ppermute(array, ('row', 'col'), [(i, i ^ 4 * 16 + 2) for i in range(1...  3.89 us
  transfers between devices with their start and end apart: 22, of which 12 were waited for; matrix products, arithmetic and copies ran while one was open for 5% of the time, Pallas kernels for 2%

profile of v5, /device:TPU:1, one launch (start us, length us, event | category | flops | bytes accessed | tf_op | source)
XLA Modules:
  0.0 91.9 jit_solution(1978994249393773307)
XLA Ops:
  0.7 1.2 %reshape.35 = f32[4,2,2,4,2048]{4,3,2,1,0:T(4,128)S(1)} reshape(f32[1,64,2048]{2,1,0:T(8,128)} %param.17) | data formatting | bytes 1048576 | tf_op jit(solution)/shard_map/reshape | solution.py:203
  2.0 1.5 %collective-permute-start = (f32[4,2,4,2048]{3,2,0,1:T(4,128)S(1)}, f32[4,2,4,2048]{3,2,0,1:T(4,128)S(1)}, u32[]{:S(2)}, u32[]{:S(2)}) collective-permute-start(f32[4,2,4,2048]{3,2,0,1:T(4,128)S(1)} %get-tuple-element.22), channel_id=1, source_target_pairs={{0,1},{1,0},{2,3},{3,2},{4,5},{5,4},{6,7},{7,6},{8,9},{9,8},{10,11... | collective-permute-start | bytes 786440 | tf_op jit(solution)/shard_map/ppermute | solution.py:149
  3.5 1.0 %dynamic-slice_bitcast_fusion.1 = (f32[2,8,1024]{2,1,0:T(8,128)S(1)}, f32[2,8,1024]{2,1,0:T(8,128)S(1)}, f32[2,8,1024]{2,1,0:T(8,128)S(1)}, f32[2,8,1024]{2,1,0:T(8,128)S(1)}) fusion(f32[2,4,8,1024]{3,2,1,0:T(8,128)} %bitcast.80, s32[]{:T(128)S(6)} %select_n.128, s32[]{:T(128)S(6)} %select_n.126, s32[]{:T(128)S(6)} %select_n.124, s32[]{:T(128)S(6)} %select_n.122), kind=kLoop, calls=%fused_computation.9 | loop fusion | bytes 524304 | tf_op jit(solution)/shard_map/jit(dynamic_index_in_dim)/squeeze | solution.py:145
  4.5 0.2 collective-permute-done
  4.7 0.1 add.182
  4.8 1.4 %collective-permute-start.1 = (f32[4,4,2048]{2,1,0:T(4,128)S(1)}, f32[4,4,2048]{2,1,0:T(4,128)S(1)}, u32[]{:S(2)}, u32[]{:S(2)}) collective-permute-start(f32[4,4,2048]{2,1,0:T(4,128)S(1)} %dynamic-slice_bitcast_fusion), channel_id=1, source_target_pairs={{0,2},{1,3},{2,0},{3,1},{4,6},{5,7},{6,4},{7,5},{8,10},{9,11},{10,... | collective-permute-start | bytes 393224 | tf_op jit(solution)/shard_map/ppermute | solution.py:153
  6.2 1.6 %collective-permute-start.5 = (f32[2,8,1024]{2,1,0:T(8,128)S(1)}, f32[2,8,1024]{2,1,0:T(8,128)S(1)}, u32[]{:S(2)}, u32[]{:S(2)}) collective-permute-start(f32[2,8,1024]{2,1,0:T(8,128)S(1)} %get-tuple-element.28), channel_id=1, source_target_pairs={{0,16},{16,32},{32,48},{48,0},{64,80},{80,96},{96,112},{112,64},{1... | collective-permute-start | bytes 196616 | tf_op jit(solution)/shard_map/ppermute | solution.py:185
  7.8 3.3 %collective-permute-start.6 = (f32[2,8,1024]{2,1,0:T(8,128)S(1)}, f32[2,8,1024]{2,1,0:T(8,128)S(1)}, u32[]{:S(2)}, u32[]{:S(2)}) collective-permute-start(f32[2,8,1024]{2,1,0:T(8,128)S(1)} %get-tuple-element.29), channel_id=1, source_target_pairs={{0,32},{16,48},{32,0},{48,16},{64,96},{80,112},{96,64},{112,80},{1... | collective-permute-start | bytes 196616 | tf_op jit(solution)/shard_map/ppermute | solution.py:185
  11.1 0.7 collective-permute-start.7
  11.8 0.0 collective-permute-done.1
  11.9 1.4 %collective-permute-start.2 = (f32[2,4,2048]{2,1,0:T(4,128)S(1)}, f32[2,4,2048]{2,1,0:T(4,128)S(1)}, u32[]{:S(2)}, u32[]{:S(2)}) collective-permute-start(f32[2,4,2048]{2,1,0:T(4,128)S(1)} %pad_maximum_fusion.2), channel_id=1, source_target_pairs={{0,4},{1,5},{2,6},{3,7},{4,0},{5,1},{6,2},{7,3},{8,12},{9,13},{10,... | collective-permute-start | bytes 196616 | tf_op jit(solution)/shard_map/ppermute | solution.py:165
  13.3 0.0 collective-permute-done.5
  13.3 0.4 collective-permute-done.6
  13.7 0.8 collective-permute-done.7
  14.5 0.6 collective-permute-done.2
  15.2 2.8 %collective-permute-start.3 = (f32[4,2048]{1,0:T(4,128)S(1)}, f32[4,2048]{1,0:T(4,128)S(1)}, u32[]{:S(2)}, u32[]{:S(2)}) collective-permute-start(f32[4,2048]{1,0:T(4,128)S(1)} %slice_bitcast_fusion.3), channel_id=1, source_target_pairs={{0,12},{1,13},{2,14},{3,15},{4,8},{5,9},{6,10},{7,11},{8,4},{9,5},... | collective-permute-start | bytes 98312 | tf_op jit(solution)/shard_map/ppermute | solution.py:165
  18.0 2.5 %collective-permute-start.8 = (f32[8,1024]{1,0:T(8,128)S(1)}, f32[8,1024]{1,0:T(8,128)S(1)}, u32[]{:S(2)}, u32[]{:S(2)}) collective-permute-start(f32[8,1024]{1,0:T(8,128)S(1)} %dynamic-slice_bitcast_fusion.5), channel_id=1, source_target_pairs={{0,64},{16,80},{32,96},{48,112},{64,0},{80,16},{96,32},{112,48},{1... | collective-permute-start | bytes 98312 | tf_op jit(solution)/shard_map/ppermute | solution.py:177
  20.5 0.1 multiply_subtract_fusion.2
  20.7 3.3 %collective-permute-start.4 = (bf16[4,2,4,128]{3,2,1,0:T(4,128)(2,1)S(1)}, bf16[4,2,4,128]{3,2,1,0:T(4,128)(2,1)S(1)}, u32[]{:S(2)}, u32[]{:S(2)}) collective-permute-start(bf16[4,2,4,128]{3,2,1,0:T(4,128)(2,1)S(1)} %bitcast.87), channel_id=1, source_target_pairs={{0,1},{1,0},{2,3},{3,2},{4,5},{5,4},{6,7},{7,6},{8,9},{9,8},{10,11... | collective-permute-start | bytes 24584 | tf_op jit(solution)/shard_map/ppermute | solution.py:149
  24.0 0.7 collective-permute-done.4
  24.8 0.1 collective-permute-start.9
  24.9 2.6 %collective-permute-done.9 = bf16[8,1536]{1,0:T(8,128)(2,1)S(1)} collective-permute-done((bf16[8,1536]{1,0:T(8,128)(2,1)S(1)}, bf16[8,1536]{1,0:T(8,128)(2,1)S(1)}, u32[]{:S(2)}, u32[]{:S(2)}) %collective-permute-start.9) | collective-permute-done | bytes 24608 | tf_op jit(solution)/shard_map/ppermute | solution.py:153
  27.6 2.2 %collective-permute-start.12 = (bf16[2,8,1152]{2,1,0:T(8,128)(2,1)S(1)}, bf16[2,8,1152]{2,1,0:T(8,128)(2,1)S(1)}, u32[]{:S(2)}, u32[]{:S(2)}) collective-permute-start(bf16[2,8,1152]{2,1,0:T(8,128)(2,1)S(1)} %get-tuple-element.57), channel_id=1, source_target_pairs={{0,12},{1,13},{2,14},{3,15},{4,0},{5,1},{6,2},{7,3},{8,4},{9,5},{1... | collective-permute-start | bytes 110600 | tf_op jit(solution)/shard_map/ppermute | solution.py:157
  29.8 0.7 collective-permute-start.10
  30.4 7.5 %all-to-all-start = ((bf16[16,128,1024]{2,1,0:T(8,128)(2,1)}), bf16[16,128,1024]{2,1,0:T(8,128)(2,1)}, u32[]{:S(2)}, u32[]{:S(2)}) async-start(bf16[16,128,1024]{2,1,0:T(8,128)(2,1)} %bitcast.79), calls=%async_computation | async-start | bytes 8388608 | tf_op jit(solution)/shard_map/all_to_all | solution.py:231
  38.0 0.7 multiply_subtract_fusion
  38.6 0.7 multiply_subtract_fusion.1
  39.3 0.0 collective-permute-done.10
  39.3 0.7 pad_maximum_fusion.1.array_ref
  40.0 1.6 %shard_map.144 = bf16[4,2,8,1024]{3,2,1,0:T(8,128)(2,1)} custom-call(bf16[4,2,8,1024]{3,2,1,0:T(8,128)(2,1)} %pad_maximum_fusion.1.array_ref), custom_call_target="tpu_custom_call" | custom-call | flops 99999997952 | bytes 262144 | tf_op jit(solution)/shard_map/pallas_call | solution.py:137
  41.6 2.9 %collective-permute-start.13 = (bf16[4,2,8,1024]{3,2,1,0:T(8,128)(2,1)}, bf16[4,2,8,1024]{3,2,1,0:T(8,128)(2,1)S(1)}, u32[]{:S(2)}, u32[]{:S(2)}) collective-permute-start(bf16[4,2,8,1024]{3,2,1,0:T(8,128)(2,1)} %shard_map.144), channel_id=1, source_target_pairs={{0,66},{1,67},{2,64},{3,65},{4,70},{5,71},{6,68},{7,69},{8,74},{9,... | collective-permute-start | bytes 393224 | tf_op jit(solution)/shard_map/ppermute | solution.py:181
  44.5 3.9 %collective-permute-done.13 = bf16[4,2,8,1024]{3,2,1,0:T(8,128)(2,1)S(1)} collective-permute-done((bf16[4,2,8,1024]{3,2,1,0:T(8,128)(2,1)}, bf16[4,2,8,1024]{3,2,1,0:T(8,128)(2,1)S(1)}, u32[]{:S(2)}, u32[]{:S(2)}) %collective-permute-start.13) | collective-permute-done | bytes 131104 | tf_op jit(solution)/shard_map/ppermute | solution.py:181
  48.4 0.9 %pad_maximum_fusion.refs_0_ = bf16[2,4,2,8,1024]{4,3,2,1,0:T(8,128)(2,1)S(1)} fusion(bf16[1,4,2,8,1024]{4,3,2,1,0:T(8,128)(2,1)S(1)} %bitcast.84, bf16[1,4,2,8,1024]{4,3,2,1,0:T(8,128)(2,1)} %bitcast.83), kind=kLoop, calls=%fused_computation | loop fusion | flops 131072 | bytes 524288 | tf_op jit(solution)/shard_map/stack | solution.py:235
  49.3 0.8 collective-permute-start.14
  50.1 2.3 %collective-permute-start.15 = (bf16[2,4,2,8,1024]{4,3,2,1,0:T(8,128)(2,1)S(1)}, bf16[2,4,2,8,1024]{4,3,2,1,0:T(8,128)(2,1)S(1)}, u32[]{:S(2)}, u32[]{:S(2)}) collective-permute-start(bf16[2,4,2,8,1024]{4,3,2,1,0:T(8,128)(2,1)S(1)} %pad_maximum_fusion.refs_0_), channel_id=1, source_target_pairs={{0,32},{16,48},{32,0},{48,16},{64,96},{80,112},{96,64},{112,80},{1... | collective-permute-start | bytes 786440 | tf_op jit(solution)/shard_map/ppermute | solution.py:185
  52.5 0.7 collective-permute-start.16
  53.2 1.7 %collective-permute-start.17 = (bf16[2,4,2,8,1024]{4,3,2,1,0:T(8,128)(2,1)S(1)}, bf16[2,4,2,8,1024]{4,3,2,1,0:T(8,128)(2,1)S(1)}, u32[]{:S(2)}, u32[]{:S(2)}) collective-permute-start(bf16[2,4,2,8,1024]{4,3,2,1,0:T(8,128)(2,1)S(1)} %pad_maximum_fusion.refs_0_), channel_id=1, source_target_pairs={{0,1},{1,0},{2,3},{3,2},{4,5},{5,4},{6,7},{7,6},{8,9},{9,8},{10,11... | collective-permute-start | bytes 786440 | tf_op jit(solution)/shard_map/ppermute | solution.py:149
  54.9 2.9 %collective-permute-done.14.refs_1_ = bf16[2,4,2,8,1024]{4,3,2,1,0:T(8,128)(2,1)S(1)} collective-permute-done((bf16[2,4,2,8,1024]{4,3,2,1,0:T(8,128)(2,1)S(1)}, bf16[2,4,2,8,1024]{4,3,2,1,0:T(8,128)(2,1)S(1)}, u32[]{:S(2)}, u32[]{:S(2)}) %collective-permute-start.14) | collective-permute-done | bytes 262176 | tf_op jit(solution)/shard_map/ppermute | solution.py:185
  57.8 2.5 %collective-permute-start.18 = (bf16[2,4,2,8,1024]{4,3,2,1,0:T(8,128)(2,1)S(1)}, bf16[2,4,2,8,1024]{4,3,2,1,0:T(8,128)(2,1)S(1)}, u32[]{:S(2)}, u32[]{:S(2)}) collective-permute-start(bf16[2,4,2,8,1024]{4,3,2,1,0:T(8,128)(2,1)S(1)} %collective-permute-done.14.refs_1_), channel_id=1, source_target_pairs={{0,1},{1,0},{2,3},{3,2},{4,5},{5,4},{6,7},{7,6},{8,9},{9,8},{10,11... | collective-permute-start | bytes 786440 | tf_op jit(solution)/shard_map/ppermute | solution.py:149
  60.3 3.4 %collective-permute-done.15.refs_2_ = bf16[2,4,2,8,1024]{4,3,2,1,0:T(8,128)(2,1)S(1)} collective-permute-done((bf16[2,4,2,8,1024]{4,3,2,1,0:T(8,128)(2,1)S(1)}, bf16[2,4,2,8,1024]{4,3,2,1,0:T(8,128)(2,1)S(1)}, u32[]{:S(2)}, u32[]{:S(2)}) %collective-permute-start.15) | collective-permute-done | bytes 262176 | tf_op jit(solution)/shard_map/ppermute | solution.py:185
  63.7 1.7 %collective-permute-start.19 = (bf16[2,4,2,8,1024]{4,3,2,1,0:T(8,128)(2,1)S(1)}, bf16[2,4,2,8,1024]{4,3,2,1,0:T(8,128)(2,1)S(1)}, u32[]{:S(2)}, u32[]{:S(2)}) collective-permute-start(bf16[2,4,2,8,1024]{4,3,2,1,0:T(8,128)(2,1)S(1)} %collective-permute-done.15.refs_2_), channel_id=1, source_target_pairs={{0,1},{1,0},{2,3},{3,2},{4,5},{5,4},{6,7},{7,6},{8,9},{9,8},{10,11... | collective-permute-start | bytes 786440 | tf_op jit(solution)/shard_map/ppermute | solution.py:149
  65.3 0.0 collective-permute-done.16.refs_3_
  65.3 0.2 collective-permute-start.20
  65.6 0.0 collective-permute-done.17.refs_4_
  65.6 0.9 collective-permute-done.19.refs_6_
  66.5 0.4 collective-permute-done.20.refs_7_
  66.9 20.8 %all-to-all-done.refs_8_ = bf16[16,128,1024]{2,1,0:T(8,128)(2,1)} async-done(((bf16[16,128,1024]{2,1,0:T(8,128)(2,1)}), bf16[16,128,1024]{2,1,0:T(8,128)(2,1)}, u32[]{:S(2)}, u32[]{:S(2)}) %all-to-all-start) | async-done | bytes 4194336 | tf_op jit(solution)/shard_map/all_to_all | solution.py:231
  87.6 4.3 %shard_map.145 = bf16[8,128,2048]{2,1,0:T(8,128)(2,1)} custom-call(f32[64,128]{1,0:T(8,128)S(1)} %bitcast_convert_fusion.bt_ref, bf16[2,4,2,8,1024]{4,3,2,1,0:T(8,128)(2,1)S(1)} %pad_maximum_fusion.refs_0_, bf16[2,4,2,8,1024]{4,3,2,1,0:T(8,128)(2,1)S(1)} %collective-permute-done.14.refs_1_, bf16[2,4,2,8,1024]{4,3,2,1,0:T(8,128)(2,1)S(1)} %collective-permute-done.15.refs_2_, ...), custom_call_target="tpu_custom_call" | custom-call | flops 268435456 | bytes 10485760 | tf_op jit(solution)/shard_map/pallas_call | solution.py:112
  (48 shorter events, 0.5 us)
Async XLA Ops:
  0.6 19.8 %copy-start = (f32[4,2048]{1,0:T(4,128)S(1)}, f32[4,2048]{1,0:T(4,128)}, u32[]{:S(2)}) copy-start(f32[4,2048]{1,0:T(4,128)} %param.13) | copy-start | bytes 98308
  0.6 19.8 %copy-start.2 = (f32[4,2048]{1,0:T(4,128)S(1)}, f32[4,2048]{1,0:T(4,128)}, u32[]{:S(2)}) copy-start(f32[4,2048]{1,0:T(4,128)} %param.14) | copy-start | bytes 98308
  0.7 19.8 %copy-start.1 = (f32[4,2048]{1,0:T(4,128)S(1)}, f32[4,2048]{1,0:T(4,128)}, u32[]{:S(2)}) copy-start(f32[4,2048]{1,0:T(4,128)} %param.15) | copy-start | bytes 98308
  0.7 23.3 %copy-start.3 = (f32[8,1024]{1,0:T(8,128)S(1)}, f32[8,1024]{1,0:T(8,128)}, u32[]{:S(2)}) copy-start(f32[8,1024]{1,0:T(8,128)} %param.10) | copy-start | bytes 98308
  0.7 23.2 %copy-start.5 = (f32[8,1024]{1,0:T(8,128)S(1)}, f32[8,1024]{1,0:T(8,128)}, u32[]{:S(2)}) copy-start(f32[8,1024]{1,0:T(8,128)} %param.11) | copy-start | bytes 98308
  0.7 23.2 %copy-start.4 = (f32[8,1024]{1,0:T(8,128)S(1)}, f32[8,1024]{1,0:T(8,128)}, u32[]{:S(2)}) copy-start(f32[8,1024]{1,0:T(8,128)} %param.12) | copy-start | bytes 98308
  2.0 2.7 %collective-permute-start = (f32[4,2,4,2048]{3,2,0,1:T(4,128)S(1)}, f32[4,2,4,2048]{3,2,0,1:T(4,128)S(1)}, u32[]{:S(2)}, u32[]{:S(2)}) collective-permute-start(f32[4,2,4,2048]{3,2,0,1:T(4,128)S(1)} %get-tuple-element.22), channel_id=1, source_target_pairs={{0,1},{1,0},{2,3},{3,2},{4,5},{5,4},{6,7},{7,6},{8,9},{9,8},{10,11... | collective-permute-start | bytes 786440 | tf_op jit(solution)/shard_map/ppermute | solution.py:149
  4.8 7.0 %collective-permute-start.1 = (f32[4,4,2048]{2,1,0:T(4,128)S(1)}, f32[4,4,2048]{2,1,0:T(4,128)S(1)}, u32[]{:S(2)}, u32[]{:S(2)}) collective-permute-start(f32[4,4,2048]{2,1,0:T(4,128)S(1)} %dynamic-slice_bitcast_fusion), channel_id=1, source_target_pairs={{0,2},{1,3},{2,0},{3,1},{4,6},{5,7},{6,4},{7,5},{8,10},{9,11},{10,... | collective-permute-start | bytes 393224 | tf_op jit(solution)/shard_map/ppermute | solution.py:153
  6.2 7.1 %collective-permute-start.5 = (f32[2,8,1024]{2,1,0:T(8,128)S(1)}, f32[2,8,1024]{2,1,0:T(8,128)S(1)}, u32[]{:S(2)}, u32[]{:S(2)}) collective-permute-start(f32[2,8,1024]{2,1,0:T(8,128)S(1)} %get-tuple-element.28), channel_id=1, source_target_pairs={{0,16},{16,32},{32,48},{48,0},{64,80},{80,96},{96,112},{112,64},{1... | collective-permute-start | bytes 196616 | tf_op jit(solution)/shard_map/ppermute | solution.py:185
  7.8 5.9 %collective-permute-start.6 = (f32[2,8,1024]{2,1,0:T(8,128)S(1)}, f32[2,8,1024]{2,1,0:T(8,128)S(1)}, u32[]{:S(2)}, u32[]{:S(2)}) collective-permute-start(f32[2,8,1024]{2,1,0:T(8,128)S(1)} %get-tuple-element.29), channel_id=1, source_target_pairs={{0,32},{16,48},{32,0},{48,16},{64,96},{80,112},{96,64},{112,80},{1... | collective-permute-start | bytes 196616 | tf_op jit(solution)/shard_map/ppermute | solution.py:185
  11.1 3.4 %collective-permute-start.7 = (f32[2,8,1024]{2,1,0:T(8,128)S(1)}, f32[2,8,1024]{2,1,0:T(8,128)S(1)}, u32[]{:S(2)}, u32[]{:S(2)}) collective-permute-start(f32[2,8,1024]{2,1,0:T(8,128)S(1)} %get-tuple-element.30), channel_id=1, source_target_pairs={{0,48},{16,0},{32,16},{48,32},{64,112},{80,64},{96,80},{112,96},{1... | collective-permute-start | bytes 196616 | tf_op jit(solution)/shard_map/ppermute | solution.py:185
  11.9 3.2 %collective-permute-start.2 = (f32[2,4,2048]{2,1,0:T(4,128)S(1)}, f32[2,4,2048]{2,1,0:T(4,128)S(1)}, u32[]{:S(2)}, u32[]{:S(2)}) collective-permute-start(f32[2,4,2048]{2,1,0:T(4,128)S(1)} %pad_maximum_fusion.2), channel_id=1, source_target_pairs={{0,4},{1,5},{2,6},{3,7},{4,0},{5,1},{6,2},{7,3},{8,12},{9,13},{10,... | collective-permute-start | bytes 196616 | tf_op jit(solution)/shard_map/ppermute | solution.py:165
  15.2 5.3 %collective-permute-start.3 = (f32[4,2048]{1,0:T(4,128)S(1)}, f32[4,2048]{1,0:T(4,128)S(1)}, u32[]{:S(2)}, u32[]{:S(2)}) collective-permute-start(f32[4,2048]{1,0:T(4,128)S(1)} %slice_bitcast_fusion.3), channel_id=1, source_target_pairs={{0,12},{1,13},{2,14},{3,15},{4,8},{5,9},{6,10},{7,11},{8,4},{9,5},... | collective-permute-start | bytes 98312 | tf_op jit(solution)/shard_map/ppermute | solution.py:165
  18.0 5.9 %collective-permute-start.8 = (f32[8,1024]{1,0:T(8,128)S(1)}, f32[8,1024]{1,0:T(8,128)S(1)}, u32[]{:S(2)}, u32[]{:S(2)}) collective-permute-start(f32[8,1024]{1,0:T(8,128)S(1)} %dynamic-slice_bitcast_fusion.5), channel_id=1, source_target_pairs={{0,64},{16,80},{32,96},{48,112},{64,0},{80,16},{96,32},{112,48},{1... | collective-permute-start | bytes 98312 | tf_op jit(solution)/shard_map/ppermute | solution.py:177
  20.7 4.1 %collective-permute-start.4 = (bf16[4,2,4,128]{3,2,1,0:T(4,128)(2,1)S(1)}, bf16[4,2,4,128]{3,2,1,0:T(4,128)(2,1)S(1)}, u32[]{:S(2)}, u32[]{:S(2)}) collective-permute-start(bf16[4,2,4,128]{3,2,1,0:T(4,128)(2,1)S(1)} %bitcast.87), channel_id=1, source_target_pairs={{0,1},{1,0},{2,3},{3,2},{4,5},{5,4},{6,7},{7,6},{8,9},{9,8},{10,11... | collective-permute-start | bytes 24584 | tf_op jit(solution)/shard_map/ppermute | solution.py:149
  24.8 2.8 %collective-permute-start.9 = (bf16[8,1536]{1,0:T(8,128)(2,1)S(1)}, bf16[8,1536]{1,0:T(8,128)(2,1)S(1)}, u32[]{:S(2)}, u32[]{:S(2)}) collective-permute-start(bf16[8,1536]{1,0:T(8,128)(2,1)S(1)} %pad_maximum_fusion.8), channel_id=1, source_target_pairs={{0,2},{1,3},{2,0},{3,1},{4,6},{5,7},{6,4},{7,5},{8,10},{9,11},{10,... | collective-permute-start | bytes 73736 | tf_op jit(solution)/shard_map/ppermute | solution.py:153
  27.6 11.7 %collective-permute-start.12 = (bf16[2,8,1152]{2,1,0:T(8,128)(2,1)S(1)}, bf16[2,8,1152]{2,1,0:T(8,128)(2,1)S(1)}, u32[]{:S(2)}, u32[]{:S(2)}) collective-permute-start(bf16[2,8,1152]{2,1,0:T(8,128)(2,1)S(1)} %get-tuple-element.57), channel_id=1, source_target_pairs={{0,12},{1,13},{2,14},{3,15},{4,0},{5,1},{6,2},{7,3},{8,4},{9,5},{1... | collective-permute-start | bytes 110600 | tf_op jit(solution)/shard_map/ppermute | solution.py:157
  29.8 9.5 %collective-permute-start.11 = (bf16[2,8,1152]{2,1,0:T(8,128)(2,1)S(1)}, bf16[2,8,1152]{2,1,0:T(8,128)(2,1)S(1)}, u32[]{:S(2)}, u32[]{:S(2)}) collective-permute-start(bf16[2,8,1152]{2,1,0:T(8,128)(2,1)S(1)} %get-tuple-element.56), channel_id=1, source_target_pairs={{0,8},{1,9},{2,10},{3,11},{4,12},{5,13},{6,14},{7,15},{8,0},{9,1},... | collective-permute-start | bytes 110600 | tf_op jit(solution)/shard_map/ppermute | solution.py:157
  29.8 9.5 %collective-permute-start.10 = (bf16[2,8,1152]{2,1,0:T(8,128)(2,1)S(1)}, bf16[2,8,1152]{2,1,0:T(8,128)(2,1)S(1)}, u32[]{:S(2)}, u32[]{:S(2)}) collective-permute-start(bf16[2,8,1152]{2,1,0:T(8,128)(2,1)S(1)} %get-tuple-element.55), channel_id=1, source_target_pairs={{0,4},{1,5},{2,6},{3,7},{4,8},{5,9},{6,10},{7,11},{8,12},{9,13},{1... | collective-permute-start | bytes 110600 | tf_op jit(solution)/shard_map/ppermute | solution.py:157
  30.4 57.2 %all-to-all-start = ((bf16[16,128,1024]{2,1,0:T(8,128)(2,1)}), bf16[16,128,1024]{2,1,0:T(8,128)(2,1)}, u32[]{:S(2)}, u32[]{:S(2)}) async-start(bf16[16,128,1024]{2,1,0:T(8,128)(2,1)} %bitcast.79), calls=%async_computation | async-start | bytes 8388608 | tf_op jit(solution)/shard_map/all_to_all | solution.py:231
  41.6 6.8 %collective-permute-start.13 = (bf16[4,2,8,1024]{3,2,1,0:T(8,128)(2,1)}, bf16[4,2,8,1024]{3,2,1,0:T(8,128)(2,1)S(1)}, u32[]{:S(2)}, u32[]{:S(2)}) collective-permute-start(bf16[4,2,8,1024]{3,2,1,0:T(8,128)(2,1)} %shard_map.144), channel_id=1, source_target_pairs={{0,66},{1,67},{2,64},{3,65},{4,70},{5,71},{6,68},{7,69},{8,74},{9,... | collective-permute-start | bytes 393224 | tf_op jit(solution)/shard_map/ppermute | solution.py:181
  49.3 8.5 %collective-permute-start.14 = (bf16[2,4,2,8,1024]{4,3,2,1,0:T(8,128)(2,1)S(1)}, bf16[2,4,2,8,1024]{4,3,2,1,0:T(8,128)(2,1)S(1)}, u32[]{:S(2)}, u32[]{:S(2)}) collective-permute-start(bf16[2,4,2,8,1024]{4,3,2,1,0:T(8,128)(2,1)S(1)} %pad_maximum_fusion.refs_0_), channel_id=1, source_target_pairs={{0,16},{16,32},{32,48},{48,0},{64,80},{80,96},{96,112},{112,64},{1... | collective-permute-start | bytes 786440 | tf_op jit(solution)/shard_map/ppermute | solution.py:185
  50.1 13.5 %collective-permute-start.15 = (bf16[2,4,2,8,1024]{4,3,2,1,0:T(8,128)(2,1)S(1)}, bf16[2,4,2,8,1024]{4,3,2,1,0:T(8,128)(2,1)S(1)}, u32[]{:S(2)}, u32[]{:S(2)}) collective-permute-start(bf16[2,4,2,8,1024]{4,3,2,1,0:T(8,128)(2,1)S(1)} %pad_maximum_fusion.refs_0_), channel_id=1, source_target_pairs={{0,32},{16,48},{32,0},{48,16},{64,96},{80,112},{96,64},{112,80},{1... | collective-permute-start | bytes 786440 | tf_op jit(solution)/shard_map/ppermute | solution.py:185
  52.5 12.9 %collective-permute-start.16 = (bf16[2,4,2,8,1024]{4,3,2,1,0:T(8,128)(2,1)S(1)}, bf16[2,4,2,8,1024]{4,3,2,1,0:T(8,128)(2,1)S(1)}, u32[]{:S(2)}, u32[]{:S(2)}) collective-permute-start(bf16[2,4,2,8,1024]{4,3,2,1,0:T(8,128)(2,1)S(1)} %pad_maximum_fusion.refs_0_), channel_id=1, source_target_pairs={{0,48},{16,0},{32,16},{48,32},{64,112},{80,64},{96,80},{112,96},{1... | collective-permute-start | bytes 786440 | tf_op jit(solution)/shard_map/ppermute | solution.py:185
  53.2 12.4 %collective-permute-start.17 = (bf16[2,4,2,8,1024]{4,3,2,1,0:T(8,128)(2,1)S(1)}, bf16[2,4,2,8,1024]{4,3,2,1,0:T(8,128)(2,1)S(1)}, u32[]{:S(2)}, u32[]{:S(2)}) collective-permute-start(bf16[2,4,2,8,1024]{4,3,2,1,0:T(8,128)(2,1)S(1)} %pad_maximum_fusion.refs_0_), channel_id=1, source_target_pairs={{0,1},{1,0},{2,3},{3,2},{4,5},{5,4},{6,7},{7,6},{8,9},{9,8},{10,11... | collective-permute-start | bytes 786440 | tf_op jit(solution)/shard_map/ppermute | solution.py:149
  57.8 7.8 %collective-permute-start.18 = (bf16[2,4,2,8,1024]{4,3,2,1,0:T(8,128)(2,1)S(1)}, bf16[2,4,2,8,1024]{4,3,2,1,0:T(8,128)(2,1)S(1)}, u32[]{:S(2)}, u32[]{:S(2)}) collective-permute-start(bf16[2,4,2,8,1024]{4,3,2,1,0:T(8,128)(2,1)S(1)} %collective-permute-done.14.refs_1_), channel_id=1, source_target_pairs={{0,1},{1,0},{2,3},{3,2},{4,5},{5,4},{6,7},{7,6},{8,9},{9,8},{10,11... | collective-permute-start | bytes 786440 | tf_op jit(solution)/shard_map/ppermute | solution.py:149
  63.7 2.8 %collective-permute-start.19 = (bf16[2,4,2,8,1024]{4,3,2,1,0:T(8,128)(2,1)S(1)}, bf16[2,4,2,8,1024]{4,3,2,1,0:T(8,128)(2,1)S(1)}, u32[]{:S(2)}, u32[]{:S(2)}) collective-permute-start(bf16[2,4,2,8,1024]{4,3,2,1,0:T(8,128)(2,1)S(1)} %collective-permute-done.15.refs_2_), channel_id=1, source_target_pairs={{0,1},{1,0},{2,3},{3,2},{4,5},{5,4},{6,7},{7,6},{8,9},{9,8},{10,11... | collective-permute-start | bytes 786440 | tf_op jit(solution)/shard_map/ppermute | solution.py:149
  65.3 1.5 %collective-permute-start.20 = (bf16[2,4,2,8,1024]{4,3,2,1,0:T(8,128)(2,1)S(1)}, bf16[2,4,2,8,1024]{4,3,2,1,0:T(8,128)(2,1)S(1)}, u32[]{:S(2)}, u32[]{:S(2)}) collective-permute-start(bf16[2,4,2,8,1024]{4,3,2,1,0:T(8,128)(2,1)S(1)} %collective-permute-done.16.refs_3_), channel_id=1, source_target_pairs={{0,1},{1,0},{2,3},{3,2},{4,5},{5,4},{6,7},{7,6},{8,9},{9,8},{10,11... | collective-permute-start | bytes 786440 | tf_op jit(solution)/shard_map/ppermute | solution.py:149

commit v6 on v5

--- a/solution.py
+++ b/solution.py
@@ -90,12 +90,7 @@
         for s in group:
             k_core, k_y, k_x = s // 8, (s // 2) % 4, s % 2
             a_block = jnp.concatenate(
-                [
-                    a_buf[4 * k_core + k_z, k_x_hi, k_y, k_x ^ k_x_hi]
-                    for k_z in range(4)
-                    for k_x_hi in range(2)
-                ],
-                axis=0,
+                [a_buf[4 * k_core + k_z, k_y, k_x] for k_z in range(4)], axis=0
             )
             increment = lax.dot_general(
                 left, a_block, (((1,), (0,)), ((), ())), preferred_element_type=jnp.float32
@@ -115,14 +110,14 @@
         out_specs=pl.BlockSpec(memory_space=pl.ANY),
         out_shape=jax.ShapeDtypeStruct((8, 128, 2048), jnp.bfloat16),
         scratch_shapes=[
-            pltpu.VMEM((8, 2, 4, 2, 8, 1024), jnp.bfloat16),
+            pltpu.VMEM((8, 4, 2, 16, 1024), jnp.bfloat16),
             pltpu.VMEM((16, 128, 1024), jnp.bfloat16),
             pltpu.VMEM((16, 128, 1024), jnp.bfloat16),
             pltpu.SemaphoreType.DMA((8,)),
             pltpu.SemaphoreType.DMA((16,)),
             pltpu.SemaphoreType.DMA((16,)),
         ],
-        compiler_params=pltpu.CompilerParams(vmem_limit_bytes=32 << 20),
+        compiler_params=pltpu.CompilerParams(vmem_limit_bytes=16 << 20),
         cost_estimate=pl.CostEstimate(
             flops=2 * 128 * 64 * 16384, bytes_accessed=10 << 20, transcendentals=0
         ),
@@ -208,9 +203,9 @@
     bt_part, *sent = lax.optimization_barrier((bt_part, *sent))
     part = kept + sum(over_z(array, k) for array, k in zip(sent, (1, 2, 3)))
     grad_a = pick(part, x_hi, 0) + over_x_hi(pick(part, 1 - x_hi, 0))
-    bt_part = pick(bt_part, x, 1) + over_x(pick(bt_part, 1 - x, 1))
-    bt_part = two_of(bt_part, y, y ^ 3, 0) + over_col(two_of(bt_part, y ^ 1, y ^ 2, 0), 4)
-    grad_bt = bt_part[0] + over_col(bt_part[1], 12)
+    bt_part = two_of(bt_part, y, y ^ 1, 0) + over_col(two_of(bt_part, y ^ 3, y ^ 2, 0), 12)
+    bt_part = bt_part[0] + over_col(bt_part[1], 4)
+    grad_bt = pick(bt_part, x, 0) + over_x(pick(bt_part, 1 - x, 0))
 
     a_new = adam_step(a_master, a_first, a_second, grad_a)[0]
     bt_new = adam_step(bt_master, bt_first, bt_second, grad_bt)[0]
@@ -231,8 +226,8 @@
     arrived = lax.all_to_all(weight, "col", 0, 0, tiled=True)
     part = jnp.stack([a_near] + [came[:, :, :1024] for came in along_y])
     bt_rows = jnp.stack([pick(bt_near, y, 0)] + [came[:, :, 1024:] for came in along_y])
-    part = hold(part)
-    part = jnp.stack([part, over_x_hi_x(part)])
+    part = hold(part.reshape(64, 1024)).reshape(4, 2, 8, 1024)
+    part = jnp.stack([part, over_x_hi_x(part)[:, ::-1]], axis=2).reshape(4, 2, 16, 1024)
     a_parts = [part] + [over_z(part, k) for k in (1, 2, 3)]
     a_parts = a_parts + [over_core(part) for part in a_parts]
     saved = merge(bt_rows.reshape(R, 128).astype(jnp.float32), a_parts, arrived)

time: 92.2 us -> 92.2 us (level)
  starting transfers between devices: 41.8 us -> 43.8 us
  waiting for transfers between devices: 37.6 us -> 35.6 us
    ppermute x6, starting transfers between devices: 10.9 us -> 13.9 us  [over_core(): return lax.ppermute(array, 'col', [(i, i ^ 1) for i in range(16)])]
    ppermute x2, starting transfers between devices: 4.19 us -> 2.98 us  [over_col(): return lax.ppermute(array, 'col', [(i, i ^ mask) for i in range(16)])]
    ppermute x3, starting transfers between devices: 2.84 us -> 1.71 us  [over_y(): lax.ppermute(array, 'col', [(i, (i + 4 * k) % 16) for i in range(16)])]
    ppermute x6, waiting for transfers between devices: 7.45 us -> 6.32 us  [over_z(): lax.ppermute(array, 'row', [(i, i // 4 * 4 + (i + k) % 4) for i in range(...]
    all_to_all x1, starting transfers between devices: 7.52 us -> 8.64 us  [per_device(): arrived = lax.all_to_all(weight, 'col', 0, 0, tiled=True)]
    reshape x0 -> x1, other arithmetic: none -> 0.93 us  [per_device(): jnp.stack([part, over_x_hi_x(part)[:, ::-1]], axis=2)]
    another operation x1 -> x0, other arithmetic: 0.93 us -> none  [per_device(): part = jnp.stack([part, over_x_hi_x(part)])]
where the time goes in v6:
time: 92.2 us; the launch traced here: 91.9 us
  starting transfers between devices  43.8 us (48%)
  waiting for transfers between devices  35.6 us (39%)
  Pallas kernels  5.83 us (6%)
  other arithmetic  3.32 us (4%)
  local copies, waits for them, and re-layouts  2.39 us (3%)
  between operations  0.98 us (1%)
    all_to_all x1, waiting for transfers between devices, per_device(): arrived = lax.all_to_all(weight, 'col', 0, 0, tiled=True)  20.8 us
    ppermute x6, starting transfers between devices, over_core(): return lax.ppermute(array, 'col', [(i, i ^ 1) for i in range(16)])  13.9 us
    ppermute x6, starting transfers between devices, over_z(): lax.ppermute(array, 'row', [(i, i // 4 * 4 + (i + k) % 4) for i in range(...  8.96 us
    all_to_all x1, starting transfers between devices, per_device(): arrived = lax.all_to_all(weight, 'col', 0, 0, tiled=True)  8.64 us
    ppermute x6, waiting for transfers between devices, over_z(): lax.ppermute(array, 'row', [(i, i // 4 * 4 + (i + k) % 4) for i in range(...  6.32 us
    pallas_call x1, Pallas kernels, merge(): pl.pallas_call(merge_kernel, in_specs=[pl.BlockSpec(memory_space=pltpu.VM...  4.26 us
    ppermute x1, waiting for transfers between devices, over_x_hi_x(): lax.ppermute(array, ('row', 'col'), [(i, i ^ 4 * 16 + 2) for i in range(1...  3.89 us
    ppermute x2, starting transfers between devices, over_col(): return lax.ppermute(array, 'col', [(i, i ^ mask) for i in range(16)])  2.98 us
  transfers between devices with their start and end apart: 22, of which 12 were waited for; matrix products, arithmetic and copies ran while one was open for 5% of the time, Pallas kernels for 2%

profile of v6, /device:TPU:1, one launch (start us, length us, event | category | flops | bytes accessed | tf_op | source)
XLA Modules:
  0.0 91.9 jit_solution(15002726406658399338)
XLA Ops:
  0.7 1.2 %reshape.44 = f32[4,2,2,4,2048]{4,3,2,1,0:T(4,128)S(1)} reshape(f32[1,64,2048]{2,1,0:T(8,128)} %param.17) | data formatting | bytes 1048576 | tf_op jit(solution)/shard_map/reshape | solution.py:198
  2.0 1.5 %collective-permute-start = (f32[4,2,4,2048]{3,2,1,0:T(4,128)S(1)}, f32[4,2,4,2048]{3,2,1,0:T(4,128)S(1)}, u32[]{:S(2)}, u32[]{:S(2)}) collective-permute-start(f32[4,2,4,2048]{3,2,1,0:T(4,128)S(1)} %get-tuple-element.22), channel_id=1, source_target_pairs={{0,1},{1,0},{2,3},{3,2},{4,5},{5,4},{6,7},{7,6},{8,9},{9,8},{10,11... | collective-permute-start | bytes 786440 | tf_op jit(solution)/shard_map/ppermute | solution.py:144
  3.5 1.0 %dynamic-slice_bitcast_fusion.2 = (f32[2,8,1024]{2,1,0:T(8,128)S(1)}, f32[2,8,1024]{2,1,0:T(8,128)S(1)}, f32[2,8,1024]{2,1,0:T(8,128)S(1)}, f32[2,8,1024]{2,1,0:T(8,128)S(1)}) fusion(f32[2,4,8,1024]{3,2,1,0:T(8,128)} %bitcast.87, s32[]{:T(128)S(6)} %select_n.128, s32[]{:T(128)S(6)} %select_n.126, s32[]{:T(128)S(6)} %select_n.124, s32[]{:T(128)S(6)} %select_n.122), kind=kLoop, calls=%fused_computation.11 | loop fusion | bytes 524304 | tf_op jit(solution)/shard_map/jit(dynamic_index_in_dim)/squeeze | solution.py:140
  4.5 0.2 collective-permute-done
  4.7 0.1 add.182
  4.8 2.9 %collective-permute-start.1 = (f32[2,2,4,2048]{3,2,1,0:T(4,128)S(1)}, f32[2,2,4,2048]{3,2,1,0:T(4,128)S(1)}, u32[]{:S(2)}, u32[]{:S(2)}) collective-permute-start(f32[2,2,4,2048]{3,2,1,0:T(4,128)S(1)} %pad_maximum_fusion), channel_id=1, source_target_pairs={{0,12},{1,13},{2,14},{3,15},{4,8},{5,9},{6,10},{7,11},{8,4},{9,5},... | collective-permute-start | bytes 393224 | tf_op jit(solution)/shard_map/ppermute | solution.py:160
  7.7 1.6 %collective-permute-start.5 = (f32[2,8,1024]{2,1,0:T(8,128)S(1)}, f32[2,8,1024]{2,1,0:T(8,128)S(1)}, u32[]{:S(2)}, u32[]{:S(2)}) collective-permute-start(f32[2,8,1024]{2,1,0:T(8,128)S(1)} %get-tuple-element.28), channel_id=1, source_target_pairs={{0,16},{16,32},{32,48},{48,0},{64,80},{80,96},{96,112},{112,64},{1... | collective-permute-start | bytes 196616 | tf_op jit(solution)/shard_map/ppermute | solution.py:180
  9.3 3.3 %collective-permute-start.6 = (f32[2,8,1024]{2,1,0:T(8,128)S(1)}, f32[2,8,1024]{2,1,0:T(8,128)S(1)}, u32[]{:S(2)}, u32[]{:S(2)}) collective-permute-start(f32[2,8,1024]{2,1,0:T(8,128)S(1)} %get-tuple-element.29), channel_id=1, source_target_pairs={{0,32},{16,48},{32,0},{48,16},{64,96},{80,112},{96,64},{112,80},{1... | collective-permute-start | bytes 196616 | tf_op jit(solution)/shard_map/ppermute | solution.py:180
  12.6 0.7 collective-permute-start.7
  13.4 0.1 collective-permute-start.2
  13.5 1.7 %collective-permute-done.6 = f32[2,8,1024]{2,1,0:T(8,128)S(1)} collective-permute-done((f32[2,8,1024]{2,1,0:T(8,128)S(1)}, f32[2,8,1024]{2,1,0:T(8,128)S(1)}, u32[]{:S(2)}, u32[]{:S(2)}) %collective-permute-start.6) | collective-permute-done | bytes 65568 | tf_op jit(solution)/shard_map/ppermute | solution.py:180
  15.3 0.8 collective-permute-done.7
  16.1 0.6 collective-permute-done.2
  16.7 1.3 %collective-permute-start.3 = (f32[4,2048]{1,0:T(4,128)S(1)}, f32[4,2048]{1,0:T(4,128)S(1)}, u32[]{:S(2)}, u32[]{:S(2)}) collective-permute-start(f32[4,2048]{1,0:T(4,128)S(1)} %dynamic-slice_bitcast_fusion.7), channel_id=1, source_target_pairs={{0,2},{1,3},{2,0},{3,1},{4,6},{5,7},{6,4},{7,5},{8,10},{9,11},{10,... | collective-permute-start | bytes 98312 | tf_op jit(solution)/shard_map/ppermute | solution.py:148
  18.0 2.5 %collective-permute-start.8 = (f32[8,1024]{1,0:T(8,128)S(1)}, f32[8,1024]{1,0:T(8,128)S(1)}, u32[]{:S(2)}, u32[]{:S(2)}) collective-permute-start(f32[8,1024]{1,0:T(8,128)S(1)} %dynamic-slice_bitcast_fusion.6), channel_id=1, source_target_pairs={{0,64},{16,80},{32,96},{48,112},{64,0},{80,16},{96,32},{112,48},{1... | collective-permute-start | bytes 98312 | tf_op jit(solution)/shard_map/ppermute | solution.py:172
  20.5 0.0 collective-permute-done.3
  20.5 0.1 multiply_subtract_fusion.2
  20.7 3.2 %collective-permute-start.4 = (bf16[4,2,4,128]{3,2,1,0:T(4,128)(2,1)S(1)}, bf16[4,2,4,128]{3,2,1,0:T(4,128)(2,1)S(1)}, u32[]{:S(2)}, u32[]{:S(2)}) collective-permute-start(bf16[4,2,4,128]{3,2,1,0:T(4,128)(2,1)S(1)} %bitcast.95), channel_id=1, source_target_pairs={{0,1},{1,0},{2,3},{3,2},{4,5},{5,4},{6,7},{7,6},{8,9},{9,8},{10,11... | collective-permute-start | bytes 24584 | tf_op jit(solution)/shard_map/ppermute | solution.py:144
  24.0 0.7 collective-permute-done.4
  24.8 1.0 %collective-permute-start.9 = (bf16[8,1536]{1,0:T(8,128)(2,1)S(1)}, bf16[8,1536]{1,0:T(8,128)(2,1)S(1)}, u32[]{:S(2)}, u32[]{:S(2)}) collective-permute-start(bf16[8,1536]{1,0:T(8,128)(2,1)S(1)} %pad_maximum_fusion.7), channel_id=1, source_target_pairs={{0,2},{1,3},{2,0},{3,1},{4,6},{5,7},{6,4},{7,5},{8,10},{9,11},{10,... | collective-permute-start | bytes 73736 | tf_op jit(solution)/shard_map/ppermute | solution.py:148
  25.7 1.8 %collective-permute-done.9 = bf16[8,1536]{1,0:T(8,128)(2,1)S(1)} collective-permute-done((bf16[8,1536]{1,0:T(8,128)(2,1)S(1)}, bf16[8,1536]{1,0:T(8,128)(2,1)S(1)}, u32[]{:S(2)}, u32[]{:S(2)}) %collective-permute-start.9) | collective-permute-done | bytes 24608 | tf_op jit(solution)/shard_map/ppermute | solution.py:148
  27.6 0.1 collective-permute-start.12
  27.7 1.6 %collective-permute-start.11 = (bf16[2,8,1152]{2,1,0:T(8,128)(2,1)S(1)}, bf16[2,8,1152]{2,1,0:T(8,128)(2,1)S(1)}, u32[]{:S(2)}, u32[]{:S(2)}) collective-permute-start(bf16[2,8,1152]{2,1,0:T(8,128)(2,1)S(1)} %get-tuple-element.56), channel_id=1, source_target_pairs={{0,8},{1,9},{2,10},{3,11},{4,12},{5,13},{6,14},{7,15},{8,0},{9,1},... | collective-permute-start | bytes 110600 | tf_op jit(solution)/shard_map/ppermute | solution.py:152
  29.3 0.0 collective-permute-start.10
  29.3 8.6 %all-to-all-start = ((bf16[16,128,1024]{2,1,0:T(8,128)(2,1)}), bf16[16,128,1024]{2,1,0:T(8,128)(2,1)}, u32[]{:S(2)}, u32[]{:S(2)}) async-start(bf16[16,128,1024]{2,1,0:T(8,128)(2,1)} %bitcast.86), calls=%async_computation | async-start | bytes 8388608 | tf_op jit(solution)/shard_map/all_to_all | solution.py:226
  37.9 0.7 multiply_subtract_fusion
  38.6 0.7 multiply_subtract_fusion.1
  39.3 0.0 collective-permute-done.12
  39.3 0.0 collective-permute-done.11
  39.3 0.0 collective-permute-done.10
  39.3 0.7 pad_maximum_fusion.1
  40.0 1.6 %shard_map.144 = bf16[64,1024]{1,0:T(8,128)(2,1)} custom-call(bf16[64,1024]{1,0:T(8,128)(2,1)} %bitcast.90), custom_call_target="tpu_custom_call" | custom-call | flops 99999997952 | bytes 262144 | tf_op jit(solution)/shard_map/pallas_call | solution.py:132
  41.6 2.9 %collective-permute-start.13 = (bf16[4,2,8,1024]{3,2,1,0:T(8,128)(2,1)}, bf16[4,2,8,1024]{3,2,1,0:T(8,128)(2,1)S(1)}, u32[]{:S(2)}, u32[]{:S(2)}) collective-permute-start(bf16[4,2,8,1024]{3,2,1,0:T(8,128)(2,1)} %bitcast.91), channel_id=1, source_target_pairs={{0,66},{1,67},{2,64},{3,65},{4,70},{5,71},{6,68},{7,69},{8,74},{9,... | collective-permute-start | bytes 393224 | tf_op jit(solution)/shard_map/ppermute | solution.py:176
  44.5 3.9 %collective-permute-done.13 = bf16[4,2,8,1024]{3,2,1,0:T(8,128)(2,1)S(1)} collective-permute-done((bf16[4,2,8,1024]{3,2,1,0:T(8,128)(2,1)}, bf16[4,2,8,1024]{3,2,1,0:T(8,128)(2,1)S(1)}, u32[]{:S(2)}, u32[]{:S(2)}) %collective-permute-start.13) | collective-permute-done | bytes 131104 | tf_op jit(solution)/shard_map/ppermute | solution.py:176
  48.4 0.9 %maximum_bitcast_fusion.refs_0_ = bf16[4,2,16,1024]{3,2,1,0:T(8,128)(2,1)S(1)} fusion(bf16[4,2,1,8,1024]{4,3,2,1,0:T(8,128)(2,1)S(1)} %reverse_bitcast_fusion, bf16[4,2,1,8,1024]{4,3,2,1,0:T(8,128)(2,1)} %bitcast.92), kind=kLoop, calls=%fused_computation | loop fusion | flops 131072 | bytes 524288 | tf_op jit(solution)/shard_map/reshape | solution.py:230
  49.3 0.8 collective-permute-start.14
  50.1 1.7 %collective-permute-start.15 = (bf16[4,2,16,1024]{3,2,1,0:T(8,128)(2,1)S(1)}, bf16[4,2,16,1024]{3,2,1,0:T(8,128)(2,1)S(1)}, u32[]{:S(2)}, u32[]{:S(2)}) collective-permute-start(bf16[4,2,16,1024]{3,2,1,0:T(8,128)(2,1)S(1)} %maximum_bitcast_fusion.refs_0_), channel_id=1, source_target_pairs={{0,32},{16,48},{32,0},{48,16},{64,96},{80,112},{96,64},{112,80},{1... | collective-permute-start | bytes 786440 | tf_op jit(solution)/shard_map/ppermute | solution.py:180
  51.9 0.8 collective-permute-start.16
  52.6 1.8 %collective-permute-start.17 = (bf16[4,2,16,1024]{3,2,1,0:T(8,128)(2,1)S(1)}, bf16[4,2,16,1024]{3,2,1,0:T(8,128)(2,1)S(1)}, u32[]{:S(2)}, u32[]{:S(2)}) collective-permute-start(bf16[4,2,16,1024]{3,2,1,0:T(8,128)(2,1)S(1)} %maximum_bitcast_fusion.refs_0_), channel_id=1, source_target_pairs={{0,1},{1,0},{2,3},{3,2},{4,5},{5,4},{6,7},{7,6},{8,9},{9,8},{10,11... | collective-permute-start | bytes 786440 | tf_op jit(solution)/shard_map/ppermute | solution.py:144
  54.4 3.8 %collective-permute-done.14.refs_1_ = bf16[4,2,16,1024]{3,2,1,0:T(8,128)(2,1)S(1)} collective-permute-done((bf16[4,2,16,1024]{3,2,1,0:T(8,128)(2,1)S(1)}, bf16[4,2,16,1024]{3,2,1,0:T(8,128)(2,1)S(1)}, u32[]{:S(2)}, u32[]{:S(2)}) %collective-permute-start.14) | collective-permute-done | bytes 262176 | tf_op jit(solution)/shard_map/ppermute | solution.py:180
  58.2 6.7 %collective-permute-start.18 = (bf16[4,2,16,1024]{3,2,1,0:T(8,128)(2,1)S(1)}, bf16[4,2,16,1024]{3,2,1,0:T(8,128)(2,1)S(1)}, u32[]{:S(2)}, u32[]{:S(2)}) collective-permute-start(bf16[4,2,16,1024]{3,2,1,0:T(8,128)(2,1)S(1)} %collective-permute-done.14.refs_1_), channel_id=1, source_target_pairs={{0,1},{1,0},{2,3},{3,2},{4,5},{5,4},{6,7},{7,6},{8,9},{9,8},{10,11... | collective-permute-start | bytes 786440 | tf_op jit(solution)/shard_map/ppermute | solution.py:144
  64.9 0.0 collective-permute-start.19
  64.9 0.6 collective-permute-start.20
  65.6 0.5 collective-permute-done.18.refs_5_
  66.1 0.4 collective-permute-done.19.refs_6_
  66.5 0.4 collective-permute-done.20.refs_7_
  66.8 20.8 %all-to-all-done.refs_8_ = bf16[16,128,1024]{2,1,0:T(8,128)(2,1)} async-done(((bf16[16,128,1024]{2,1,0:T(8,128)(2,1)}), bf16[16,128,1024]{2,1,0:T(8,128)(2,1)}, u32[]{:S(2)}, u32[]{:S(2)}) %all-to-all-start) | async-done | bytes 4194336 | tf_op jit(solution)/shard_map/all_to_all | solution.py:226
  87.6 4.3 %shard_map.145 = bf16[8,128,2048]{2,1,0:T(8,128)(2,1)} custom-call(f32[64,128]{1,0:T(8,128)S(1)} %bitcast_convert_fusion.bt_ref, bf16[4,2,16,1024]{3,2,1,0:T(8,128)(2,1)S(1)} %maximum_bitcast_fusion.refs_0_, bf16[4,2,16,1024]{3,2,1,0:T(8,128)(2,1)S(1)} %collective-permute-done.14.refs_1_, bf16[4,2,16,1024]{3,2,1,0:T(8,128)(2,1)S(1)} %collective-permute-done.15.refs_2_, ...), custom_call_target="tpu_custom_call" | custom-call | flops 268435456 | bytes 10485760 | tf_op jit(solution)/shard_map/pallas_call | solution.py:107
  (48 shorter events, 0.5 us)
Async XLA Ops:
  0.6 19.9 %copy-start = (f32[4,2048]{1,0:T(4,128)S(1)}, f32[4,2048]{1,0:T(4,128)}, u32[]{:S(2)}) copy-start(f32[4,2048]{1,0:T(4,128)} %param.13) | copy-start | bytes 98308
  0.6 19.8 %copy-start.2 = (f32[4,2048]{1,0:T(4,128)S(1)}, f32[4,2048]{1,0:T(4,128)}, u32[]{:S(2)}) copy-start(f32[4,2048]{1,0:T(4,128)} %param.14) | copy-start | bytes 98308
  0.7 19.8 %copy-start.1 = (f32[4,2048]{1,0:T(4,128)S(1)}, f32[4,2048]{1,0:T(4,128)}, u32[]{:S(2)}) copy-start(f32[4,2048]{1,0:T(4,128)} %param.15) | copy-start | bytes 98308
  0.7 23.2 %copy-start.3 = (f32[8,1024]{1,0:T(8,128)S(1)}, f32[8,1024]{1,0:T(8,128)}, u32[]{:S(2)}) copy-start(f32[8,1024]{1,0:T(8,128)} %param.10) | copy-start | bytes 98308
  0.7 23.2 %copy-start.5 = (f32[8,1024]{1,0:T(8,128)S(1)}, f32[8,1024]{1,0:T(8,128)}, u32[]{:S(2)}) copy-start(f32[8,1024]{1,0:T(8,128)} %param.11) | copy-start | bytes 98308
  0.7 23.2 %copy-start.4 = (f32[8,1024]{1,0:T(8,128)S(1)}, f32[8,1024]{1,0:T(8,128)}, u32[]{:S(2)}) copy-start(f32[8,1024]{1,0:T(8,128)} %param.12) | copy-start | bytes 98308
  2.0 2.7 %collective-permute-start = (f32[4,2,4,2048]{3,2,1,0:T(4,128)S(1)}, f32[4,2,4,2048]{3,2,1,0:T(4,128)S(1)}, u32[]{:S(2)}, u32[]{:S(2)}) collective-permute-start(f32[4,2,4,2048]{3,2,1,0:T(4,128)S(1)} %get-tuple-element.22), channel_id=1, source_target_pairs={{0,1},{1,0},{2,3},{3,2},{4,5},{5,4},{6,7},{7,6},{8,9},{9,8},{10,11... | collective-permute-start | bytes 786440 | tf_op jit(solution)/shard_map/ppermute | solution.py:144
  4.8 8.6 %collective-permute-start.1 = (f32[2,2,4,2048]{3,2,1,0:T(4,128)S(1)}, f32[2,2,4,2048]{3,2,1,0:T(4,128)S(1)}, u32[]{:S(2)}, u32[]{:S(2)}) collective-permute-start(f32[2,2,4,2048]{3,2,1,0:T(4,128)S(1)} %pad_maximum_fusion), channel_id=1, source_target_pairs={{0,12},{1,13},{2,14},{3,15},{4,8},{5,9},{6,10},{7,11},{8,4},{9,5},... | collective-permute-start | bytes 393224 | tf_op jit(solution)/shard_map/ppermute | solution.py:160
  7.7 5.8 %collective-permute-start.5 = (f32[2,8,1024]{2,1,0:T(8,128)S(1)}, f32[2,8,1024]{2,1,0:T(8,128)S(1)}, u32[]{:S(2)}, u32[]{:S(2)}) collective-permute-start(f32[2,8,1024]{2,1,0:T(8,128)S(1)} %get-tuple-element.28), channel_id=1, source_target_pairs={{0,16},{16,32},{32,48},{48,0},{64,80},{80,96},{96,112},{112,64},{1... | collective-permute-start | bytes 196616 | tf_op jit(solution)/shard_map/ppermute | solution.py:180
  9.3 5.9 %collective-permute-start.6 = (f32[2,8,1024]{2,1,0:T(8,128)S(1)}, f32[2,8,1024]{2,1,0:T(8,128)S(1)}, u32[]{:S(2)}, u32[]{:S(2)}) collective-permute-start(f32[2,8,1024]{2,1,0:T(8,128)S(1)} %get-tuple-element.29), channel_id=1, source_target_pairs={{0,32},{16,48},{32,0},{48,16},{64,96},{80,112},{96,64},{112,80},{1... | collective-permute-start | bytes 196616 | tf_op jit(solution)/shard_map/ppermute | solution.py:180
  12.6 3.4 %collective-permute-start.7 = (f32[2,8,1024]{2,1,0:T(8,128)S(1)}, f32[2,8,1024]{2,1,0:T(8,128)S(1)}, u32[]{:S(2)}, u32[]{:S(2)}) collective-permute-start(f32[2,8,1024]{2,1,0:T(8,128)S(1)} %get-tuple-element.30), channel_id=1, source_target_pairs={{0,48},{16,0},{32,16},{48,32},{64,112},{80,64},{96,80},{112,96},{1... | collective-permute-start | bytes 196616 | tf_op jit(solution)/shard_map/ppermute | solution.py:180
  13.4 3.3 %collective-permute-start.2 = (f32[2,4,2048]{2,1,0:T(4,128)S(1)}, f32[2,4,2048]{2,1,0:T(4,128)S(1)}, u32[]{:S(2)}, u32[]{:S(2)}) collective-permute-start(f32[2,4,2048]{2,1,0:T(4,128)S(1)} %slice_bitcast_fusion), channel_id=1, source_target_pairs={{0,4},{1,5},{2,6},{3,7},{4,0},{5,1},{6,2},{7,3},{8,12},{9,13},{10,... | collective-permute-start | bytes 196616 | tf_op jit(solution)/shard_map/ppermute | solution.py:160
  16.7 3.7 %collective-permute-start.3 = (f32[4,2048]{1,0:T(4,128)S(1)}, f32[4,2048]{1,0:T(4,128)S(1)}, u32[]{:S(2)}, u32[]{:S(2)}) collective-permute-start(f32[4,2048]{1,0:T(4,128)S(1)} %dynamic-slice_bitcast_fusion.7), channel_id=1, source_target_pairs={{0,2},{1,3},{2,0},{3,1},{4,6},{5,7},{6,4},{7,5},{8,10},{9,11},{10,... | collective-permute-start | bytes 98312 | tf_op jit(solution)/shard_map/ppermute | solution.py:148
  18.0 5.9 %collective-permute-start.8 = (f32[8,1024]{1,0:T(8,128)S(1)}, f32[8,1024]{1,0:T(8,128)S(1)}, u32[]{:S(2)}, u32[]{:S(2)}) collective-permute-start(f32[8,1024]{1,0:T(8,128)S(1)} %dynamic-slice_bitcast_fusion.6), channel_id=1, source_target_pairs={{0,64},{16,80},{32,96},{48,112},{64,0},{80,16},{96,32},{112,48},{1... | collective-permute-start | bytes 98312 | tf_op jit(solution)/shard_map/ppermute | solution.py:172
  20.7 4.1 %collective-permute-start.4 = (bf16[4,2,4,128]{3,2,1,0:T(4,128)(2,1)S(1)}, bf16[4,2,4,128]{3,2,1,0:T(4,128)(2,1)S(1)}, u32[]{:S(2)}, u32[]{:S(2)}) collective-permute-start(bf16[4,2,4,128]{3,2,1,0:T(4,128)(2,1)S(1)} %bitcast.95), channel_id=1, source_target_pairs={{0,1},{1,0},{2,3},{3,2},{4,5},{5,4},{6,7},{7,6},{8,9},{9,8},{10,11... | collective-permute-start | bytes 24584 | tf_op jit(solution)/shard_map/ppermute | solution.py:144
  24.8 2.8 %collective-permute-start.9 = (bf16[8,1536]{1,0:T(8,128)(2,1)S(1)}, bf16[8,1536]{1,0:T(8,128)(2,1)S(1)}, u32[]{:S(2)}, u32[]{:S(2)}) collective-permute-start(bf16[8,1536]{1,0:T(8,128)(2,1)S(1)} %pad_maximum_fusion.7), channel_id=1, source_target_pairs={{0,2},{1,3},{2,0},{3,1},{4,6},{5,7},{6,4},{7,5},{8,10},{9,11},{10,... | collective-permute-start | bytes 73736 | tf_op jit(solution)/shard_map/ppermute | solution.py:148
  27.6 11.7 %collective-permute-start.12 = (bf16[2,8,1152]{2,1,0:T(8,128)(2,1)S(1)}, bf16[2,8,1152]{2,1,0:T(8,128)(2,1)S(1)}, u32[]{:S(2)}, u32[]{:S(2)}) collective-permute-start(bf16[2,8,1152]{2,1,0:T(8,128)(2,1)S(1)} %get-tuple-element.57), channel_id=1, source_target_pairs={{0,12},{1,13},{2,14},{3,15},{4,0},{5,1},{6,2},{7,3},{8,4},{9,5},{1... | collective-permute-start | bytes 110600 | tf_op jit(solution)/shard_map/ppermute | solution.py:152
  27.7 11.6 %collective-permute-start.11 = (bf16[2,8,1152]{2,1,0:T(8,128)(2,1)S(1)}, bf16[2,8,1152]{2,1,0:T(8,128)(2,1)S(1)}, u32[]{:S(2)}, u32[]{:S(2)}) collective-permute-start(bf16[2,8,1152]{2,1,0:T(8,128)(2,1)S(1)} %get-tuple-element.56), channel_id=1, source_target_pairs={{0,8},{1,9},{2,10},{3,11},{4,12},{5,13},{6,14},{7,15},{8,0},{9,1},... | collective-permute-start | bytes 110600 | tf_op jit(solution)/shard_map/ppermute | solution.py:152
  29.3 10.0 %collective-permute-start.10 = (bf16[2,8,1152]{2,1,0:T(8,128)(2,1)S(1)}, bf16[2,8,1152]{2,1,0:T(8,128)(2,1)S(1)}, u32[]{:S(2)}, u32[]{:S(2)}) collective-permute-start(bf16[2,8,1152]{2,1,0:T(8,128)(2,1)S(1)} %get-tuple-element.55), channel_id=1, source_target_pairs={{0,4},{1,5},{2,6},{3,7},{4,8},{5,9},{6,10},{7,11},{8,12},{9,13},{1... | collective-permute-start | bytes 110600 | tf_op jit(solution)/shard_map/ppermute | solution.py:152
  29.3 58.3 %all-to-all-start = ((bf16[16,128,1024]{2,1,0:T(8,128)(2,1)}), bf16[16,128,1024]{2,1,0:T(8,128)(2,1)}, u32[]{:S(2)}, u32[]{:S(2)}) async-start(bf16[16,128,1024]{2,1,0:T(8,128)(2,1)} %bitcast.86), calls=%async_computation | async-start | bytes 8388608 | tf_op jit(solution)/shard_map/all_to_all | solution.py:226
  41.6 6.8 %collective-permute-start.13 = (bf16[4,2,8,1024]{3,2,1,0:T(8,128)(2,1)}, bf16[4,2,8,1024]{3,2,1,0:T(8,128)(2,1)S(1)}, u32[]{:S(2)}, u32[]{:S(2)}) collective-permute-start(bf16[4,2,8,1024]{3,2,1,0:T(8,128)(2,1)} %bitcast.91), channel_id=1, source_target_pairs={{0,66},{1,67},{2,64},{3,65},{4,70},{5,71},{6,68},{7,69},{8,74},{9,... | collective-permute-start | bytes 393224 | tf_op jit(solution)/shard_map/ppermute | solution.py:176
  49.3 8.9 %collective-permute-start.14 = (bf16[4,2,16,1024]{3,2,1,0:T(8,128)(2,1)S(1)}, bf16[4,2,16,1024]{3,2,1,0:T(8,128)(2,1)S(1)}, u32[]{:S(2)}, u32[]{:S(2)}) collective-permute-start(bf16[4,2,16,1024]{3,2,1,0:T(8,128)(2,1)S(1)} %maximum_bitcast_fusion.refs_0_), channel_id=1, source_target_pairs={{0,16},{16,32},{32,48},{48,0},{64,80},{80,96},{96,112},{112,64},{1... | collective-permute-start | bytes 786440 | tf_op jit(solution)/shard_map/ppermute | solution.py:180
  50.1 14.8 %collective-permute-start.15 = (bf16[4,2,16,1024]{3,2,1,0:T(8,128)(2,1)S(1)}, bf16[4,2,16,1024]{3,2,1,0:T(8,128)(2,1)S(1)}, u32[]{:S(2)}, u32[]{:S(2)}) collective-permute-start(bf16[4,2,16,1024]{3,2,1,0:T(8,128)(2,1)S(1)} %maximum_bitcast_fusion.refs_0_), channel_id=1, source_target_pairs={{0,32},{16,48},{32,0},{48,16},{64,96},{80,112},{96,64},{112,80},{1... | collective-permute-start | bytes 786440 | tf_op jit(solution)/shard_map/ppermute | solution.py:180
  51.9 13.1 %collective-permute-start.16 = (bf16[4,2,16,1024]{3,2,1,0:T(8,128)(2,1)S(1)}, bf16[4,2,16,1024]{3,2,1,0:T(8,128)(2,1)S(1)}, u32[]{:S(2)}, u32[]{:S(2)}) collective-permute-start(bf16[4,2,16,1024]{3,2,1,0:T(8,128)(2,1)S(1)} %maximum_bitcast_fusion.refs_0_), channel_id=1, source_target_pairs={{0,48},{16,0},{32,16},{48,32},{64,112},{80,64},{96,80},{112,96},{1... | collective-permute-start | bytes 786440 | tf_op jit(solution)/shard_map/ppermute | solution.py:180
  52.6 13.0 %collective-permute-start.17 = (bf16[4,2,16,1024]{3,2,1,0:T(8,128)(2,1)S(1)}, bf16[4,2,16,1024]{3,2,1,0:T(8,128)(2,1)S(1)}, u32[]{:S(2)}, u32[]{:S(2)}) collective-permute-start(bf16[4,2,16,1024]{3,2,1,0:T(8,128)(2,1)S(1)} %maximum_bitcast_fusion.refs_0_), channel_id=1, source_target_pairs={{0,1},{1,0},{2,3},{3,2},{4,5},{5,4},{6,7},{7,6},{8,9},{9,8},{10,11... | collective-permute-start | bytes 786440 | tf_op jit(solution)/shard_map/ppermute | solution.py:144
  58.2 7.9 %collective-permute-start.18 = (bf16[4,2,16,1024]{3,2,1,0:T(8,128)(2,1)S(1)}, bf16[4,2,16,1024]{3,2,1,0:T(8,128)(2,1)S(1)}, u32[]{:S(2)}, u32[]{:S(2)}) collective-permute-start(bf16[4,2,16,1024]{3,2,1,0:T(8,128)(2,1)S(1)} %collective-permute-done.14.refs_1_), channel_id=1, source_target_pairs={{0,1},{1,0},{2,3},{3,2},{4,5},{5,4},{6,7},{7,6},{8,9},{9,8},{10,11... | collective-permute-start | bytes 786440 | tf_op jit(solution)/shard_map/ppermute | solution.py:144
  64.9 1.5 %collective-permute-start.19 = (bf16[4,2,16,1024]{3,2,1,0:T(8,128)(2,1)S(1)}, bf16[4,2,16,1024]{3,2,1,0:T(8,128)(2,1)S(1)}, u32[]{:S(2)}, u32[]{:S(2)}) collective-permute-start(bf16[4,2,16,1024]{3,2,1,0:T(8,128)(2,1)S(1)} %collective-permute-done.15.refs_2_), channel_id=1, source_target_pairs={{0,1},{1,0},{2,3},{3,2},{4,5},{5,4},{6,7},{7,6},{8,9},{9,8},{10,11... | collective-permute-start | bytes 786440 | tf_op jit(solution)/shard_map/ppermute | solution.py:144
  64.9 1.9 %collective-permute-start.20 = (bf16[4,2,16,1024]{3,2,1,0:T(8,128)(2,1)S(1)}, bf16[4,2,16,1024]{3,2,1,0:T(8,128)(2,1)S(1)}, u32[]{:S(2)}, u32[]{:S(2)}) collective-permute-start(bf16[4,2,16,1024]{3,2,1,0:T(8,128)(2,1)S(1)} %collective-permute-done.16.refs_3_), channel_id=1, source_target_pairs={{0,1},{1,0},{2,3},{3,2},{4,5},{5,4},{6,7},{7,6},{8,9},{9,8},{10,11... | collective-permute-start | bytes 786440 | tf_op jit(solution)/shard_map/ppermute | solution.py:144

commit v7 on v6

--- a/solution.py
+++ b/solution.py
@@ -201,7 +201,7 @@
     part = grad_a_parts.reshape(2, 4, 8, 1024)
     kept, *sent = lax.optimization_barrier([pick(part, (z + k) % 4, 1) for k in range(4)])
     bt_part, *sent = lax.optimization_barrier((bt_part, *sent))
-    part = kept + sum(over_z(array, k) for array, k in zip(sent, (1, 2, 3)))
+    part = kept + sum(over_z(sent[k - 1], k) for k in (3, 2, 1))
     grad_a = pick(part, x_hi, 0) + over_x_hi(pick(part, 1 - x_hi, 0))
     bt_part = two_of(bt_part, y, y ^ 1, 0) + over_col(two_of(bt_part, y ^ 3, y ^ 2, 0), 12)
     bt_part = bt_part[0] + over_col(bt_part[1], 4)

time: 92.2 us -> 91.5 us (level)
  starting transfers between devices: 43.8 us -> 40.3 us
  waiting for transfers between devices: 35.6 us -> 38.5 us
    ppermute x6, waiting for transfers between devices: 6.32 us -> 10 us  [over_z(): lax.ppermute(array, 'row', [(i, i // 4 * 4 + (i + k) % 4) for i in range(...]
    ppermute x6, starting transfers between devices: 13.9 us -> 10.6 us  [over_core(): return lax.ppermute(array, 'col', [(i, i ^ 1) for i in range(16)])]
where the time goes in v7:
time: 91.5 us; the launch traced here: 91.2 us
  starting transfers between devices  40.3 us (44%)
  waiting for transfers between devices  38.5 us (42%)
  Pallas kernels  5.83 us (6%)
  other arithmetic  3.32 us (4%)
  local copies, waits for them, and re-layouts  2.39 us (3%)
  between operations  0.99 us (1%)
    all_to_all x1, waiting for transfers between devices, per_device(): arrived = lax.all_to_all(weight, 'col', 0, 0, tiled=True)  20.7 us
    ppermute x6, starting transfers between devices, over_core(): return lax.ppermute(array, 'col', [(i, i ^ 1) for i in range(16)])  10.6 us
    ppermute x6, waiting for transfers between devices, over_z(): lax.ppermute(array, 'row', [(i, i // 4 * 4 + (i + k) % 4) for i in range(...  10 us
    all_to_all x1, starting transfers between devices, per_device(): arrived = lax.all_to_all(weight, 'col', 0, 0, tiled=True)  8.64 us
    ppermute x6, starting transfers between devices, over_z(): lax.ppermute(array, 'row', [(i, i // 4 * 4 + (i + k) % 4) for i in range(...  8.41 us
    pallas_call x1, Pallas kernels, merge(): pl.pallas_call(merge_kernel, in_specs=[pl.BlockSpec(memory_space=pltpu.VM...  4.26 us
    ppermute x1, waiting for transfers between devices, over_x_hi_x(): lax.ppermute(array, ('row', 'col'), [(i, i ^ 4 * 16 + 2) for i in range(1...  3.89 us
    ppermute x2, starting transfers between devices, over_col(): return lax.ppermute(array, 'col', [(i, i ^ mask) for i in range(16)])  2.98 us
  transfers between devices with their start and end apart: 22, of which 12 were waited for; matrix products, arithmetic and copies ran while one was open for 5% of the time, Pallas kernels for 2%

profile of v7, /device:TPU:1, one launch (start us, length us, event | category | flops | bytes accessed | tf_op | source)
XLA Modules:
  0.0 91.2 jit_solution(4290957262857640562)
XLA Ops:
  0.7 1.2 %reshape.44 = f32[4,2,2,4,2048]{4,3,2,1,0:T(4,128)S(1)} reshape(f32[1,64,2048]{2,1,0:T(8,128)} %param.17) | data formatting | bytes 1048576 | tf_op jit(solution)/shard_map/reshape | solution.py:198
  2.0 1.5 %collective-permute-start = (f32[4,2,4,2048]{3,2,1,0:T(4,128)S(1)}, f32[4,2,4,2048]{3,2,1,0:T(4,128)S(1)}, u32[]{:S(2)}, u32[]{:S(2)}) collective-permute-start(f32[4,2,4,2048]{3,2,1,0:T(4,128)S(1)} %get-tuple-element.22), channel_id=1, source_target_pairs={{0,1},{1,0},{2,3},{3,2},{4,5},{5,4},{6,7},{7,6},{8,9},{9,8},{10,11... | collective-permute-start | bytes 786440 | tf_op jit(solution)/shard_map/ppermute | solution.py:144
  3.5 1.0 %dynamic-slice_bitcast_fusion.2 = (f32[2,8,1024]{2,1,0:T(8,128)S(1)}, f32[2,8,1024]{2,1,0:T(8,128)S(1)}, f32[2,8,1024]{2,1,0:T(8,128)S(1)}, f32[2,8,1024]{2,1,0:T(8,128)S(1)}) fusion(f32[2,4,8,1024]{3,2,1,0:T(8,128)} %bitcast.87, s32[]{:T(128)S(6)} %select_n.128, s32[]{:T(128)S(6)} %select_n.126, s32[]{:T(128)S(6)} %select_n.124, s32[]{:T(128)S(6)} %select_n.122), kind=kLoop, calls=%fused_computation.11 | loop fusion | bytes 524304 | tf_op jit(solution)/shard_map/jit(dynamic_index_in_dim)/squeeze | solution.py:140
  4.5 0.2 collective-permute-done
  4.7 0.1 add.182
  4.8 2.9 %collective-permute-start.1 = (f32[2,2,4,2048]{3,2,1,0:T(4,128)S(1)}, f32[2,2,4,2048]{3,2,1,0:T(4,128)S(1)}, u32[]{:S(2)}, u32[]{:S(2)}) collective-permute-start(f32[2,2,4,2048]{3,2,1,0:T(4,128)S(1)} %pad_maximum_fusion), channel_id=1, source_target_pairs={{0,12},{1,13},{2,14},{3,15},{4,8},{5,9},{6,10},{7,11},{8,4},{9,5},... | collective-permute-start | bytes 393224 | tf_op jit(solution)/shard_map/ppermute | solution.py:160
  7.7 3.8 %collective-permute-start.5 = (f32[2,8,1024]{2,1,0:T(8,128)S(1)}, f32[2,8,1024]{2,1,0:T(8,128)S(1)}, u32[]{:S(2)}, u32[]{:S(2)}) collective-permute-start(f32[2,8,1024]{2,1,0:T(8,128)S(1)} %get-tuple-element.28), channel_id=1, source_target_pairs={{0,48},{16,0},{32,16},{48,32},{64,112},{80,64},{96,80},{112,96},{1... | collective-permute-start | bytes 196616 | tf_op jit(solution)/shard_map/ppermute | solution.py:180
  11.5 0.7 collective-permute-start.7
  12.2 0.1 collective-permute-start.2
  12.3 0.5 collective-permute-done.5
  12.8 3.4 %collective-permute-done.6 = f32[2,8,1024]{2,1,0:T(8,128)S(1)} collective-permute-done((f32[2,8,1024]{2,1,0:T(8,128)S(1)}, f32[2,8,1024]{2,1,0:T(8,128)S(1)}, u32[]{:S(2)}, u32[]{:S(2)}) %collective-permute-start.6) | collective-permute-done | bytes 65568 | tf_op jit(solution)/shard_map/ppermute | solution.py:180
  16.2 0.3 collective-permute-done.7
  16.6 1.3 %collective-permute-start.3 = (f32[4,2048]{1,0:T(4,128)S(1)}, f32[4,2048]{1,0:T(4,128)S(1)}, u32[]{:S(2)}, u32[]{:S(2)}) collective-permute-start(f32[4,2048]{1,0:T(4,128)S(1)} %dynamic-slice_bitcast_fusion.7), channel_id=1, source_target_pairs={{0,2},{1,3},{2,0},{3,1},{4,6},{5,7},{6,4},{7,5},{8,10},{9,11},{10,... | collective-permute-start | bytes 98312 | tf_op jit(solution)/shard_map/ppermute | solution.py:148
  17.9 2.5 %collective-permute-start.8 = (f32[8,1024]{1,0:T(8,128)S(1)}, f32[8,1024]{1,0:T(8,128)S(1)}, u32[]{:S(2)}, u32[]{:S(2)}) collective-permute-start(f32[8,1024]{1,0:T(8,128)S(1)} %dynamic-slice_bitcast_fusion.6), channel_id=1, source_target_pairs={{0,64},{16,80},{32,96},{48,112},{64,0},{80,16},{96,32},{112,48},{1... | collective-permute-start | bytes 98312 | tf_op jit(solution)/shard_map/ppermute | solution.py:172
  20.3 0.0 collective-permute-done.3
  20.3 0.1 multiply_subtract_fusion.2
  20.5 2.7 %collective-permute-start.4 = (bf16[4,2,4,128]{3,2,1,0:T(4,128)(2,1)S(1)}, bf16[4,2,4,128]{3,2,1,0:T(4,128)(2,1)S(1)}, u32[]{:S(2)}, u32[]{:S(2)}) collective-permute-start(bf16[4,2,4,128]{3,2,1,0:T(4,128)(2,1)S(1)} %bitcast.95), channel_id=1, source_target_pairs={{0,1},{1,0},{2,3},{3,2},{4,5},{5,4},{6,7},{7,6},{8,9},{9,8},{10,11... | collective-permute-start | bytes 24584 | tf_op jit(solution)/shard_map/ppermute | solution.py:144
  23.3 0.7 collective-permute-done.4
  24.1 1.2 %collective-permute-start.9 = (bf16[8,1536]{1,0:T(8,128)(2,1)S(1)}, bf16[8,1536]{1,0:T(8,128)(2,1)S(1)}, u32[]{:S(2)}, u32[]{:S(2)}) collective-permute-start(bf16[8,1536]{1,0:T(8,128)(2,1)S(1)} %pad_maximum_fusion.7), channel_id=1, source_target_pairs={{0,2},{1,3},{2,0},{3,1},{4,6},{5,7},{6,4},{7,5},{8,10},{9,11},{10,... | collective-permute-start | bytes 73736 | tf_op jit(solution)/shard_map/ppermute | solution.py:148
  25.3 1.5 %collective-permute-done.9 = bf16[8,1536]{1,0:T(8,128)(2,1)S(1)} collective-permute-done((bf16[8,1536]{1,0:T(8,128)(2,1)S(1)}, bf16[8,1536]{1,0:T(8,128)(2,1)S(1)}, u32[]{:S(2)}, u32[]{:S(2)}) %collective-permute-start.9) | collective-permute-done | bytes 24608 | tf_op jit(solution)/shard_map/ppermute | solution.py:148
  26.9 0.7 collective-permute-start.12
  27.6 1.0 %collective-permute-start.11 = (bf16[2,8,1152]{2,1,0:T(8,128)(2,1)S(1)}, bf16[2,8,1152]{2,1,0:T(8,128)(2,1)S(1)}, u32[]{:S(2)}, u32[]{:S(2)}) collective-permute-start(bf16[2,8,1152]{2,1,0:T(8,128)(2,1)S(1)} %get-tuple-element.56), channel_id=1, source_target_pairs={{0,8},{1,9},{2,10},{3,11},{4,12},{5,13},{6,14},{7,15},{8,0},{9,1},... | collective-permute-start | bytes 110600 | tf_op jit(solution)/shard_map/ppermute | solution.py:152
  28.6 0.0 collective-permute-start.10
  28.6 8.6 %all-to-all-start = ((bf16[16,128,1024]{2,1,0:T(8,128)(2,1)}), bf16[16,128,1024]{2,1,0:T(8,128)(2,1)}, u32[]{:S(2)}, u32[]{:S(2)}) async-start(bf16[16,128,1024]{2,1,0:T(8,128)(2,1)} %bitcast.86), calls=%async_computation | async-start | bytes 8388608 | tf_op jit(solution)/shard_map/all_to_all | solution.py:226
  37.3 0.7 multiply_subtract_fusion
  38.0 0.7 multiply_subtract_fusion.1
  38.6 0.0 collective-permute-done.12
  38.6 0.0 collective-permute-done.11
  38.6 0.0 collective-permute-done.10
  38.7 0.7 pad_maximum_fusion.1
  39.3 1.6 %shard_map.144 = bf16[64,1024]{1,0:T(8,128)(2,1)} custom-call(bf16[64,1024]{1,0:T(8,128)(2,1)} %bitcast.90), custom_call_target="tpu_custom_call" | custom-call | flops 99999997952 | bytes 262144 | tf_op jit(solution)/shard_map/pallas_call | solution.py:132
  40.9 2.9 %collective-permute-start.13 = (bf16[4,2,8,1024]{3,2,1,0:T(8,128)(2,1)}, bf16[4,2,8,1024]{3,2,1,0:T(8,128)(2,1)S(1)}, u32[]{:S(2)}, u32[]{:S(2)}) collective-permute-start(bf16[4,2,8,1024]{3,2,1,0:T(8,128)(2,1)} %bitcast.91), channel_id=1, source_target_pairs={{0,66},{1,67},{2,64},{3,65},{4,70},{5,71},{6,68},{7,69},{8,74},{9,... | collective-permute-start | bytes 393224 | tf_op jit(solution)/shard_map/ppermute | solution.py:176
  43.8 3.9 %collective-permute-done.13 = bf16[4,2,8,1024]{3,2,1,0:T(8,128)(2,1)S(1)} collective-permute-done((bf16[4,2,8,1024]{3,2,1,0:T(8,128)(2,1)}, bf16[4,2,8,1024]{3,2,1,0:T(8,128)(2,1)S(1)}, u32[]{:S(2)}, u32[]{:S(2)}) %collective-permute-start.13) | collective-permute-done | bytes 131104 | tf_op jit(solution)/shard_map/ppermute | solution.py:176
  47.7 0.9 %maximum_bitcast_fusion.refs_0_ = bf16[4,2,16,1024]{3,2,1,0:T(8,128)(2,1)S(1)} fusion(bf16[4,2,1,8,1024]{4,3,2,1,0:T(8,128)(2,1)S(1)} %reverse_bitcast_fusion, bf16[4,2,1,8,1024]{4,3,2,1,0:T(8,128)(2,1)} %bitcast.92), kind=kLoop, calls=%fused_computation | loop fusion | flops 131072 | bytes 524288 | tf_op jit(solution)/shard_map/reshape | solution.py:230
  48.7 1.5 %collective-permute-start.14 = (bf16[4,2,16,1024]{3,2,1,0:T(8,128)(2,1)S(1)}, bf16[4,2,16,1024]{3,2,1,0:T(8,128)(2,1)S(1)}, u32[]{:S(2)}, u32[]{:S(2)}) collective-permute-start(bf16[4,2,16,1024]{3,2,1,0:T(8,128)(2,1)S(1)} %maximum_bitcast_fusion.refs_0_), channel_id=1, source_target_pairs={{0,16},{16,32},{32,48},{48,0},{64,80},{80,96},{96,112},{112,64},{1... | collective-permute-start | bytes 786440 | tf_op jit(solution)/shard_map/ppermute | solution.py:180
  50.1 1.7 %collective-permute-start.15 = (bf16[4,2,16,1024]{3,2,1,0:T(8,128)(2,1)S(1)}, bf16[4,2,16,1024]{3,2,1,0:T(8,128)(2,1)S(1)}, u32[]{:S(2)}, u32[]{:S(2)}) collective-permute-start(bf16[4,2,16,1024]{3,2,1,0:T(8,128)(2,1)S(1)} %maximum_bitcast_fusion.refs_0_), channel_id=1, source_target_pairs={{0,32},{16,48},{32,0},{48,16},{64,96},{80,112},{96,64},{112,80},{1... | collective-permute-start | bytes 786440 | tf_op jit(solution)/shard_map/ppermute | solution.py:180
  51.9 0.8 collective-permute-start.16
  52.6 1.8 %collective-permute-start.17 = (bf16[4,2,16,1024]{3,2,1,0:T(8,128)(2,1)S(1)}, bf16[4,2,16,1024]{3,2,1,0:T(8,128)(2,1)S(1)}, u32[]{:S(2)}, u32[]{:S(2)}) collective-permute-start(bf16[4,2,16,1024]{3,2,1,0:T(8,128)(2,1)S(1)} %maximum_bitcast_fusion.refs_0_), channel_id=1, source_target_pairs={{0,1},{1,0},{2,3},{3,2},{4,5},{5,4},{6,7},{7,6},{8,9},{9,8},{10,11... | collective-permute-start | bytes 786440 | tf_op jit(solution)/shard_map/ppermute | solution.py:144
  54.4 2.7 %collective-permute-done.14.refs_1_ = bf16[4,2,16,1024]{3,2,1,0:T(8,128)(2,1)S(1)} collective-permute-done((bf16[4,2,16,1024]{3,2,1,0:T(8,128)(2,1)S(1)}, bf16[4,2,16,1024]{3,2,1,0:T(8,128)(2,1)S(1)}, u32[]{:S(2)}, u32[]{:S(2)}) %collective-permute-start.14) | collective-permute-done | bytes 262176 | tf_op jit(solution)/shard_map/ppermute | solution.py:180
  57.1 2.6 %collective-permute-start.18 = (bf16[4,2,16,1024]{3,2,1,0:T(8,128)(2,1)S(1)}, bf16[4,2,16,1024]{3,2,1,0:T(8,128)(2,1)S(1)}, u32[]{:S(2)}, u32[]{:S(2)}) collective-permute-start(bf16[4,2,16,1024]{3,2,1,0:T(8,128)(2,1)S(1)} %collective-permute-done.14.refs_1_), channel_id=1, source_target_pairs={{0,1},{1,0},{2,3},{3,2},{4,5},{5,4},{6,7},{7,6},{8,9},{9,8},{10,11... | collective-permute-start | bytes 786440 | tf_op jit(solution)/shard_map/ppermute | solution.py:144
  59.7 3.2 %collective-permute-done.15.refs_2_ = bf16[4,2,16,1024]{3,2,1,0:T(8,128)(2,1)S(1)} collective-permute-done((bf16[4,2,16,1024]{3,2,1,0:T(8,128)(2,1)S(1)}, bf16[4,2,16,1024]{3,2,1,0:T(8,128)(2,1)S(1)}, u32[]{:S(2)}, u32[]{:S(2)}) %collective-permute-start.15) | collective-permute-done | bytes 262176 | tf_op jit(solution)/shard_map/ppermute | solution.py:180
  62.9 1.8 %collective-permute-start.19 = (bf16[4,2,16,1024]{3,2,1,0:T(8,128)(2,1)S(1)}, bf16[4,2,16,1024]{3,2,1,0:T(8,128)(2,1)S(1)}, u32[]{:S(2)}, u32[]{:S(2)}) collective-permute-start(bf16[4,2,16,1024]{3,2,1,0:T(8,128)(2,1)S(1)} %collective-permute-done.15.refs_2_), channel_id=1, source_target_pairs={{0,1},{1,0},{2,3},{3,2},{4,5},{5,4},{6,7},{7,6},{8,9},{9,8},{10,11... | collective-permute-start | bytes 786440 | tf_op jit(solution)/shard_map/ppermute | solution.py:144
  64.7 0.0 collective-permute-done.16.refs_3_
  64.7 0.2 collective-permute-start.20
  64.9 1.0 %collective-permute-done.19.refs_6_ = bf16[4,2,16,1024]{3,2,1,0:T(8,128)(2,1)S(1)} collective-permute-done((bf16[4,2,16,1024]{3,2,1,0:T(8,128)(2,1)S(1)}, bf16[4,2,16,1024]{3,2,1,0:T(8,128)(2,1)S(1)}, u32[]{:S(2)}, u32[]{:S(2)}) %collective-permute-start.19) | collective-permute-done | bytes 262176 | tf_op jit(solution)/shard_map/ppermute | solution.py:144
  65.9 0.4 collective-permute-done.20.refs_7_
  66.3 20.7 %all-to-all-done.refs_8_ = bf16[16,128,1024]{2,1,0:T(8,128)(2,1)} async-done(((bf16[16,128,1024]{2,1,0:T(8,128)(2,1)}), bf16[16,128,1024]{2,1,0:T(8,128)(2,1)}, u32[]{:S(2)}, u32[]{:S(2)}) %all-to-all-start) | async-done | bytes 4194336 | tf_op jit(solution)/shard_map/all_to_all | solution.py:226
  87.0 4.3 %shard_map.145 = bf16[8,128,2048]{2,1,0:T(8,128)(2,1)} custom-call(f32[64,128]{1,0:T(8,128)S(1)} %bitcast_convert_fusion.bt_ref, bf16[4,2,16,1024]{3,2,1,0:T(8,128)(2,1)S(1)} %maximum_bitcast_fusion.refs_0_, bf16[4,2,16,1024]{3,2,1,0:T(8,128)(2,1)S(1)} %collective-permute-done.14.refs_1_, bf16[4,2,16,1024]{3,2,1,0:T(8,128)(2,1)S(1)} %collective-permute-done.15.refs_2_, ...), custom_call_target="tpu_custom_call" | custom-call | flops 268435456 | bytes 10485760 | tf_op jit(solution)/shard_map/pallas_call | solution.py:107
  (48 shorter events, 0.5 us)
Async XLA Ops:
  0.6 19.7 %copy-start = (f32[4,2048]{1,0:T(4,128)S(1)}, f32[4,2048]{1,0:T(4,128)}, u32[]{:S(2)}) copy-start(f32[4,2048]{1,0:T(4,128)} %param.13) | copy-start | bytes 98308
  0.6 19.7 %copy-start.2 = (f32[4,2048]{1,0:T(4,128)S(1)}, f32[4,2048]{1,0:T(4,128)}, u32[]{:S(2)}) copy-start(f32[4,2048]{1,0:T(4,128)} %param.14) | copy-start | bytes 98308
  0.7 19.7 %copy-start.1 = (f32[4,2048]{1,0:T(4,128)S(1)}, f32[4,2048]{1,0:T(4,128)}, u32[]{:S(2)}) copy-start(f32[4,2048]{1,0:T(4,128)} %param.15) | copy-start | bytes 98308
  0.7 22.6 %copy-start.3 = (f32[8,1024]{1,0:T(8,128)S(1)}, f32[8,1024]{1,0:T(8,128)}, u32[]{:S(2)}) copy-start(f32[8,1024]{1,0:T(8,128)} %param.10) | copy-start | bytes 98308
  0.7 22.6 %copy-start.5 = (f32[8,1024]{1,0:T(8,128)S(1)}, f32[8,1024]{1,0:T(8,128)}, u32[]{:S(2)}) copy-start(f32[8,1024]{1,0:T(8,128)} %param.11) | copy-start | bytes 98308
  0.7 22.6 %copy-start.4 = (f32[8,1024]{1,0:T(8,128)S(1)}, f32[8,1024]{1,0:T(8,128)}, u32[]{:S(2)}) copy-start(f32[8,1024]{1,0:T(8,128)} %param.12) | copy-start | bytes 98308
  2.0 2.7 %collective-permute-start = (f32[4,2,4,2048]{3,2,1,0:T(4,128)S(1)}, f32[4,2,4,2048]{3,2,1,0:T(4,128)S(1)}, u32[]{:S(2)}, u32[]{:S(2)}) collective-permute-start(f32[4,2,4,2048]{3,2,1,0:T(4,128)S(1)} %get-tuple-element.22), channel_id=1, source_target_pairs={{0,1},{1,0},{2,3},{3,2},{4,5},{5,4},{6,7},{7,6},{8,9},{9,8},{10,11... | collective-permute-start | bytes 786440 | tf_op jit(solution)/shard_map/ppermute | solution.py:144
  4.8 7.4 %collective-permute-start.1 = (f32[2,2,4,2048]{3,2,1,0:T(4,128)S(1)}, f32[2,2,4,2048]{3,2,1,0:T(4,128)S(1)}, u32[]{:S(2)}, u32[]{:S(2)}) collective-permute-start(f32[2,2,4,2048]{3,2,1,0:T(4,128)S(1)} %pad_maximum_fusion), channel_id=1, source_target_pairs={{0,12},{1,13},{2,14},{3,15},{4,8},{5,9},{6,10},{7,11},{8,4},{9,5},... | collective-permute-start | bytes 393224 | tf_op jit(solution)/shard_map/ppermute | solution.py:160
  7.7 5.1 %collective-permute-start.5 = (f32[2,8,1024]{2,1,0:T(8,128)S(1)}, f32[2,8,1024]{2,1,0:T(8,128)S(1)}, u32[]{:S(2)}, u32[]{:S(2)}) collective-permute-start(f32[2,8,1024]{2,1,0:T(8,128)S(1)} %get-tuple-element.28), channel_id=1, source_target_pairs={{0,48},{16,0},{32,16},{48,32},{64,112},{80,64},{96,80},{112,96},{1... | collective-permute-start | bytes 196616 | tf_op jit(solution)/shard_map/ppermute | solution.py:180
  11.5 4.7 %collective-permute-start.6 = (f32[2,8,1024]{2,1,0:T(8,128)S(1)}, f32[2,8,1024]{2,1,0:T(8,128)S(1)}, u32[]{:S(2)}, u32[]{:S(2)}) collective-permute-start(f32[2,8,1024]{2,1,0:T(8,128)S(1)} %get-tuple-element.29), channel_id=1, source_target_pairs={{0,32},{16,48},{32,0},{48,16},{64,96},{80,112},{96,64},{112,80},{1... | collective-permute-start | bytes 196616 | tf_op jit(solution)/shard_map/ppermute | solution.py:180
  11.5 5.0 %collective-permute-start.7 = (f32[2,8,1024]{2,1,0:T(8,128)S(1)}, f32[2,8,1024]{2,1,0:T(8,128)S(1)}, u32[]{:S(2)}, u32[]{:S(2)}) collective-permute-start(f32[2,8,1024]{2,1,0:T(8,128)S(1)} %get-tuple-element.30), channel_id=1, source_target_pairs={{0,16},{16,32},{32,48},{48,0},{64,80},{80,96},{96,112},{112,64},{1... | collective-permute-start | bytes 196616 | tf_op jit(solution)/shard_map/ppermute | solution.py:180
  12.2 4.3 %collective-permute-start.2 = (f32[2,4,2048]{2,1,0:T(4,128)S(1)}, f32[2,4,2048]{2,1,0:T(4,128)S(1)}, u32[]{:S(2)}, u32[]{:S(2)}) collective-permute-start(f32[2,4,2048]{2,1,0:T(4,128)S(1)} %slice_bitcast_fusion), channel_id=1, source_target_pairs={{0,4},{1,5},{2,6},{3,7},{4,0},{5,1},{6,2},{7,3},{8,12},{9,13},{10,... | collective-permute-start | bytes 196616 | tf_op jit(solution)/shard_map/ppermute | solution.py:160
  16.6 3.7 %collective-permute-start.3 = (f32[4,2048]{1,0:T(4,128)S(1)}, f32[4,2048]{1,0:T(4,128)S(1)}, u32[]{:S(2)}, u32[]{:S(2)}) collective-permute-start(f32[4,2048]{1,0:T(4,128)S(1)} %dynamic-slice_bitcast_fusion.7), channel_id=1, source_target_pairs={{0,2},{1,3},{2,0},{3,1},{4,6},{5,7},{6,4},{7,5},{8,10},{9,11},{10,... | collective-permute-start | bytes 98312 | tf_op jit(solution)/shard_map/ppermute | solution.py:148
  17.9 5.4 %collective-permute-start.8 = (f32[8,1024]{1,0:T(8,128)S(1)}, f32[8,1024]{1,0:T(8,128)S(1)}, u32[]{:S(2)}, u32[]{:S(2)}) collective-permute-start(f32[8,1024]{1,0:T(8,128)S(1)} %dynamic-slice_bitcast_fusion.6), channel_id=1, source_target_pairs={{0,64},{16,80},{32,96},{48,112},{64,0},{80,16},{96,32},{112,48},{1... | collective-permute-start | bytes 98312 | tf_op jit(solution)/shard_map/ppermute | solution.py:172
  20.5 3.6 %collective-permute-start.4 = (bf16[4,2,4,128]{3,2,1,0:T(4,128)(2,1)S(1)}, bf16[4,2,4,128]{3,2,1,0:T(4,128)(2,1)S(1)}, u32[]{:S(2)}, u32[]{:S(2)}) collective-permute-start(bf16[4,2,4,128]{3,2,1,0:T(4,128)(2,1)S(1)} %bitcast.95), channel_id=1, source_target_pairs={{0,1},{1,0},{2,3},{3,2},{4,5},{5,4},{6,7},{7,6},{8,9},{9,8},{10,11... | collective-permute-start | bytes 24584 | tf_op jit(solution)/shard_map/ppermute | solution.py:144
  24.1 2.8 %collective-permute-start.9 = (bf16[8,1536]{1,0:T(8,128)(2,1)S(1)}, bf16[8,1536]{1,0:T(8,128)(2,1)S(1)}, u32[]{:S(2)}, u32[]{:S(2)}) collective-permute-start(bf16[8,1536]{1,0:T(8,128)(2,1)S(1)} %pad_maximum_fusion.7), channel_id=1, source_target_pairs={{0,2},{1,3},{2,0},{3,1},{4,6},{5,7},{6,4},{7,5},{8,10},{9,11},{10,... | collective-permute-start | bytes 73736 | tf_op jit(solution)/shard_map/ppermute | solution.py:148
  26.9 11.7 %collective-permute-start.12 = (bf16[2,8,1152]{2,1,0:T(8,128)(2,1)S(1)}, bf16[2,8,1152]{2,1,0:T(8,128)(2,1)S(1)}, u32[]{:S(2)}, u32[]{:S(2)}) collective-permute-start(bf16[2,8,1152]{2,1,0:T(8,128)(2,1)S(1)} %get-tuple-element.57), channel_id=1, source_target_pairs={{0,12},{1,13},{2,14},{3,15},{4,0},{5,1},{6,2},{7,3},{8,4},{9,5},{1... | collective-permute-start | bytes 110600 | tf_op jit(solution)/shard_map/ppermute | solution.py:152
  27.6 11.0 %collective-permute-start.11 = (bf16[2,8,1152]{2,1,0:T(8,128)(2,1)S(1)}, bf16[2,8,1152]{2,1,0:T(8,128)(2,1)S(1)}, u32[]{:S(2)}, u32[]{:S(2)}) collective-permute-start(bf16[2,8,1152]{2,1,0:T(8,128)(2,1)S(1)} %get-tuple-element.56), channel_id=1, source_target_pairs={{0,8},{1,9},{2,10},{3,11},{4,12},{5,13},{6,14},{7,15},{8,0},{9,1},... | collective-permute-start | bytes 110600 | tf_op jit(solution)/shard_map/ppermute | solution.py:152
  28.6 10.0 %collective-permute-start.10 = (bf16[2,8,1152]{2,1,0:T(8,128)(2,1)S(1)}, bf16[2,8,1152]{2,1,0:T(8,128)(2,1)S(1)}, u32[]{:S(2)}, u32[]{:S(2)}) collective-permute-start(bf16[2,8,1152]{2,1,0:T(8,128)(2,1)S(1)} %get-tuple-element.55), channel_id=1, source_target_pairs={{0,4},{1,5},{2,6},{3,7},{4,8},{5,9},{6,10},{7,11},{8,12},{9,13},{1... | collective-permute-start | bytes 110600 | tf_op jit(solution)/shard_map/ppermute | solution.py:152
  28.6 58.3 %all-to-all-start = ((bf16[16,128,1024]{2,1,0:T(8,128)(2,1)}), bf16[16,128,1024]{2,1,0:T(8,128)(2,1)}, u32[]{:S(2)}, u32[]{:S(2)}) async-start(bf16[16,128,1024]{2,1,0:T(8,128)(2,1)} %bitcast.86), calls=%async_computation | async-start | bytes 8388608 | tf_op jit(solution)/shard_map/all_to_all | solution.py:226
  40.9 6.8 %collective-permute-start.13 = (bf16[4,2,8,1024]{3,2,1,0:T(8,128)(2,1)}, bf16[4,2,8,1024]{3,2,1,0:T(8,128)(2,1)S(1)}, u32[]{:S(2)}, u32[]{:S(2)}) collective-permute-start(bf16[4,2,8,1024]{3,2,1,0:T(8,128)(2,1)} %bitcast.91), channel_id=1, source_target_pairs={{0,66},{1,67},{2,64},{3,65},{4,70},{5,71},{6,68},{7,69},{8,74},{9,... | collective-permute-start | bytes 393224 | tf_op jit(solution)/shard_map/ppermute | solution.py:176
  48.7 8.5 %collective-permute-start.14 = (bf16[4,2,16,1024]{3,2,1,0:T(8,128)(2,1)S(1)}, bf16[4,2,16,1024]{3,2,1,0:T(8,128)(2,1)S(1)}, u32[]{:S(2)}, u32[]{:S(2)}) collective-permute-start(bf16[4,2,16,1024]{3,2,1,0:T(8,128)(2,1)S(1)} %maximum_bitcast_fusion.refs_0_), channel_id=1, source_target_pairs={{0,16},{16,32},{32,48},{48,0},{64,80},{80,96},{96,112},{112,64},{1... | collective-permute-start | bytes 786440 | tf_op jit(solution)/shard_map/ppermute | solution.py:180
  50.1 12.8 %collective-permute-start.15 = (bf16[4,2,16,1024]{3,2,1,0:T(8,128)(2,1)S(1)}, bf16[4,2,16,1024]{3,2,1,0:T(8,128)(2,1)S(1)}, u32[]{:S(2)}, u32[]{:S(2)}) collective-permute-start(bf16[4,2,16,1024]{3,2,1,0:T(8,128)(2,1)S(1)} %maximum_bitcast_fusion.refs_0_), channel_id=1, source_target_pairs={{0,32},{16,48},{32,0},{48,16},{64,96},{80,112},{96,64},{112,80},{1... | collective-permute-start | bytes 786440 | tf_op jit(solution)/shard_map/ppermute | solution.py:180
  51.9 12.9 %collective-permute-start.16 = (bf16[4,2,16,1024]{3,2,1,0:T(8,128)(2,1)S(1)}, bf16[4,2,16,1024]{3,2,1,0:T(8,128)(2,1)S(1)}, u32[]{:S(2)}, u32[]{:S(2)}) collective-permute-start(bf16[4,2,16,1024]{3,2,1,0:T(8,128)(2,1)S(1)} %maximum_bitcast_fusion.refs_0_), channel_id=1, source_target_pairs={{0,48},{16,0},{32,16},{48,32},{64,112},{80,64},{96,80},{112,96},{1... | collective-permute-start | bytes 786440 | tf_op jit(solution)/shard_map/ppermute | solution.py:180
  52.6 12.3 %collective-permute-start.17 = (bf16[4,2,16,1024]{3,2,1,0:T(8,128)(2,1)S(1)}, bf16[4,2,16,1024]{3,2,1,0:T(8,128)(2,1)S(1)}, u32[]{:S(2)}, u32[]{:S(2)}) collective-permute-start(bf16[4,2,16,1024]{3,2,1,0:T(8,128)(2,1)S(1)} %maximum_bitcast_fusion.refs_0_), channel_id=1, source_target_pairs={{0,1},{1,0},{2,3},{3,2},{4,5},{5,4},{6,7},{7,6},{8,9},{9,8},{10,11... | collective-permute-start | bytes 786440 | tf_op jit(solution)/shard_map/ppermute | solution.py:144
  57.1 7.8 %collective-permute-start.18 = (bf16[4,2,16,1024]{3,2,1,0:T(8,128)(2,1)S(1)}, bf16[4,2,16,1024]{3,2,1,0:T(8,128)(2,1)S(1)}, u32[]{:S(2)}, u32[]{:S(2)}) collective-permute-start(bf16[4,2,16,1024]{3,2,1,0:T(8,128)(2,1)S(1)} %collective-permute-done.14.refs_1_), channel_id=1, source_target_pairs={{0,1},{1,0},{2,3},{3,2},{4,5},{5,4},{6,7},{7,6},{8,9},{9,8},{10,11... | collective-permute-start | bytes 786440 | tf_op jit(solution)/shard_map/ppermute | solution.py:144
  62.9 3.0 %collective-permute-start.19 = (bf16[4,2,16,1024]{3,2,1,0:T(8,128)(2,1)S(1)}, bf16[4,2,16,1024]{3,2,1,0:T(8,128)(2,1)S(1)}, u32[]{:S(2)}, u32[]{:S(2)}) collective-permute-start(bf16[4,2,16,1024]{3,2,1,0:T(8,128)(2,1)S(1)} %collective-permute-done.15.refs_2_), channel_id=1, source_target_pairs={{0,1},{1,0},{2,3},{3,2},{4,5},{5,4},{6,7},{7,6},{8,9},{9,8},{10,11... | collective-permute-start | bytes 786440 | tf_op jit(solution)/shard_map/ppermute | solution.py:144
  64.7 1.5 %collective-permute-start.20 = (bf16[4,2,16,1024]{3,2,1,0:T(8,128)(2,1)S(1)}, bf16[4,2,16,1024]{3,2,1,0:T(8,128)(2,1)S(1)}, u32[]{:S(2)}, u32[]{:S(2)}) collective-permute-start(bf16[4,2,16,1024]{3,2,1,0:T(8,128)(2,1)S(1)} %collective-permute-done.16.refs_3_), channel_id=1, source_target_pairs={{0,1},{1,0},{2,3},{3,2},{4,5},{5,4},{6,7},{7,6},{8,9},{9,8},{10,11... | collective-permute-start | bytes 786440 | tf_op jit(solution)/shard_map/ppermute | solution.py:144

commit v8 on v7

--- a/solution.py
+++ b/solution.py
@@ -49,11 +49,26 @@
     return (rank_a == rank_b).astype(jnp.bfloat16)
 
 
-def merge_kernel(bt_ref, *refs):
+def reorder_kernel(bt_ref, left_ref):
+    row, col = lax.axis_index("row"), lax.axis_index("col")
+    x_hi, z = row // 4, row % 4
+    y, x, core = col // 4, (col // 2) % 2, col % 2
+    left_ref[...] = lax.dot_general(
+        bt_ref[...].astype(jnp.bfloat16),
+        rank_order(y, x, core, x_hi, z),
+        (((0,), (1,)), ((), ())),
+        preferred_element_type=jnp.float32,
+    ).astype(jnp.bfloat16)
+
+
+def reorder(bt_rows):
+    return pl.pallas_call(reorder_kernel, out_shape=jax.ShapeDtypeStruct((128, R), jnp.bfloat16))(bt_rows)
+
+
+def merge_kernel(left_ref, *refs):
     a_refs, arrived_ref, saved_ref = refs[:8], refs[8], refs[9]
     a_buf, in_buf, out_buf, a_sem, in_sem, out_sem = refs[10:]
-    row, col = lax.axis_index("row"), lax.axis_index("col")
-    x_hi, z = row // 4, row % 4
+    col = lax.axis_index("col")
     y, x, core = col // 4, (col // 2) % 2, col % 2
 
     def source(step):
@@ -75,12 +90,7 @@
     ]
     for copy in a_copies[:4] + in_copies[:8] + a_copies[4:] + in_copies[8:]:
         copy.start()
-    left = lax.dot_general(
-        bt_ref[...].astype(jnp.bfloat16),
-        rank_order(y, x, core, x_hi, z),
-        (((0,), (1,)), ((), ())),
-        preferred_element_type=jnp.float32,
-    ).astype(jnp.bfloat16)
+    left = left_ref[...]
     for copy in a_copies:
         copy.wait()
     for first in range(0, 16, 4):
@@ -103,7 +113,7 @@
         copy.wait()
 
 
-def merge(bt_rows, a_parts, arrived):
+def merge(left, a_parts, arrived):
     return pl.pallas_call(
         merge_kernel,
         in_specs=[pl.BlockSpec(memory_space=pltpu.VMEM)] + [pl.BlockSpec(memory_space=pl.ANY)] * 9,
@@ -121,7 +131,7 @@
         cost_estimate=pl.CostEstimate(
             flops=2 * 128 * 64 * 16384, bytes_accessed=10 << 20, transcendentals=0
         ),
-    )(bt_rows, *a_parts, arrived)
+    )(left, *a_parts, arrived)
 
 
 def hold_kernel(array_ref, held_ref):
@@ -230,7 +240,7 @@
     part = jnp.stack([part, over_x_hi_x(part)[:, ::-1]], axis=2).reshape(4, 2, 16, 1024)
     a_parts = [part] + [over_z(part, k) for k in (1, 2, 3)]
     a_parts = a_parts + [over_core(part) for part in a_parts]
-    saved = merge(bt_rows.reshape(R, 128).astype(jnp.float32), a_parts, arrived)
+    saved = merge(reorder(bt_rows.reshape(R, 128).astype(jnp.float32)), a_parts, arrived)
     a_new, a_first_new, a_second_new = adam_step(a_master, a_first, a_second, grad_a)
     bt_new, bt_first_new, bt_second_new = adam_step(bt_master, bt_first, bt_second, grad_bt)
     return (saved, a_new, a_first_new, a_second_new, bt_new, bt_first_new, bt_second_new)

time: 91.5 us -> 92.4 us (level)
  waiting for transfers between devices: 38.5 us -> 36.3 us
  Pallas kernels: 5.83 us -> 7.37 us
    pallas_call x0 -> x1, Pallas kernels: none -> 1.55 us  [reorder(): pl.pallas_call(reorder_kernel, out_shape=jax.ShapeDtypeStruct((128, R), j...]
    ppermute x6, waiting for transfers between devices: 2.26 us -> 0.94 us  [over_core(): return lax.ppermute(array, 'col', [(i, i ^ 1) for i in range(16)])]
  transfers between devices with their start and end apart: 22 -> 22, of which waited for: 12 -> 10; matrix products, arithmetic and copies ran while one was open for 5% -> 5% of each run, Pallas kernels for 2% -> 3%
where the time goes in v8:
time: 92.4 us; the launch traced here: 92 us
  starting transfers between devices  40.2 us (44%)
  waiting for transfers between devices  36.3 us (39%)
  Pallas kernels  7.37 us (8%)
  other arithmetic  3.93 us (4%)
  local copies, waits for them, and re-layouts  3.14 us (3%)
  between operations  0.99 us (1%)
    all_to_all x1, waiting for transfers between devices, per_device(): arrived = lax.all_to_all(weight, 'col', 0, 0, tiled=True)  19.9 us
    ppermute x6, starting transfers between devices, over_core(): return lax.ppermute(array, 'col', [(i, i ^ 1) for i in range(16)])  10.6 us
    ppermute x6, waiting for transfers between devices, over_z(): lax.ppermute(array, 'row', [(i, i // 4 * 4 + (i + k) % 4) for i in range(...  10.1 us
    all_to_all x1, starting transfers between devices, per_device(): arrived = lax.all_to_all(weight, 'col', 0, 0, tiled=True)  8.64 us
    ppermute x6, starting transfers between devices, over_z(): lax.ppermute(array, 'row', [(i, i // 4 * 4 + (i + k) % 4) for i in range(...  8.41 us
    pallas_call x1, Pallas kernels, merge(): pl.pallas_call(merge_kernel, in_specs=[pl.BlockSpec(memory_space=pltpu.VM...  4.25 us
    ppermute x1, waiting for transfers between devices, over_x_hi_x(): lax.ppermute(array, ('row', 'col'), [(i, i ^ 4 * 16 + 2) for i in range(1...  3.89 us
    ppermute x2, starting transfers between devices, over_col(): return lax.ppermute(array, 'col', [(i, i ^ mask) for i in range(16)])  2.98 us
  transfers between devices with their start and end apart: 22, of which 10 were waited for; matrix products, arithmetic and copies ran while one was open for 5% of the time, Pallas kernels for 3%

profile of v8, /device:TPU:1, one launch (start us, length us, event | category | flops | bytes accessed | tf_op | source)
XLA Modules:
  0.0 92.0 jit_solution(15448898938079841896)
XLA Ops:
  0.7 1.2 %reshape.44 = f32[4,2,2,4,2048]{4,3,2,1,0:T(4,128)S(1)} reshape(f32[1,64,2048]{2,1,0:T(8,128)} %param.17) | data formatting | bytes 1048576 | tf_op jit(solution)/shard_map/reshape | solution.py:208
  2.0 1.5 %collective-permute-start = (f32[4,2,4,2048]{3,2,1,0:T(4,128)S(1)}, f32[4,2,4,2048]{3,2,1,0:T(4,128)S(1)}, u32[]{:S(2)}, u32[]{:S(2)}) collective-permute-start(f32[4,2,4,2048]{3,2,1,0:T(4,128)S(1)} %get-tuple-element.22), channel_id=1, source_target_pairs={{0,1},{1,0},{2,3},{3,2},{4,5},{5,4},{6,7},{7,6},{8,9},{9,8},{10,11... | collective-permute-start | bytes 786440 | tf_op jit(solution)/shard_map/ppermute | solution.py:154
  3.5 1.0 %dynamic-slice_bitcast_fusion.2 = (f32[2,8,1024]{2,1,0:T(8,128)S(1)}, f32[2,8,1024]{2,1,0:T(8,128)S(1)}, f32[2,8,1024]{2,1,0:T(8,128)S(1)}, f32[2,8,1024]{2,1,0:T(8,128)S(1)}) fusion(f32[2,4,8,1024]{3,2,1,0:T(8,128)} %bitcast.87, s32[]{:T(128)S(6)} %select_n.128, s32[]{:T(128)S(6)} %select_n.126, s32[]{:T(128)S(6)} %select_n.124, s32[]{:T(128)S(6)} %select_n.122), kind=kLoop, calls=%fused_computation.11 | loop fusion | bytes 524304 | tf_op jit(solution)/shard_map/jit(dynamic_index_in_dim)/squeeze | solution.py:150
  4.5 0.2 collective-permute-done
  4.7 0.1 add.182
  4.8 2.9 %collective-permute-start.1 = (f32[2,2,4,2048]{3,2,1,0:T(4,128)S(1)}, f32[2,2,4,2048]{3,2,1,0:T(4,128)S(1)}, u32[]{:S(2)}, u32[]{:S(2)}) collective-permute-start(f32[2,2,4,2048]{3,2,1,0:T(4,128)S(1)} %pad_maximum_fusion), channel_id=1, source_target_pairs={{0,12},{1,13},{2,14},{3,15},{4,8},{5,9},{6,10},{7,11},{8,4},{9,5},... | collective-permute-start | bytes 393224 | tf_op jit(solution)/shard_map/ppermute | solution.py:170
  7.7 3.8 %collective-permute-start.5 = (f32[2,8,1024]{2,1,0:T(8,128)S(1)}, f32[2,8,1024]{2,1,0:T(8,128)S(1)}, u32[]{:S(2)}, u32[]{:S(2)}) collective-permute-start(f32[2,8,1024]{2,1,0:T(8,128)S(1)} %get-tuple-element.28), channel_id=1, source_target_pairs={{0,48},{16,0},{32,16},{48,32},{64,112},{80,64},{96,80},{112,96},{1... | collective-permute-start | bytes 196616 | tf_op jit(solution)/shard_map/ppermute | solution.py:190
  11.5 0.0 collective-permute-start.6
  11.5 0.7 collective-permute-start.7
  12.2 0.0 collective-permute-done.1
  12.2 0.1 collective-permute-start.2
  12.3 0.5 collective-permute-done.5
  12.8 3.4 %collective-permute-done.6 = f32[2,8,1024]{2,1,0:T(8,128)S(1)} collective-permute-done((f32[2,8,1024]{2,1,0:T(8,128)S(1)}, f32[2,8,1024]{2,1,0:T(8,128)S(1)}, u32[]{:S(2)}, u32[]{:S(2)}) %collective-permute-start.6) | collective-permute-done | bytes 65568 | tf_op jit(solution)/shard_map/ppermute | solution.py:190
  16.2 0.3 collective-permute-done.7
  16.5 0.0 collective-permute-done.2
  16.6 1.3 %collective-permute-start.3 = (f32[4,2048]{1,0:T(4,128)S(1)}, f32[4,2048]{1,0:T(4,128)S(1)}, u32[]{:S(2)}, u32[]{:S(2)}) collective-permute-start(f32[4,2048]{1,0:T(4,128)S(1)} %dynamic-slice_bitcast_fusion.7), channel_id=1, source_target_pairs={{0,2},{1,3},{2,0},{3,1},{4,6},{5,7},{6,4},{7,5},{8,10},{9,11},{10,... | collective-permute-start | bytes 98312 | tf_op jit(solution)/shard_map/ppermute | solution.py:158
  17.9 2.5 %collective-permute-start.8 = (f32[8,1024]{1,0:T(8,128)S(1)}, f32[8,1024]{1,0:T(8,128)S(1)}, u32[]{:S(2)}, u32[]{:S(2)}) collective-permute-start(f32[8,1024]{1,0:T(8,128)S(1)} %dynamic-slice_bitcast_fusion.6), channel_id=1, source_target_pairs={{0,64},{16,80},{32,96},{48,112},{64,0},{80,16},{96,32},{112,48},{1... | collective-permute-start | bytes 98312 | tf_op jit(solution)/shard_map/ppermute | solution.py:182
  20.3 0.0 collective-permute-done.3
  20.3 0.1 multiply_subtract_fusion.2
  20.5 2.7 %collective-permute-start.4 = (bf16[4,2,4,128]{3,2,1,0:T(4,128)(2,1)S(1)}, bf16[4,2,4,128]{3,2,1,0:T(4,128)(2,1)S(1)}, u32[]{:S(2)}, u32[]{:S(2)}) collective-permute-start(bf16[4,2,4,128]{3,2,1,0:T(4,128)(2,1)S(1)} %bitcast.95), channel_id=1, source_target_pairs={{0,1},{1,0},{2,3},{3,2},{4,5},{5,4},{6,7},{7,6},{8,9},{9,8},{10,11... | collective-permute-start | bytes 24584 | tf_op jit(solution)/shard_map/ppermute | solution.py:154
  23.2 0.0 collective-permute-done.8
  23.3 0.7 collective-permute-done.4
  24.1 1.2 %collective-permute-start.9 = (bf16[8,1536]{1,0:T(8,128)(2,1)S(1)}, bf16[8,1536]{1,0:T(8,128)(2,1)S(1)}, u32[]{:S(2)}, u32[]{:S(2)}) collective-permute-start(bf16[8,1536]{1,0:T(8,128)(2,1)S(1)} %pad_maximum_fusion.7), channel_id=1, source_target_pairs={{0,2},{1,3},{2,0},{3,1},{4,6},{5,7},{6,4},{7,5},{8,10},{9,11},{10,... | collective-permute-start | bytes 73736 | tf_op jit(solution)/shard_map/ppermute | solution.py:158
  25.3 1.5 %collective-permute-done.9 = bf16[8,1536]{1,0:T(8,128)(2,1)S(1)} collective-permute-done((bf16[8,1536]{1,0:T(8,128)(2,1)S(1)}, bf16[8,1536]{1,0:T(8,128)(2,1)S(1)}, u32[]{:S(2)}, u32[]{:S(2)}) %collective-permute-start.9) | collective-permute-done | bytes 24608 | tf_op jit(solution)/shard_map/ppermute | solution.py:158
  26.9 0.7 collective-permute-start.12
  27.6 1.0 %collective-permute-start.11 = (bf16[2,8,1152]{2,1,0:T(8,128)(2,1)S(1)}, bf16[2,8,1152]{2,1,0:T(8,128)(2,1)S(1)}, u32[]{:S(2)}, u32[]{:S(2)}) collective-permute-start(bf16[2,8,1152]{2,1,0:T(8,128)(2,1)S(1)} %get-tuple-element.56), channel_id=1, source_target_pairs={{0,8},{1,9},{2,10},{3,11},{4,12},{5,13},{6,14},{7,15},{8,0},{9,1},... | collective-permute-start | bytes 110600 | tf_op jit(solution)/shard_map/ppermute | solution.py:162
  28.6 8.6 %all-to-all-start = ((bf16[16,128,1024]{2,1,0:T(8,128)(2,1)}), bf16[16,128,1024]{2,1,0:T(8,128)(2,1)}, u32[]{:S(2)}, u32[]{:S(2)}) async-start(bf16[16,128,1024]{2,1,0:T(8,128)(2,1)} %bitcast.86), calls=%async_computation | async-start | bytes 8388608 | tf_op jit(solution)/shard_map/all_to_all | solution.py:236
  37.3 0.7 multiply_subtract_fusion
  38.0 0.7 multiply_subtract_fusion.1
  38.7 0.7 pad_maximum_fusion.1
  39.3 1.6 %shard_map.145 = bf16[64,1024]{1,0:T(8,128)(2,1)} custom-call(bf16[64,1024]{1,0:T(8,128)(2,1)} %bitcast.90), custom_call_target="tpu_custom_call" | custom-call | flops 99999997952 | bytes 262144 | tf_op jit(solution)/shard_map/pallas_call | solution.py:142
  40.9 2.9 %collective-permute-start.13 = (bf16[4,2,8,1024]{3,2,1,0:T(8,128)(2,1)}, bf16[4,2,8,1024]{3,2,1,0:T(8,128)(2,1)S(1)}, u32[]{:S(2)}, u32[]{:S(2)}) collective-permute-start(bf16[4,2,8,1024]{3,2,1,0:T(8,128)(2,1)} %bitcast.91), channel_id=1, source_target_pairs={{0,66},{1,67},{2,64},{3,65},{4,70},{5,71},{6,68},{7,69},{8,74},{9,... | collective-permute-start | bytes 393224 | tf_op jit(solution)/shard_map/ppermute | solution.py:186
  43.8 3.9 %collective-permute-done.13 = bf16[4,2,8,1024]{3,2,1,0:T(8,128)(2,1)S(1)} collective-permute-done((bf16[4,2,8,1024]{3,2,1,0:T(8,128)(2,1)}, bf16[4,2,8,1024]{3,2,1,0:T(8,128)(2,1)S(1)}, u32[]{:S(2)}, u32[]{:S(2)}) %collective-permute-start.13) | collective-permute-done | bytes 131104 | tf_op jit(solution)/shard_map/ppermute | solution.py:186
  47.7 0.9 %maximum_bitcast_fusion.refs_0_ = bf16[4,2,16,1024]{3,2,1,0:T(8,128)(2,1)S(1)} fusion(bf16[4,2,1,8,1024]{4,3,2,1,0:T(8,128)(2,1)S(1)} %reverse_bitcast_fusion, bf16[4,2,1,8,1024]{4,3,2,1,0:T(8,128)(2,1)} %bitcast.92), kind=kLoop, calls=%fused_computation | loop fusion | flops 131072 | bytes 524288 | tf_op jit(solution)/shard_map/reshape | solution.py:240
  48.7 1.5 %collective-permute-start.14 = (bf16[4,2,16,1024]{3,2,1,0:T(8,128)(2,1)S(1)}, bf16[4,2,16,1024]{3,2,1,0:T(8,128)(2,1)S(1)}, u32[]{:S(2)}, u32[]{:S(2)}) collective-permute-start(bf16[4,2,16,1024]{3,2,1,0:T(8,128)(2,1)S(1)} %maximum_bitcast_fusion.refs_0_), channel_id=1, source_target_pairs={{0,16},{16,32},{32,48},{48,0},{64,80},{80,96},{96,112},{112,64},{1... | collective-permute-start | bytes 786440 | tf_op jit(solution)/shard_map/ppermute | solution.py:190
  50.1 1.7 %collective-permute-start.15 = (bf16[4,2,16,1024]{3,2,1,0:T(8,128)(2,1)S(1)}, bf16[4,2,16,1024]{3,2,1,0:T(8,128)(2,1)S(1)}, u32[]{:S(2)}, u32[]{:S(2)}) collective-permute-start(bf16[4,2,16,1024]{3,2,1,0:T(8,128)(2,1)S(1)} %maximum_bitcast_fusion.refs_0_), channel_id=1, source_target_pairs={{0,32},{16,48},{32,0},{48,16},{64,96},{80,112},{96,64},{112,80},{1... | collective-permute-start | bytes 786440 | tf_op jit(solution)/shard_map/ppermute | solution.py:190
  51.9 0.7 collective-permute-start.16
  52.6 1.8 %collective-permute-start.17 = (bf16[4,2,16,1024]{3,2,1,0:T(8,128)(2,1)S(1)}, bf16[4,2,16,1024]{3,2,1,0:T(8,128)(2,1)S(1)}, u32[]{:S(2)}, u32[]{:S(2)}) collective-permute-start(bf16[4,2,16,1024]{3,2,1,0:T(8,128)(2,1)S(1)} %maximum_bitcast_fusion.refs_0_), channel_id=1, source_target_pairs={{0,1},{1,0},{2,3},{3,2},{4,5},{5,4},{6,7},{7,6},{8,9},{9,8},{10,11... | collective-permute-start | bytes 786440 | tf_op jit(solution)/shard_map/ppermute | solution.py:154
  54.4 2.7 %collective-permute-done.14.refs_1_ = bf16[4,2,16,1024]{3,2,1,0:T(8,128)(2,1)S(1)} collective-permute-done((bf16[4,2,16,1024]{3,2,1,0:T(8,128)(2,1)S(1)}, bf16[4,2,16,1024]{3,2,1,0:T(8,128)(2,1)S(1)}, u32[]{:S(2)}, u32[]{:S(2)}) %collective-permute-start.14) | collective-permute-done | bytes 262176 | tf_op jit(solution)/shard_map/ppermute | solution.py:190
  57.1 2.6 %collective-permute-start.18 = (bf16[4,2,16,1024]{3,2,1,0:T(8,128)(2,1)S(1)}, bf16[4,2,16,1024]{3,2,1,0:T(8,128)(2,1)S(1)}, u32[]{:S(2)}, u32[]{:S(2)}) collective-permute-start(bf16[4,2,16,1024]{3,2,1,0:T(8,128)(2,1)S(1)} %collective-permute-done.14.refs_1_), channel_id=1, source_target_pairs={{0,1},{1,0},{2,3},{3,2},{4,5},{5,4},{6,7},{7,6},{8,9},{9,8},{10,11... | collective-permute-start | bytes 786440 | tf_op jit(solution)/shard_map/ppermute | solution.py:154
  59.7 3.2 %collective-permute-done.15.refs_2_ = bf16[4,2,16,1024]{3,2,1,0:T(8,128)(2,1)S(1)} collective-permute-done((bf16[4,2,16,1024]{3,2,1,0:T(8,128)(2,1)S(1)}, bf16[4,2,16,1024]{3,2,1,0:T(8,128)(2,1)S(1)}, u32[]{:S(2)}, u32[]{:S(2)}) %collective-permute-start.15) | collective-permute-done | bytes 262176 | tf_op jit(solution)/shard_map/ppermute | solution.py:190
  62.9 1.8 %collective-permute-start.19 = (bf16[4,2,16,1024]{3,2,1,0:T(8,128)(2,1)S(1)}, bf16[4,2,16,1024]{3,2,1,0:T(8,128)(2,1)S(1)}, u32[]{:S(2)}, u32[]{:S(2)}) collective-permute-start(bf16[4,2,16,1024]{3,2,1,0:T(8,128)(2,1)S(1)} %collective-permute-done.15.refs_2_), channel_id=1, source_target_pairs={{0,1},{1,0},{2,3},{3,2},{4,5},{5,4},{6,7},{7,6},{8,9},{9,8},{10,11... | collective-permute-start | bytes 786440 | tf_op jit(solution)/shard_map/ppermute | solution.py:154
  64.7 0.2 collective-permute-start.20
  64.9 0.6 bitcast_convert_fusion.bt_ref
  65.5 1.5 %shard_map.144.left_ref = bf16[128,64]{1,0:T(8,128)(2,1)} custom-call(f32[64,128]{1,0:T(8,128)} %bitcast_convert_fusion.bt_ref), custom_call_target="tpu_custom_call" | custom-call | tf_op jit(solution)/shard_map/pallas_call | solution.py:65
  67.1 19.9 %all-to-all-done.refs_8_ = bf16[16,128,1024]{2,1,0:T(8,128)(2,1)} async-done(((bf16[16,128,1024]{2,1,0:T(8,128)(2,1)}), bf16[16,128,1024]{2,1,0:T(8,128)(2,1)}, u32[]{:S(2)}, u32[]{:S(2)}) %all-to-all-start) | async-done | bytes 4194336 | tf_op jit(solution)/shard_map/all_to_all | solution.py:236
  87.0 0.8 copy-done
  87.7 4.3 %shard_map.146 = bf16[8,128,2048]{2,1,0:T(8,128)(2,1)} custom-call(bf16[128,64]{1,0:T(8,128)(2,1)S(1)} %copy-done, bf16[4,2,16,1024]{3,2,1,0:T(8,128)(2,1)S(1)} %maximum_bitcast_fusion.refs_0_, bf16[4,2,16,1024]{3,2,1,0:T(8,128)(2,1)S(1)} %collective-permute-done.14.refs_1_, bf16[4,2,16,1024]{3,2,1,0:T(8,128)(2,1)S(1)} %collective-permute-done.15.refs_2_, ...), custom_call_target="tpu_custom_call" | custom-call | flops 268435456 | bytes 10485760 | tf_op jit(solution)/shard_map/pallas_call | solution.py:117
  (51 shorter events, 0.5 us)
Async XLA Ops:
  0.6 19.7 %copy-start.1 = (f32[4,2048]{1,0:T(4,128)S(1)}, f32[4,2048]{1,0:T(4,128)}, u32[]{:S(2)}) copy-start(f32[4,2048]{1,0:T(4,128)} %param.13) | copy-start | bytes 98308
  0.6 19.7 %copy-start.3 = (f32[4,2048]{1,0:T(4,128)S(1)}, f32[4,2048]{1,0:T(4,128)}, u32[]{:S(2)}) copy-start(f32[4,2048]{1,0:T(4,128)} %param.14) | copy-start | bytes 98308
  0.7 19.7 %copy-start.2 = (f32[4,2048]{1,0:T(4,128)S(1)}, f32[4,2048]{1,0:T(4,128)}, u32[]{:S(2)}) copy-start(f32[4,2048]{1,0:T(4,128)} %param.15) | copy-start | bytes 98308
  0.7 22.6 %copy-start.4 = (f32[8,1024]{1,0:T(8,128)S(1)}, f32[8,1024]{1,0:T(8,128)}, u32[]{:S(2)}) copy-start(f32[8,1024]{1,0:T(8,128)} %param.10) | copy-start | bytes 98308
  0.7 22.6 %copy-start.6 = (f32[8,1024]{1,0:T(8,128)S(1)}, f32[8,1024]{1,0:T(8,128)}, u32[]{:S(2)}) copy-start(f32[8,1024]{1,0:T(8,128)} %param.11) | copy-start | bytes 98308
  0.7 22.6 %copy-start.5 = (f32[8,1024]{1,0:T(8,128)S(1)}, f32[8,1024]{1,0:T(8,128)}, u32[]{:S(2)}) copy-start(f32[8,1024]{1,0:T(8,128)} %param.12) | copy-start | bytes 98308
  2.0 2.7 %collective-permute-start = (f32[4,2,4,2048]{3,2,1,0:T(4,128)S(1)}, f32[4,2,4,2048]{3,2,1,0:T(4,128)S(1)}, u32[]{:S(2)}, u32[]{:S(2)}) collective-permute-start(f32[4,2,4,2048]{3,2,1,0:T(4,128)S(1)} %get-tuple-element.22), channel_id=1, source_target_pairs={{0,1},{1,0},{2,3},{3,2},{4,5},{5,4},{6,7},{7,6},{8,9},{9,8},{10,11... | collective-permute-start | bytes 786440 | tf_op jit(solution)/shard_map/ppermute | solution.py:154
  4.8 7.4 %collective-permute-start.1 = (f32[2,2,4,2048]{3,2,1,0:T(4,128)S(1)}, f32[2,2,4,2048]{3,2,1,0:T(4,128)S(1)}, u32[]{:S(2)}, u32[]{:S(2)}) collective-permute-start(f32[2,2,4,2048]{3,2,1,0:T(4,128)S(1)} %pad_maximum_fusion), channel_id=1, source_target_pairs={{0,12},{1,13},{2,14},{3,15},{4,8},{5,9},{6,10},{7,11},{8,4},{9,5},... | collective-permute-start | bytes 393224 | tf_op jit(solution)/shard_map/ppermute | solution.py:170
  7.7 5.1 %collective-permute-start.5 = (f32[2,8,1024]{2,1,0:T(8,128)S(1)}, f32[2,8,1024]{2,1,0:T(8,128)S(1)}, u32[]{:S(2)}, u32[]{:S(2)}) collective-permute-start(f32[2,8,1024]{2,1,0:T(8,128)S(1)} %get-tuple-element.28), channel_id=1, source_target_pairs={{0,48},{16,0},{32,16},{48,32},{64,112},{80,64},{96,80},{112,96},{1... | collective-permute-start | bytes 196616 | tf_op jit(solution)/shard_map/ppermute | solution.py:190
  11.5 4.7 %collective-permute-start.6 = (f32[2,8,1024]{2,1,0:T(8,128)S(1)}, f32[2,8,1024]{2,1,0:T(8,128)S(1)}, u32[]{:S(2)}, u32[]{:S(2)}) collective-permute-start(f32[2,8,1024]{2,1,0:T(8,128)S(1)} %get-tuple-element.29), channel_id=1, source_target_pairs={{0,32},{16,48},{32,0},{48,16},{64,96},{80,112},{96,64},{112,80},{1... | collective-permute-start | bytes 196616 | tf_op jit(solution)/shard_map/ppermute | solution.py:190
  11.5 5.0 %collective-permute-start.7 = (f32[2,8,1024]{2,1,0:T(8,128)S(1)}, f32[2,8,1024]{2,1,0:T(8,128)S(1)}, u32[]{:S(2)}, u32[]{:S(2)}) collective-permute-start(f32[2,8,1024]{2,1,0:T(8,128)S(1)} %get-tuple-element.30), channel_id=1, source_target_pairs={{0,16},{16,32},{32,48},{48,0},{64,80},{80,96},{96,112},{112,64},{1... | collective-permute-start | bytes 196616 | tf_op jit(solution)/shard_map/ppermute | solution.py:190
  12.2 4.3 %collective-permute-start.2 = (f32[2,4,2048]{2,1,0:T(4,128)S(1)}, f32[2,4,2048]{2,1,0:T(4,128)S(1)}, u32[]{:S(2)}, u32[]{:S(2)}) collective-permute-start(f32[2,4,2048]{2,1,0:T(4,128)S(1)} %slice_bitcast_fusion), channel_id=1, source_target_pairs={{0,4},{1,5},{2,6},{3,7},{4,0},{5,1},{6,2},{7,3},{8,12},{9,13},{10,... | collective-permute-start | bytes 196616 | tf_op jit(solution)/shard_map/ppermute | solution.py:170
  16.6 3.7 %collective-permute-start.3 = (f32[4,2048]{1,0:T(4,128)S(1)}, f32[4,2048]{1,0:T(4,128)S(1)}, u32[]{:S(2)}, u32[]{:S(2)}) collective-permute-start(f32[4,2048]{1,0:T(4,128)S(1)} %dynamic-slice_bitcast_fusion.7), channel_id=1, source_target_pairs={{0,2},{1,3},{2,0},{3,1},{4,6},{5,7},{6,4},{7,5},{8,10},{9,11},{10,... | collective-permute-start | bytes 98312 | tf_op jit(solution)/shard_map/ppermute | solution.py:158
  17.9 5.4 %collective-permute-start.8 = (f32[8,1024]{1,0:T(8,128)S(1)}, f32[8,1024]{1,0:T(8,128)S(1)}, u32[]{:S(2)}, u32[]{:S(2)}) collective-permute-start(f32[8,1024]{1,0:T(8,128)S(1)} %dynamic-slice_bitcast_fusion.6), channel_id=1, source_target_pairs={{0,64},{16,80},{32,96},{48,112},{64,0},{80,16},{96,32},{112,48},{1... | collective-permute-start | bytes 98312 | tf_op jit(solution)/shard_map/ppermute | solution.py:182
  20.5 3.6 %collective-permute-start.4 = (bf16[4,2,4,128]{3,2,1,0:T(4,128)(2,1)S(1)}, bf16[4,2,4,128]{3,2,1,0:T(4,128)(2,1)S(1)}, u32[]{:S(2)}, u32[]{:S(2)}) collective-permute-start(bf16[4,2,4,128]{3,2,1,0:T(4,128)(2,1)S(1)} %bitcast.95), channel_id=1, source_target_pairs={{0,1},{1,0},{2,3},{3,2},{4,5},{5,4},{6,7},{7,6},{8,9},{9,8},{10,11... | collective-permute-start | bytes 24584 | tf_op jit(solution)/shard_map/ppermute | solution.py:154
  24.1 2.8 %collective-permute-start.9 = (bf16[8,1536]{1,0:T(8,128)(2,1)S(1)}, bf16[8,1536]{1,0:T(8,128)(2,1)S(1)}, u32[]{:S(2)}, u32[]{:S(2)}) collective-permute-start(bf16[8,1536]{1,0:T(8,128)(2,1)S(1)} %pad_maximum_fusion.7), channel_id=1, source_target_pairs={{0,2},{1,3},{2,0},{3,1},{4,6},{5,7},{6,4},{7,5},{8,10},{9,11},{10,... | collective-permute-start | bytes 73736 | tf_op jit(solution)/shard_map/ppermute | solution.py:158
  26.9 11.7 %collective-permute-start.12 = (bf16[2,8,1152]{2,1,0:T(8,128)(2,1)S(1)}, bf16[2,8,1152]{2,1,0:T(8,128)(2,1)S(1)}, u32[]{:S(2)}, u32[]{:S(2)}) collective-permute-start(bf16[2,8,1152]{2,1,0:T(8,128)(2,1)S(1)} %get-tuple-element.57), channel_id=1, source_target_pairs={{0,12},{1,13},{2,14},{3,15},{4,0},{5,1},{6,2},{7,3},{8,4},{9,5},{1... | collective-permute-start | bytes 110600 | tf_op jit(solution)/shard_map/ppermute | solution.py:162
  27.6 11.0 %collective-permute-start.11 = (bf16[2,8,1152]{2,1,0:T(8,128)(2,1)S(1)}, bf16[2,8,1152]{2,1,0:T(8,128)(2,1)S(1)}, u32[]{:S(2)}, u32[]{:S(2)}) collective-permute-start(bf16[2,8,1152]{2,1,0:T(8,128)(2,1)S(1)} %get-tuple-element.56), channel_id=1, source_target_pairs={{0,8},{1,9},{2,10},{3,11},{4,12},{5,13},{6,14},{7,15},{8,0},{9,1},... | collective-permute-start | bytes 110600 | tf_op jit(solution)/shard_map/ppermute | solution.py:162
  28.6 10.0 %collective-permute-start.10 = (bf16[2,8,1152]{2,1,0:T(8,128)(2,1)S(1)}, bf16[2,8,1152]{2,1,0:T(8,128)(2,1)S(1)}, u32[]{:S(2)}, u32[]{:S(2)}) collective-permute-start(bf16[2,8,1152]{2,1,0:T(8,128)(2,1)S(1)} %get-tuple-element.55), channel_id=1, source_target_pairs={{0,4},{1,5},{2,6},{3,7},{4,8},{5,9},{6,10},{7,11},{8,12},{9,13},{1... | collective-permute-start | bytes 110600 | tf_op jit(solution)/shard_map/ppermute | solution.py:162
  28.6 58.3 %all-to-all-start = ((bf16[16,128,1024]{2,1,0:T(8,128)(2,1)}), bf16[16,128,1024]{2,1,0:T(8,128)(2,1)}, u32[]{:S(2)}, u32[]{:S(2)}) async-start(bf16[16,128,1024]{2,1,0:T(8,128)(2,1)} %bitcast.86), calls=%async_computation | async-start | bytes 8388608 | tf_op jit(solution)/shard_map/all_to_all | solution.py:236
  40.9 6.8 %collective-permute-start.13 = (bf16[4,2,8,1024]{3,2,1,0:T(8,128)(2,1)}, bf16[4,2,8,1024]{3,2,1,0:T(8,128)(2,1)S(1)}, u32[]{:S(2)}, u32[]{:S(2)}) collective-permute-start(bf16[4,2,8,1024]{3,2,1,0:T(8,128)(2,1)} %bitcast.91), channel_id=1, source_target_pairs={{0,66},{1,67},{2,64},{3,65},{4,70},{5,71},{6,68},{7,69},{8,74},{9,... | collective-permute-start | bytes 393224 | tf_op jit(solution)/shard_map/ppermute | solution.py:186
  48.7 8.5 %collective-permute-start.14 = (bf16[4,2,16,1024]{3,2,1,0:T(8,128)(2,1)S(1)}, bf16[4,2,16,1024]{3,2,1,0:T(8,128)(2,1)S(1)}, u32[]{:S(2)}, u32[]{:S(2)}) collective-permute-start(bf16[4,2,16,1024]{3,2,1,0:T(8,128)(2,1)S(1)} %maximum_bitcast_fusion.refs_0_), channel_id=1, source_target_pairs={{0,16},{16,32},{32,48},{48,0},{64,80},{80,96},{96,112},{112,64},{1... | collective-permute-start | bytes 786440 | tf_op jit(solution)/shard_map/ppermute | solution.py:190
  50.1 12.8 %collective-permute-start.15 = (bf16[4,2,16,1024]{3,2,1,0:T(8,128)(2,1)S(1)}, bf16[4,2,16,1024]{3,2,1,0:T(8,128)(2,1)S(1)}, u32[]{:S(2)}, u32[]{:S(2)}) collective-permute-start(bf16[4,2,16,1024]{3,2,1,0:T(8,128)(2,1)S(1)} %maximum_bitcast_fusion.refs_0_), channel_id=1, source_target_pairs={{0,32},{16,48},{32,0},{48,16},{64,96},{80,112},{96,64},{112,80},{1... | collective-permute-start | bytes 786440 | tf_op jit(solution)/shard_map/ppermute | solution.py:190
  51.9 12.9 %collective-permute-start.16 = (bf16[4,2,16,1024]{3,2,1,0:T(8,128)(2,1)S(1)}, bf16[4,2,16,1024]{3,2,1,0:T(8,128)(2,1)S(1)}, u32[]{:S(2)}, u32[]{:S(2)}) collective-permute-start(bf16[4,2,16,1024]{3,2,1,0:T(8,128)(2,1)S(1)} %maximum_bitcast_fusion.refs_0_), channel_id=1, source_target_pairs={{0,48},{16,0},{32,16},{48,32},{64,112},{80,64},{96,80},{112,96},{1... | collective-permute-start | bytes 786440 | tf_op jit(solution)/shard_map/ppermute | solution.py:190
  52.6 14.5 %collective-permute-start.17 = (bf16[4,2,16,1024]{3,2,1,0:T(8,128)(2,1)S(1)}, bf16[4,2,16,1024]{3,2,1,0:T(8,128)(2,1)S(1)}, u32[]{:S(2)}, u32[]{:S(2)}) collective-permute-start(bf16[4,2,16,1024]{3,2,1,0:T(8,128)(2,1)S(1)} %maximum_bitcast_fusion.refs_0_), channel_id=1, source_target_pairs={{0,1},{1,0},{2,3},{3,2},{4,5},{5,4},{6,7},{7,6},{8,9},{9,8},{10,11... | collective-permute-start | bytes 786440 | tf_op jit(solution)/shard_map/ppermute | solution.py:154
  57.1 10.0 %collective-permute-start.18 = (bf16[4,2,16,1024]{3,2,1,0:T(8,128)(2,1)S(1)}, bf16[4,2,16,1024]{3,2,1,0:T(8,128)(2,1)S(1)}, u32[]{:S(2)}, u32[]{:S(2)}) collective-permute-start(bf16[4,2,16,1024]{3,2,1,0:T(8,128)(2,1)S(1)} %collective-permute-done.14.refs_1_), channel_id=1, source_target_pairs={{0,1},{1,0},{2,3},{3,2},{4,5},{5,4},{6,7},{7,6},{8,9},{9,8},{10,11... | collective-permute-start | bytes 786440 | tf_op jit(solution)/shard_map/ppermute | solution.py:154
  62.9 4.2 %collective-permute-start.19 = (bf16[4,2,16,1024]{3,2,1,0:T(8,128)(2,1)S(1)}, bf16[4,2,16,1024]{3,2,1,0:T(8,128)(2,1)S(1)}, u32[]{:S(2)}, u32[]{:S(2)}) collective-permute-start(bf16[4,2,16,1024]{3,2,1,0:T(8,128)(2,1)S(1)} %collective-permute-done.15.refs_2_), channel_id=1, source_target_pairs={{0,1},{1,0},{2,3},{3,2},{4,5},{5,4},{6,7},{7,6},{8,9},{9,8},{10,11... | collective-permute-start | bytes 786440 | tf_op jit(solution)/shard_map/ppermute | solution.py:154
  64.7 2.4 %collective-permute-start.20 = (bf16[4,2,16,1024]{3,2,1,0:T(8,128)(2,1)S(1)}, bf16[4,2,16,1024]{3,2,1,0:T(8,128)(2,1)S(1)}, u32[]{:S(2)}, u32[]{:S(2)}) collective-permute-start(bf16[4,2,16,1024]{3,2,1,0:T(8,128)(2,1)S(1)} %collective-permute-done.16.refs_3_), channel_id=1, source_target_pairs={{0,1},{1,0},{2,3},{3,2},{4,5},{5,4},{6,7},{7,6},{8,9},{9,8},{10,11... | collective-permute-start | bytes 786440 | tf_op jit(solution)/shard_map/ppermute | solution.py:154
  87.0 0.8 copy-start

commit v9 on v7

--- a/solution.py
+++ b/solution.py
@@ -83,8 +83,8 @@
     ).astype(jnp.bfloat16)
     for copy in a_copies:
         copy.wait()
-    for first in range(0, 16, 4):
-        group = range(first, first + 4)
+    for first, last in ((0, 2), (2, 6), (6, 10), (10, 14), (14, 16)):
+        group = range(first, last)
         for s in group:
             in_copies[s].wait()
         for s in group:

time: 91.5 us -> 91.4 us (level)
  no operation moved by 1% of the time
where the time goes in v9:
time: 91.4 us; the launch traced here: 91.1 us
  starting transfers between devices  40.3 us (44%)
  waiting for transfers between devices  38.5 us (42%)
  Pallas kernels  5.72 us (6%)
  other arithmetic  3.32 us (4%)
  local copies, waits for them, and re-layouts  2.39 us (3%)
  between operations  0.99 us (1%)
    all_to_all x1, waiting for transfers between devices, per_device(): arrived = lax.all_to_all(weight, 'col', 0, 0, tiled=True)  20.7 us
    ppermute x6, starting transfers between devices, over_core(): return lax.ppermute(array, 'col', [(i, i ^ 1) for i in range(16)])  10.6 us
    ppermute x6, waiting for transfers between devices, over_z(): lax.ppermute(array, 'row', [(i, i // 4 * 4 + (i + k) % 4) for i in range(...  10 us
    all_to_all x1, starting transfers between devices, per_device(): arrived = lax.all_to_all(weight, 'col', 0, 0, tiled=True)  8.64 us
    ppermute x6, starting transfers between devices, over_z(): lax.ppermute(array, 'row', [(i, i // 4 * 4 + (i + k) % 4) for i in range(...  8.41 us
    pallas_call x1, Pallas kernels, merge(): pl.pallas_call(merge_kernel, in_specs=[pl.BlockSpec(memory_space=pltpu.VM...  4.16 us
    ppermute x1, waiting for transfers between devices, over_x_hi_x(): lax.ppermute(array, ('row', 'col'), [(i, i ^ 4 * 16 + 2) for i in range(1...  3.89 us
    ppermute x2, starting transfers between devices, over_col(): return lax.ppermute(array, 'col', [(i, i ^ mask) for i in range(16)])  2.98 us
  transfers between devices with their start and end apart: 22, of which 12 were waited for; matrix products, arithmetic and copies ran while one was open for 5% of the time, Pallas kernels for 2%

profile of v9, /device:TPU:1, one launch (start us, length us, event | category | flops | bytes accessed | tf_op | source)
XLA Modules:
  0.0 91.1 jit_solution(15205624202547780426)
XLA Ops:
  0.7 1.2 %reshape.44 = f32[4,2,2,4,2048]{4,3,2,1,0:T(4,128)S(1)} reshape(f32[1,64,2048]{2,1,0:T(8,128)} %param.17) | data formatting | bytes 1048576 | tf_op jit(solution)/shard_map/reshape | solution.py:198
  2.0 1.5 %collective-permute-start = (f32[4,2,4,2048]{3,2,1,0:T(4,128)S(1)}, f32[4,2,4,2048]{3,2,1,0:T(4,128)S(1)}, u32[]{:S(2)}, u32[]{:S(2)}) collective-permute-start(f32[4,2,4,2048]{3,2,1,0:T(4,128)S(1)} %get-tuple-element.22), channel_id=1, source_target_pairs={{0,1},{1,0},{2,3},{3,2},{4,5},{5,4},{6,7},{7,6},{8,9},{9,8},{10,11... | collective-permute-start | bytes 786440 | tf_op jit(solution)/shard_map/ppermute | solution.py:144
  3.5 1.0 %dynamic-slice_bitcast_fusion.2 = (f32[2,8,1024]{2,1,0:T(8,128)S(1)}, f32[2,8,1024]{2,1,0:T(8,128)S(1)}, f32[2,8,1024]{2,1,0:T(8,128)S(1)}, f32[2,8,1024]{2,1,0:T(8,128)S(1)}) fusion(f32[2,4,8,1024]{3,2,1,0:T(8,128)} %bitcast.87, s32[]{:T(128)S(6)} %select_n.128, s32[]{:T(128)S(6)} %select_n.126, s32[]{:T(128)S(6)} %select_n.124, s32[]{:T(128)S(6)} %select_n.122), kind=kLoop, calls=%fused_computation.11 | loop fusion | bytes 524304 | tf_op jit(solution)/shard_map/jit(dynamic_index_in_dim)/squeeze | solution.py:140
  4.5 0.2 collective-permute-done
  4.7 0.1 add.182
  4.8 2.9 %collective-permute-start.1 = (f32[2,2,4,2048]{3,2,1,0:T(4,128)S(1)}, f32[2,2,4,2048]{3,2,1,0:T(4,128)S(1)}, u32[]{:S(2)}, u32[]{:S(2)}) collective-permute-start(f32[2,2,4,2048]{3,2,1,0:T(4,128)S(1)} %pad_maximum_fusion), channel_id=1, source_target_pairs={{0,12},{1,13},{2,14},{3,15},{4,8},{5,9},{6,10},{7,11},{8,4},{9,5},... | collective-permute-start | bytes 393224 | tf_op jit(solution)/shard_map/ppermute | solution.py:160
  7.7 3.8 %collective-permute-start.5 = (f32[2,8,1024]{2,1,0:T(8,128)S(1)}, f32[2,8,1024]{2,1,0:T(8,128)S(1)}, u32[]{:S(2)}, u32[]{:S(2)}) collective-permute-start(f32[2,8,1024]{2,1,0:T(8,128)S(1)} %get-tuple-element.28), channel_id=1, source_target_pairs={{0,48},{16,0},{32,16},{48,32},{64,112},{80,64},{96,80},{112,96},{1... | collective-permute-start | bytes 196616 | tf_op jit(solution)/shard_map/ppermute | solution.py:180
  11.5 0.7 collective-permute-start.7
  12.2 0.0 collective-permute-done.1
  12.2 0.1 collective-permute-start.2
  12.3 0.5 collective-permute-done.5
  12.8 3.4 %collective-permute-done.6 = f32[2,8,1024]{2,1,0:T(8,128)S(1)} collective-permute-done((f32[2,8,1024]{2,1,0:T(8,128)S(1)}, f32[2,8,1024]{2,1,0:T(8,128)S(1)}, u32[]{:S(2)}, u32[]{:S(2)}) %collective-permute-start.6) | collective-permute-done | bytes 65568 | tf_op jit(solution)/shard_map/ppermute | solution.py:180
  16.2 0.3 collective-permute-done.7
  16.5 0.0 collective-permute-done.2
  16.6 1.3 %collective-permute-start.3 = (f32[4,2048]{1,0:T(4,128)S(1)}, f32[4,2048]{1,0:T(4,128)S(1)}, u32[]{:S(2)}, u32[]{:S(2)}) collective-permute-start(f32[4,2048]{1,0:T(4,128)S(1)} %dynamic-slice_bitcast_fusion.7), channel_id=1, source_target_pairs={{0,2},{1,3},{2,0},{3,1},{4,6},{5,7},{6,4},{7,5},{8,10},{9,11},{10,... | collective-permute-start | bytes 98312 | tf_op jit(solution)/shard_map/ppermute | solution.py:148
  17.9 2.5 %collective-permute-start.8 = (f32[8,1024]{1,0:T(8,128)S(1)}, f32[8,1024]{1,0:T(8,128)S(1)}, u32[]{:S(2)}, u32[]{:S(2)}) collective-permute-start(f32[8,1024]{1,0:T(8,128)S(1)} %dynamic-slice_bitcast_fusion.6), channel_id=1, source_target_pairs={{0,64},{16,80},{32,96},{48,112},{64,0},{80,16},{96,32},{112,48},{1... | collective-permute-start | bytes 98312 | tf_op jit(solution)/shard_map/ppermute | solution.py:172
  20.3 0.0 collective-permute-done.3
  20.3 0.1 multiply_subtract_fusion.2
  20.5 2.7 %collective-permute-start.4 = (bf16[4,2,4,128]{3,2,1,0:T(4,128)(2,1)S(1)}, bf16[4,2,4,128]{3,2,1,0:T(4,128)(2,1)S(1)}, u32[]{:S(2)}, u32[]{:S(2)}) collective-permute-start(bf16[4,2,4,128]{3,2,1,0:T(4,128)(2,1)S(1)} %bitcast.95), channel_id=1, source_target_pairs={{0,1},{1,0},{2,3},{3,2},{4,5},{5,4},{6,7},{7,6},{8,9},{9,8},{10,11... | collective-permute-start | bytes 24584 | tf_op jit(solution)/shard_map/ppermute | solution.py:144
  23.3 0.7 collective-permute-done.4
  24.1 1.2 %collective-permute-start.9 = (bf16[8,1536]{1,0:T(8,128)(2,1)S(1)}, bf16[8,1536]{1,0:T(8,128)(2,1)S(1)}, u32[]{:S(2)}, u32[]{:S(2)}) collective-permute-start(bf16[8,1536]{1,0:T(8,128)(2,1)S(1)} %pad_maximum_fusion.7), channel_id=1, source_target_pairs={{0,2},{1,3},{2,0},{3,1},{4,6},{5,7},{6,4},{7,5},{8,10},{9,11},{10,... | collective-permute-start | bytes 73736 | tf_op jit(solution)/shard_map/ppermute | solution.py:148
  25.3 1.5 %collective-permute-done.9 = bf16[8,1536]{1,0:T(8,128)(2,1)S(1)} collective-permute-done((bf16[8,1536]{1,0:T(8,128)(2,1)S(1)}, bf16[8,1536]{1,0:T(8,128)(2,1)S(1)}, u32[]{:S(2)}, u32[]{:S(2)}) %collective-permute-start.9) | collective-permute-done | bytes 24608 | tf_op jit(solution)/shard_map/ppermute | solution.py:148
  26.9 0.7 collective-permute-start.12
  27.6 1.0 %collective-permute-start.11 = (bf16[2,8,1152]{2,1,0:T(8,128)(2,1)S(1)}, bf16[2,8,1152]{2,1,0:T(8,128)(2,1)S(1)}, u32[]{:S(2)}, u32[]{:S(2)}) collective-permute-start(bf16[2,8,1152]{2,1,0:T(8,128)(2,1)S(1)} %get-tuple-element.56), channel_id=1, source_target_pairs={{0,8},{1,9},{2,10},{3,11},{4,12},{5,13},{6,14},{7,15},{8,0},{9,1},... | collective-permute-start | bytes 110600 | tf_op jit(solution)/shard_map/ppermute | solution.py:152
  28.6 8.6 %all-to-all-start = ((bf16[16,128,1024]{2,1,0:T(8,128)(2,1)}), bf16[16,128,1024]{2,1,0:T(8,128)(2,1)}, u32[]{:S(2)}, u32[]{:S(2)}) async-start(bf16[16,128,1024]{2,1,0:T(8,128)(2,1)} %bitcast.86), calls=%async_computation | async-start | bytes 8388608 | tf_op jit(solution)/shard_map/all_to_all | solution.py:226
  37.3 0.7 multiply_subtract_fusion
  38.0 0.7 multiply_subtract_fusion.1
  38.6 0.0 collective-permute-done.12
  38.6 0.0 collective-permute-done.11
  38.6 0.0 collective-permute-done.10
  38.7 0.7 pad_maximum_fusion.1
  39.3 1.6 %shard_map.144 = bf16[64,1024]{1,0:T(8,128)(2,1)} custom-call(bf16[64,1024]{1,0:T(8,128)(2,1)} %bitcast.90), custom_call_target="tpu_custom_call" | custom-call | flops 99999997952 | bytes 262144 | tf_op jit(solution)/shard_map/pallas_call | solution.py:132
  40.9 2.9 %collective-permute-start.13 = (bf16[4,2,8,1024]{3,2,1,0:T(8,128)(2,1)}, bf16[4,2,8,1024]{3,2,1,0:T(8,128)(2,1)S(1)}, u32[]{:S(2)}, u32[]{:S(2)}) collective-permute-start(bf16[4,2,8,1024]{3,2,1,0:T(8,128)(2,1)} %bitcast.91), channel_id=1, source_target_pairs={{0,66},{1,67},{2,64},{3,65},{4,70},{5,71},{6,68},{7,69},{8,74},{9,... | collective-permute-start | bytes 393224 | tf_op jit(solution)/shard_map/ppermute | solution.py:176
  43.8 3.9 %collective-permute-done.13 = bf16[4,2,8,1024]{3,2,1,0:T(8,128)(2,1)S(1)} collective-permute-done((bf16[4,2,8,1024]{3,2,1,0:T(8,128)(2,1)}, bf16[4,2,8,1024]{3,2,1,0:T(8,128)(2,1)S(1)}, u32[]{:S(2)}, u32[]{:S(2)}) %collective-permute-start.13) | collective-permute-done | bytes 131104 | tf_op jit(solution)/shard_map/ppermute | solution.py:176
  47.7 0.9 %maximum_bitcast_fusion.refs_0_ = bf16[4,2,16,1024]{3,2,1,0:T(8,128)(2,1)S(1)} fusion(bf16[4,2,1,8,1024]{4,3,2,1,0:T(8,128)(2,1)S(1)} %reverse_bitcast_fusion, bf16[4,2,1,8,1024]{4,3,2,1,0:T(8,128)(2,1)} %bitcast.92), kind=kLoop, calls=%fused_computation | loop fusion | flops 131072 | bytes 524288 | tf_op jit(solution)/shard_map/reshape | solution.py:230
  48.7 1.5 %collective-permute-start.14 = (bf16[4,2,16,1024]{3,2,1,0:T(8,128)(2,1)S(1)}, bf16[4,2,16,1024]{3,2,1,0:T(8,128)(2,1)S(1)}, u32[]{:S(2)}, u32[]{:S(2)}) collective-permute-start(bf16[4,2,16,1024]{3,2,1,0:T(8,128)(2,1)S(1)} %maximum_bitcast_fusion.refs_0_), channel_id=1, source_target_pairs={{0,16},{16,32},{32,48},{48,0},{64,80},{80,96},{96,112},{112,64},{1... | collective-permute-start | bytes 786440 | tf_op jit(solution)/shard_map/ppermute | solution.py:180
  50.1 1.7 %collective-permute-start.15 = (bf16[4,2,16,1024]{3,2,1,0:T(8,128)(2,1)S(1)}, bf16[4,2,16,1024]{3,2,1,0:T(8,128)(2,1)S(1)}, u32[]{:S(2)}, u32[]{:S(2)}) collective-permute-start(bf16[4,2,16,1024]{3,2,1,0:T(8,128)(2,1)S(1)} %maximum_bitcast_fusion.refs_0_), channel_id=1, source_target_pairs={{0,32},{16,48},{32,0},{48,16},{64,96},{80,112},{96,64},{112,80},{1... | collective-permute-start | bytes 786440 | tf_op jit(solution)/shard_map/ppermute | solution.py:180
  51.9 0.8 collective-permute-start.16
  52.6 1.8 %collective-permute-start.17 = (bf16[4,2,16,1024]{3,2,1,0:T(8,128)(2,1)S(1)}, bf16[4,2,16,1024]{3,2,1,0:T(8,128)(2,1)S(1)}, u32[]{:S(2)}, u32[]{:S(2)}) collective-permute-start(bf16[4,2,16,1024]{3,2,1,0:T(8,128)(2,1)S(1)} %maximum_bitcast_fusion.refs_0_), channel_id=1, source_target_pairs={{0,1},{1,0},{2,3},{3,2},{4,5},{5,4},{6,7},{7,6},{8,9},{9,8},{10,11... | collective-permute-start | bytes 786440 | tf_op jit(solution)/shard_map/ppermute | solution.py:144
  54.4 2.7 %collective-permute-done.14.refs_1_ = bf16[4,2,16,1024]{3,2,1,0:T(8,128)(2,1)S(1)} collective-permute-done((bf16[4,2,16,1024]{3,2,1,0:T(8,128)(2,1)S(1)}, bf16[4,2,16,1024]{3,2,1,0:T(8,128)(2,1)S(1)}, u32[]{:S(2)}, u32[]{:S(2)}) %collective-permute-start.14) | collective-permute-done | bytes 262176 | tf_op jit(solution)/shard_map/ppermute | solution.py:180
  57.1 2.6 %collective-permute-start.18 = (bf16[4,2,16,1024]{3,2,1,0:T(8,128)(2,1)S(1)}, bf16[4,2,16,1024]{3,2,1,0:T(8,128)(2,1)S(1)}, u32[]{:S(2)}, u32[]{:S(2)}) collective-permute-start(bf16[4,2,16,1024]{3,2,1,0:T(8,128)(2,1)S(1)} %collective-permute-done.14.refs_1_), channel_id=1, source_target_pairs={{0,1},{1,0},{2,3},{3,2},{4,5},{5,4},{6,7},{7,6},{8,9},{9,8},{10,11... | collective-permute-start | bytes 786440 | tf_op jit(solution)/shard_map/ppermute | solution.py:144
  59.7 3.2 %collective-permute-done.15.refs_2_ = bf16[4,2,16,1024]{3,2,1,0:T(8,128)(2,1)S(1)} collective-permute-done((bf16[4,2,16,1024]{3,2,1,0:T(8,128)(2,1)S(1)}, bf16[4,2,16,1024]{3,2,1,0:T(8,128)(2,1)S(1)}, u32[]{:S(2)}, u32[]{:S(2)}) %collective-permute-start.15) | collective-permute-done | bytes 262176 | tf_op jit(solution)/shard_map/ppermute | solution.py:180
  62.9 1.8 %collective-permute-start.19 = (bf16[4,2,16,1024]{3,2,1,0:T(8,128)(2,1)S(1)}, bf16[4,2,16,1024]{3,2,1,0:T(8,128)(2,1)S(1)}, u32[]{:S(2)}, u32[]{:S(2)}) collective-permute-start(bf16[4,2,16,1024]{3,2,1,0:T(8,128)(2,1)S(1)} %collective-permute-done.15.refs_2_), channel_id=1, source_target_pairs={{0,1},{1,0},{2,3},{3,2},{4,5},{5,4},{6,7},{7,6},{8,9},{9,8},{10,11... | collective-permute-start | bytes 786440 | tf_op jit(solution)/shard_map/ppermute | solution.py:144
  64.7 0.2 collective-permute-start.20
  64.9 1.0 %collective-permute-done.19.refs_6_ = bf16[4,2,16,1024]{3,2,1,0:T(8,128)(2,1)S(1)} collective-permute-done((bf16[4,2,16,1024]{3,2,1,0:T(8,128)(2,1)S(1)}, bf16[4,2,16,1024]{3,2,1,0:T(8,128)(2,1)S(1)}, u32[]{:S(2)}, u32[]{:S(2)}) %collective-permute-start.19) | collective-permute-done | bytes 262176 | tf_op jit(solution)/shard_map/ppermute | solution.py:144
  65.9 0.4 collective-permute-done.20.refs_7_
  66.3 20.7 %all-to-all-done.refs_8_ = bf16[16,128,1024]{2,1,0:T(8,128)(2,1)} async-done(((bf16[16,128,1024]{2,1,0:T(8,128)(2,1)}), bf16[16,128,1024]{2,1,0:T(8,128)(2,1)}, u32[]{:S(2)}, u32[]{:S(2)}) %all-to-all-start) | async-done | bytes 4194336 | tf_op jit(solution)/shard_map/all_to_all | solution.py:226
  87.0 4.2 %shard_map.145 = bf16[8,128,2048]{2,1,0:T(8,128)(2,1)} custom-call(f32[64,128]{1,0:T(8,128)S(1)} %bitcast_convert_fusion.bt_ref, bf16[4,2,16,1024]{3,2,1,0:T(8,128)(2,1)S(1)} %maximum_bitcast_fusion.refs_0_, bf16[4,2,16,1024]{3,2,1,0:T(8,128)(2,1)S(1)} %collective-permute-done.14.refs_1_, bf16[4,2,16,1024]{3,2,1,0:T(8,128)(2,1)S(1)} %collective-permute-done.15.refs_2_, ...), custom_call_target="tpu_custom_call" | custom-call | flops 268435456 | bytes 10485760 | tf_op jit(solution)/shard_map/pallas_call | solution.py:107
  (48 shorter events, 0.5 us)
Async XLA Ops:
  0.6 19.7 %copy-start = (f32[4,2048]{1,0:T(4,128)S(1)}, f32[4,2048]{1,0:T(4,128)}, u32[]{:S(2)}) copy-start(f32[4,2048]{1,0:T(4,128)} %param.13) | copy-start | bytes 98308
  0.6 19.7 %copy-start.2 = (f32[4,2048]{1,0:T(4,128)S(1)}, f32[4,2048]{1,0:T(4,128)}, u32[]{:S(2)}) copy-start(f32[4,2048]{1,0:T(4,128)} %param.14) | copy-start | bytes 98308
  0.7 19.7 %copy-start.1 = (f32[4,2048]{1,0:T(4,128)S(1)}, f32[4,2048]{1,0:T(4,128)}, u32[]{:S(2)}) copy-start(f32[4,2048]{1,0:T(4,128)} %param.15) | copy-start | bytes 98308
  0.7 22.6 %copy-start.3 = (f32[8,1024]{1,0:T(8,128)S(1)}, f32[8,1024]{1,0:T(8,128)}, u32[]{:S(2)}) copy-start(f32[8,1024]{1,0:T(8,128)} %param.10) | copy-start | bytes 98308
  0.7 22.6 %copy-start.5 = (f32[8,1024]{1,0:T(8,128)S(1)}, f32[8,1024]{1,0:T(8,128)}, u32[]{:S(2)}) copy-start(f32[8,1024]{1,0:T(8,128)} %param.11) | copy-start | bytes 98308
  0.7 22.6 %copy-start.4 = (f32[8,1024]{1,0:T(8,128)S(1)}, f32[8,1024]{1,0:T(8,128)}, u32[]{:S(2)}) copy-start(f32[8,1024]{1,0:T(8,128)} %param.12) | copy-start | bytes 98308
  2.0 2.7 %collective-permute-start = (f32[4,2,4,2048]{3,2,1,0:T(4,128)S(1)}, f32[4,2,4,2048]{3,2,1,0:T(4,128)S(1)}, u32[]{:S(2)}, u32[]{:S(2)}) collective-permute-start(f32[4,2,4,2048]{3,2,1,0:T(4,128)S(1)} %get-tuple-element.22), channel_id=1, source_target_pairs={{0,1},{1,0},{2,3},{3,2},{4,5},{5,4},{6,7},{7,6},{8,9},{9,8},{10,11... | collective-permute-start | bytes 786440 | tf_op jit(solution)/shard_map/ppermute | solution.py:144
  4.8 7.4 %collective-permute-start.1 = (f32[2,2,4,2048]{3,2,1,0:T(4,128)S(1)}, f32[2,2,4,2048]{3,2,1,0:T(4,128)S(1)}, u32[]{:S(2)}, u32[]{:S(2)}) collective-permute-start(f32[2,2,4,2048]{3,2,1,0:T(4,128)S(1)} %pad_maximum_fusion), channel_id=1, source_target_pairs={{0,12},{1,13},{2,14},{3,15},{4,8},{5,9},{6,10},{7,11},{8,4},{9,5},... | collective-permute-start | bytes 393224 | tf_op jit(solution)/shard_map/ppermute | solution.py:160
  7.7 5.1 %collective-permute-start.5 = (f32[2,8,1024]{2,1,0:T(8,128)S(1)}, f32[2,8,1024]{2,1,0:T(8,128)S(1)}, u32[]{:S(2)}, u32[]{:S(2)}) collective-permute-start(f32[2,8,1024]{2,1,0:T(8,128)S(1)} %get-tuple-element.28), channel_id=1, source_target_pairs={{0,48},{16,0},{32,16},{48,32},{64,112},{80,64},{96,80},{112,96},{1... | collective-permute-start | bytes 196616 | tf_op jit(solution)/shard_map/ppermute | solution.py:180
  11.5 4.7 %collective-permute-start.6 = (f32[2,8,1024]{2,1,0:T(8,128)S(1)}, f32[2,8,1024]{2,1,0:T(8,128)S(1)}, u32[]{:S(2)}, u32[]{:S(2)}) collective-permute-start(f32[2,8,1024]{2,1,0:T(8,128)S(1)} %get-tuple-element.29), channel_id=1, source_target_pairs={{0,32},{16,48},{32,0},{48,16},{64,96},{80,112},{96,64},{112,80},{1... | collective-permute-start | bytes 196616 | tf_op jit(solution)/shard_map/ppermute | solution.py:180
  11.5 5.0 %collective-permute-start.7 = (f32[2,8,1024]{2,1,0:T(8,128)S(1)}, f32[2,8,1024]{2,1,0:T(8,128)S(1)}, u32[]{:S(2)}, u32[]{:S(2)}) collective-permute-start(f32[2,8,1024]{2,1,0:T(8,128)S(1)} %get-tuple-element.30), channel_id=1, source_target_pairs={{0,16},{16,32},{32,48},{48,0},{64,80},{80,96},{96,112},{112,64},{1... | collective-permute-start | bytes 196616 | tf_op jit(solution)/shard_map/ppermute | solution.py:180
  12.2 4.3 %collective-permute-start.2 = (f32[2,4,2048]{2,1,0:T(4,128)S(1)}, f32[2,4,2048]{2,1,0:T(4,128)S(1)}, u32[]{:S(2)}, u32[]{:S(2)}) collective-permute-start(f32[2,4,2048]{2,1,0:T(4,128)S(1)} %slice_bitcast_fusion), channel_id=1, source_target_pairs={{0,4},{1,5},{2,6},{3,7},{4,0},{5,1},{6,2},{7,3},{8,12},{9,13},{10,... | collective-permute-start | bytes 196616 | tf_op jit(solution)/shard_map/ppermute | solution.py:160
  16.6 3.7 %collective-permute-start.3 = (f32[4,2048]{1,0:T(4,128)S(1)}, f32[4,2048]{1,0:T(4,128)S(1)}, u32[]{:S(2)}, u32[]{:S(2)}) collective-permute-start(f32[4,2048]{1,0:T(4,128)S(1)} %dynamic-slice_bitcast_fusion.7), channel_id=1, source_target_pairs={{0,2},{1,3},{2,0},{3,1},{4,6},{5,7},{6,4},{7,5},{8,10},{9,11},{10,... | collective-permute-start | bytes 98312 | tf_op jit(solution)/shard_map/ppermute | solution.py:148
  17.9 5.4 %collective-permute-start.8 = (f32[8,1024]{1,0:T(8,128)S(1)}, f32[8,1024]{1,0:T(8,128)S(1)}, u32[]{:S(2)}, u32[]{:S(2)}) collective-permute-start(f32[8,1024]{1,0:T(8,128)S(1)} %dynamic-slice_bitcast_fusion.6), channel_id=1, source_target_pairs={{0,64},{16,80},{32,96},{48,112},{64,0},{80,16},{96,32},{112,48},{1... | collective-permute-start | bytes 98312 | tf_op jit(solution)/shard_map/ppermute | solution.py:172
  20.5 3.6 %collective-permute-start.4 = (bf16[4,2,4,128]{3,2,1,0:T(4,128)(2,1)S(1)}, bf16[4,2,4,128]{3,2,1,0:T(4,128)(2,1)S(1)}, u32[]{:S(2)}, u32[]{:S(2)}) collective-permute-start(bf16[4,2,4,128]{3,2,1,0:T(4,128)(2,1)S(1)} %bitcast.95), channel_id=1, source_target_pairs={{0,1},{1,0},{2,3},{3,2},{4,5},{5,4},{6,7},{7,6},{8,9},{9,8},{10,11... | collective-permute-start | bytes 24584 | tf_op jit(solution)/shard_map/ppermute | solution.py:144
  24.1 2.8 %collective-permute-start.9 = (bf16[8,1536]{1,0:T(8,128)(2,1)S(1)}, bf16[8,1536]{1,0:T(8,128)(2,1)S(1)}, u32[]{:S(2)}, u32[]{:S(2)}) collective-permute-start(bf16[8,1536]{1,0:T(8,128)(2,1)S(1)} %pad_maximum_fusion.7), channel_id=1, source_target_pairs={{0,2},{1,3},{2,0},{3,1},{4,6},{5,7},{6,4},{7,5},{8,10},{9,11},{10,... | collective-permute-start | bytes 73736 | tf_op jit(solution)/shard_map/ppermute | solution.py:148
  26.9 11.7 %collective-permute-start.12 = (bf16[2,8,1152]{2,1,0:T(8,128)(2,1)S(1)}, bf16[2,8,1152]{2,1,0:T(8,128)(2,1)S(1)}, u32[]{:S(2)}, u32[]{:S(2)}) collective-permute-start(bf16[2,8,1152]{2,1,0:T(8,128)(2,1)S(1)} %get-tuple-element.57), channel_id=1, source_target_pairs={{0,12},{1,13},{2,14},{3,15},{4,0},{5,1},{6,2},{7,3},{8,4},{9,5},{1... | collective-permute-start | bytes 110600 | tf_op jit(solution)/shard_map/ppermute | solution.py:152
  27.6 11.0 %collective-permute-start.11 = (bf16[2,8,1152]{2,1,0:T(8,128)(2,1)S(1)}, bf16[2,8,1152]{2,1,0:T(8,128)(2,1)S(1)}, u32[]{:S(2)}, u32[]{:S(2)}) collective-permute-start(bf16[2,8,1152]{2,1,0:T(8,128)(2,1)S(1)} %get-tuple-element.56), channel_id=1, source_target_pairs={{0,8},{1,9},{2,10},{3,11},{4,12},{5,13},{6,14},{7,15},{8,0},{9,1},... | collective-permute-start | bytes 110600 | tf_op jit(solution)/shard_map/ppermute | solution.py:152
  28.6 10.0 %collective-permute-start.10 = (bf16[2,8,1152]{2,1,0:T(8,128)(2,1)S(1)}, bf16[2,8,1152]{2,1,0:T(8,128)(2,1)S(1)}, u32[]{:S(2)}, u32[]{:S(2)}) collective-permute-start(bf16[2,8,1152]{2,1,0:T(8,128)(2,1)S(1)} %get-tuple-element.55), channel_id=1, source_target_pairs={{0,4},{1,5},{2,6},{3,7},{4,8},{5,9},{6,10},{7,11},{8,12},{9,13},{1... | collective-permute-start | bytes 110600 | tf_op jit(solution)/shard_map/ppermute | solution.py:152
  28.6 58.3 %all-to-all-start = ((bf16[16,128,1024]{2,1,0:T(8,128)(2,1)}), bf16[16,128,1024]{2,1,0:T(8,128)(2,1)}, u32[]{:S(2)}, u32[]{:S(2)}) async-start(bf16[16,128,1024]{2,1,0:T(8,128)(2,1)} %bitcast.86), calls=%async_computation | async-start | bytes 8388608 | tf_op jit(solution)/shard_map/all_to_all | solution.py:226
  40.9 6.8 %collective-permute-start.13 = (bf16[4,2,8,1024]{3,2,1,0:T(8,128)(2,1)}, bf16[4,2,8,1024]{3,2,1,0:T(8,128)(2,1)S(1)}, u32[]{:S(2)}, u32[]{:S(2)}) collective-permute-start(bf16[4,2,8,1024]{3,2,1,0:T(8,128)(2,1)} %bitcast.91), channel_id=1, source_target_pairs={{0,66},{1,67},{2,64},{3,65},{4,70},{5,71},{6,68},{7,69},{8,74},{9,... | collective-permute-start | bytes 393224 | tf_op jit(solution)/shard_map/ppermute | solution.py:176
  48.7 8.5 %collective-permute-start.14 = (bf16[4,2,16,1024]{3,2,1,0:T(8,128)(2,1)S(1)}, bf16[4,2,16,1024]{3,2,1,0:T(8,128)(2,1)S(1)}, u32[]{:S(2)}, u32[]{:S(2)}) collective-permute-start(bf16[4,2,16,1024]{3,2,1,0:T(8,128)(2,1)S(1)} %maximum_bitcast_fusion.refs_0_), channel_id=1, source_target_pairs={{0,16},{16,32},{32,48},{48,0},{64,80},{80,96},{96,112},{112,64},{1... | collective-permute-start | bytes 786440 | tf_op jit(solution)/shard_map/ppermute | solution.py:180
  50.1 12.8 %collective-permute-start.15 = (bf16[4,2,16,1024]{3,2,1,0:T(8,128)(2,1)S(1)}, bf16[4,2,16,1024]{3,2,1,0:T(8,128)(2,1)S(1)}, u32[]{:S(2)}, u32[]{:S(2)}) collective-permute-start(bf16[4,2,16,1024]{3,2,1,0:T(8,128)(2,1)S(1)} %maximum_bitcast_fusion.refs_0_), channel_id=1, source_target_pairs={{0,32},{16,48},{32,0},{48,16},{64,96},{80,112},{96,64},{112,80},{1... | collective-permute-start | bytes 786440 | tf_op jit(solution)/shard_map/ppermute | solution.py:180
  51.9 12.9 %collective-permute-start.16 = (bf16[4,2,16,1024]{3,2,1,0:T(8,128)(2,1)S(1)}, bf16[4,2,16,1024]{3,2,1,0:T(8,128)(2,1)S(1)}, u32[]{:S(2)}, u32[]{:S(2)}) collective-permute-start(bf16[4,2,16,1024]{3,2,1,0:T(8,128)(2,1)S(1)} %maximum_bitcast_fusion.refs_0_), channel_id=1, source_target_pairs={{0,48},{16,0},{32,16},{48,32},{64,112},{80,64},{96,80},{112,96},{1... | collective-permute-start | bytes 786440 | tf_op jit(solution)/shard_map/ppermute | solution.py:180
  52.6 12.3 %collective-permute-start.17 = (bf16[4,2,16,1024]{3,2,1,0:T(8,128)(2,1)S(1)}, bf16[4,2,16,1024]{3,2,1,0:T(8,128)(2,1)S(1)}, u32[]{:S(2)}, u32[]{:S(2)}) collective-permute-start(bf16[4,2,16,1024]{3,2,1,0:T(8,128)(2,1)S(1)} %maximum_bitcast_fusion.refs_0_), channel_id=1, source_target_pairs={{0,1},{1,0},{2,3},{3,2},{4,5},{5,4},{6,7},{7,6},{8,9},{9,8},{10,11... | collective-permute-start | bytes 786440 | tf_op jit(solution)/shard_map/ppermute | solution.py:144
  57.1 7.8 %collective-permute-start.18 = (bf16[4,2,16,1024]{3,2,1,0:T(8,128)(2,1)S(1)}, bf16[4,2,16,1024]{3,2,1,0:T(8,128)(2,1)S(1)}, u32[]{:S(2)}, u32[]{:S(2)}) collective-permute-start(bf16[4,2,16,1024]{3,2,1,0:T(8,128)(2,1)S(1)} %collective-permute-done.14.refs_1_), channel_id=1, source_target_pairs={{0,1},{1,0},{2,3},{3,2},{4,5},{5,4},{6,7},{7,6},{8,9},{9,8},{10,11... | collective-permute-start | bytes 786440 | tf_op jit(solution)/shard_map/ppermute | solution.py:144
  62.9 3.0 %collective-permute-start.19 = (bf16[4,2,16,1024]{3,2,1,0:T(8,128)(2,1)S(1)}, bf16[4,2,16,1024]{3,2,1,0:T(8,128)(2,1)S(1)}, u32[]{:S(2)}, u32[]{:S(2)}) collective-permute-start(bf16[4,2,16,1024]{3,2,1,0:T(8,128)(2,1)S(1)} %collective-permute-done.15.refs_2_), channel_id=1, source_target_pairs={{0,1},{1,0},{2,3},{3,2},{4,5},{5,4},{6,7},{7,6},{8,9},{9,8},{10,11... | collective-permute-start | bytes 786440 | tf_op jit(solution)/shard_map/ppermute | solution.py:144
  64.7 1.5 %collective-permute-start.20 = (bf16[4,2,16,1024]{3,2,1,0:T(8,128)(2,1)S(1)}, bf16[4,2,16,1024]{3,2,1,0:T(8,128)(2,1)S(1)}, u32[]{:S(2)}, u32[]{:S(2)}) collective-permute-start(bf16[4,2,16,1024]{3,2,1,0:T(8,128)(2,1)S(1)} %collective-permute-done.16.refs_3_), channel_id=1, source_target_pairs={{0,1},{1,0},{2,3},{3,2},{4,5},{5,4},{6,7},{7,6},{8,9},{9,8},{10,11... | collective-permute-start | bytes 786440 | tf_op jit(solution)/shard_map/ppermute | solution.py:144
